TPU v7x, 32 devices: a whole 2x2x4 slice. The times are simulated.
32 devices in a mesh: ctx: 16 (over z, y, core), head: 2 (over x).
Axes of the slice: x: 2, y: 2, z: 4, core: 2. Of those that a mesh axis runs over, the one named last changes fastest.
Arguments:
- queries: bfloat16 [1, 16384, 256], P(None, ('ctx', 'head')), may hold values from -150 to 150
- keys: bfloat16 [1, 16384, 256], P(None, ('ctx', 'head')), may hold values from -32 to 32
- values: bfloat16 [1, 16384, 256], P(None, ('ctx', 'head')), may hold values from -6 to 6
- rates: float32 [1, 2, 16384], P(None, 'head', 'ctx'), may hold values from 0.0002 to 0.004
- tail_keys: bfloat16 [8192, 256], P('ctx', 'head'), may hold values from -6 to 6
- tail_values: bfloat16 [8192, 256], P('ctx', 'head'), may hold values from -6 to 6
- state_in_gu: float32 [16, 2, 2, 128, 256], P('ctx', 'head'), may hold values from -0.5 to 0.5
- state_in_down: float32 [16, 2, 256, 128], P('ctx', 'head'), may hold values from -0.375 to 0.375
- fresh_gu: float32 [2, 2, 128, 256], P('head'), may hold values from -0.5 to 0.5
- fresh_down: float32 [2, 256, 128], P('head'), may hold values from -0.375 to 0.375
- out_gain: float32 [256], P('head'), may hold values from 0.1 to 1.9
- seq_ids: int32 [16, 2], replicated, may hold values from 0 to 31, as said below
- live_lengths: int32 [16, 1], replicated, may hold values from 1 to 1024, as said below
Outputs:
- mixed: bfloat16 [1, 16384, 256], P(None, ('ctx', 'head'))
- state_out_gu: float32 [16, 2, 2, 128, 256], P('ctx', 'head')
- state_out_down: float32 [16, 2, 256, 128], P('ctx', 'head')
Inputs may be any that keep to these rules, and one draw needn't show every extreme that they name: `seq_ids`: block (c, t + 1) continues the sequence of block ((c - 1) mod 16, t) exactly when their numbers agree, else it begins a new sequence; different sequences have different numbers. `live_lengths`: only a block whose successor (device c + 1 mod 16, step t + 1) begins a new sequence is shorter than 1024; its live tokens are the first ones.
All inputs are finite; a program needn't handle non-finite values.
Results may differ from a plain program's by a relative error of at most 0.0028.
Values may be sent and summed in bfloat16 or wider, within the bound.
No kernel may reach another device: no remote copies, remote signals or barrier semaphores. Data moves between devices by JAX's collectives and lax.ppermute only.
A program may use at most 64 MiB of HBM per device.

v0:
```python
import math

import jax
import jax.numpy as jnp
from jax import lax
from jax.sharding import PartitionSpec as P

epsilon = 1e-06


def from_behind(shard, axis, by):
    size = lax.axis_size(axis)
    return lax.ppermute(shard, axis, [(i, (i + by) % size) for i in range(size)])


def highest(left, right):
    return jnp.dot(left, right, precision=lax.Precision.HIGHEST)


def rms_rows(matrix):
    return matrix / jnp.sqrt(jnp.mean(matrix * matrix, axis=-1, keepdims=True) + epsilon)


def renormed(old_weight, new_weight):
    old_scale = jnp.sqrt(jnp.mean(old_weight * old_weight, axis=0, keepdims=True) + epsilon)
    new_scale = jnp.sqrt(jnp.mean(new_weight * new_weight, axis=0, keepdims=True) + epsilon)
    return new_weight * (old_scale / new_scale)


def fast_block(
    block_q,
    block_k,
    block_v,
    rate_row,
    prior_keys,
    prior_values,
    gate_up,
    down_proj,
    fresh_pair,
    fresh_proj,
    head_gain,
    length,
    linked,
):
    block_len = block_q.shape[0]
    window = prior_keys.shape[0]
    head_dim = block_q.shape[1]
    gate_up = jnp.where(linked, gate_up, fresh_pair)
    down_proj = jnp.where(linked, down_proj, fresh_proj)
    joined_keys = jnp.concatenate([prior_keys, block_k], axis=0)
    joined_values = jnp.concatenate([prior_values, block_v], axis=0)
    row_index = jnp.arange(window)[:, None]
    col_index = jnp.arange(2 * window)[None, :]
    pieces = []
    for offset in range(0, block_len, window):
        query_pos = offset + row_index
        key_pos = offset - window + col_index
        allowed = (
            (key_pos <= query_pos)
            & (key_pos > query_pos - window)
            & ((key_pos < length) | (key_pos == query_pos))
            & ((key_pos >= 0) | linked)
        )
        scores = jnp.einsum(
            "qd,kd->qk",
            block_q[offset : offset + window],
            joined_keys[offset : offset + 2 * window],
            preferred_element_type=jnp.float32,
        ) * (1.0 / math.sqrt(head_dim))
        scores = jnp.where(allowed, scores, -1e30)
        largest = jnp.max(scores, axis=-1, keepdims=True)
        exponent = jnp.exp(scores - largest)
        weights = (exponent / jnp.sum(exponent, axis=-1, keepdims=True)).astype(jnp.bfloat16)
        pieces.append(
            jnp.dot(
                weights,
                joined_values[offset : offset + 2 * window],
                preferred_element_type=jnp.float32,
            )
        )
    attended = jnp.concatenate(pieces, axis=0)
    query_unit = rms_rows(block_q.astype(jnp.float32))
    key_unit = rms_rows(block_k.astype(jnp.float32))
    w_gate = gate_up[0]
    w_up = gate_up[1]
    fast_out = highest(
        jax.nn.silu(highest(query_unit, w_gate)) * highest(query_unit, w_up), down_proj
    )
    live_rows = (jnp.arange(block_len) < length).astype(jnp.float32)[:, None]
    mixed = ((attended + rms_rows(fast_out) * head_gain) * live_rows).astype(jnp.bfloat16)
    key_gate = highest(key_unit, w_gate)
    key_up = highest(key_unit, w_up)
    gate_sigmoid = jax.nn.sigmoid(key_gate)
    gate_act = key_gate * gate_sigmoid
    out_grad = -(rate_row[:, None] * live_rows) * block_v.astype(jnp.float32)
    grad_down = highest((gate_act * key_up).T, out_grad)
    hidden_grad = highest(out_grad, down_proj.T)
    grad_up = highest(key_unit.T, hidden_grad * gate_act)
    grad_gate = highest(
        key_unit.T, hidden_grad * key_up * gate_sigmoid * (1.0 + key_gate * (1.0 - gate_sigmoid))
    )
    new_pair = jnp.stack([renormed(w_gate, w_gate - grad_gate), renormed(w_up, w_up - grad_up)])
    new_down = renormed(down_proj, down_proj - grad_down)
    return (mixed, new_pair, new_down)


def advance(
    block_q,
    block_k,
    block_v,
    rate_row,
    prior_keys,
    prior_values,
    gate_up,
    down_proj,
    fresh_pair,
    fresh_proj,
    head_gain,
    length,
    linked,
):
    moved_pair, moved_proj = from_behind((gate_up, down_proj), "ctx", 1)
    return fast_block(
        block_q,
        block_k,
        block_v,
        rate_row,
        prior_keys,
        prior_values,
        moved_pair,
        moved_proj,
        fresh_pair,
        fresh_proj,
        head_gain,
        length,
        linked,
    )


def on_device(
    queries,
    keys,
    values,
    rates,
    tail_keys,
    tail_values,
    state_in_gu,
    state_in_down,
    fresh_gu,
    fresh_down,
    out_gain,
    seq_ids,
    live_lengths,
):
    ctx_count = lax.axis_size("ctx")
    here_index = lax.axis_index("ctx")
    before_index = (here_index + ctx_count - 1) % ctx_count
    own_ids = lax.dynamic_index_in_dim(seq_ids, here_index, 0, keepdims=False)
    prior_ids = lax.dynamic_index_in_dim(seq_ids, before_index, 0, keepdims=False)
    own_lengths = lax.dynamic_index_in_dim(live_lengths, here_index, 0, keepdims=False)
    gate_up = state_in_gu[0, 0]
    down_proj = state_in_down[0, 0]
    fresh_pair = fresh_gu[0]
    fresh_proj = fresh_down[0]
    block_q = lax.all_to_all(queries[0], "head", split_axis=1, concat_axis=0, tiled=True)
    block_k = lax.all_to_all(keys[0], "head", split_axis=1, concat_axis=0, tiled=True)
    block_v = lax.all_to_all(values[0], "head", split_axis=1, concat_axis=0, tiled=True)
    prior_keys, prior_values = from_behind((tail_keys, tail_values), "ctx", 1)
    linked = own_ids[1] == prior_ids[0]
    mixed_step, gate_up, down_proj = advance(
        block_q,
        block_k,
        block_v,
        rates[0, 0],
        prior_keys,
        prior_values,
        gate_up,
        down_proj,
        fresh_pair,
        fresh_proj,
        out_gain,
        own_lengths[0],
        linked,
    )
    results = [lax.all_to_all(mixed_step, "head", split_axis=0, concat_axis=1, tiled=True)]
    mixed = jnp.stack(results)
    return (mixed, gate_up[None, None], down_proj[None, None])


def solution(mesh):
    placed = (
        P(None, ("ctx", "head"), None),
        P(None, ("ctx", "head"), None),
        P(None, ("ctx", "head"), None),
        P(None, "head", "ctx"),
        P("ctx", "head"),
        P("ctx", "head"),
        P("ctx", "head", None, None, None),
        P("ctx", "head", None, None),
        P("head", None, None, None),
        P("head", None, None),
        P("head"),
        P(),
        P(),
    )
    return jax.shard_map(
        on_device,
        mesh=mesh,
        in_specs=placed,
        out_specs=(
            P(None, ("ctx", "head"), None),
            P("ctx", "head", None, None, None),
            P("ctx", "head", None, None),
        ),
        check_vma=False,
    )
```

profile of v0, /device:TPU:0, one launch (start us, length us, event | category | flops | bytes accessed | tf_op | source)
XLA Modules:
  0.0 64.6 jit_solution(1546731135339959085)
XLA Ops:
  1.2 2.6 %collective-permute-start.3 = (f32[256,128]{1,0:T(8,128)}, f32[256,128]{1,0:T(8,128)S(1)}, u32[]{:S(2)}, u32[]{:S(2)}) collective-permute-start(f32[256,128]{1,0:T(8,128)} %bitcast.96), channel_id=1, source_target_pairs={{0,2},{2,4},{4,6},{6,8},{8,10},{10,12},{12,14},{14,16},{16,18},{18... | collective-permute-start | bytes 393224 | tf_op jit(solution)/shard_map/ppermute | solution.py:13
  3.8 1.8 %copy.24 = bf16[1,512,256]{1,2,0:T(8,128)(2,1)} copy(bf16[1,512,256]{2,1,0:T(8,128)(2,1)} %param.15) | data formatting | bytes 524288 | tf_op args[2]
  5.6 3.4 %all-to-all-start.2 = ((bf16[512,2,128]{0,2,1:T(8,128)(2,1)}), bf16[512,2,128]{0,2,1:T(8,128)(2,1)S(1)}, u32[]{:S(2)}, u32[]{:S(2)}) async-start(bf16[512,2,128]{0,2,1:T(8,128)(2,1)} %bitcast.9), calls=%async_computation.2 | async-start | bytes 524288 | tf_op jit(solution)/shard_map/all_to_all | solution.py:167
  9.2 1.6 %collective-permute-start.1 = (bf16[512,128]{1,0:T(8,128)(2,1)}, bf16[512,128]{1,0:T(8,128)(2,1)S(1)}, u32[]{:S(2)}, u32[]{:S(2)}) collective-permute-start(bf16[512,128]{1,0:T(8,128)(2,1)} %param.18), channel_id=1, source_target_pairs={{0,2},{2,4},{4,6},{6,8},{8,10},{10,12},{12,14},{14,16},{16,18},{18... | collective-permute-start | bytes 393224 | tf_op jit(solution)/shard_map/ppermute | solution.py:13
  10.7 0.8 %constant_dynamic-slice_fusion = (s32[1,2]{0,1:T(2,128)S(1)}, s32[1,2]{0,1:T(2,128)S(1)}) fusion(s32[16,2]{0,1:T(2,128)} %param.24, s32[]{:T(128)S(6)} %select_n.41, s32[]{:T(128)S(6)} %select_n.39), kind=kLoop, calls=%fused_computation.98 | loop fusion | bytes 40 | tf_op jit(solution)/shard_map/jit(dynamic_index_in_dim)/dynamic_slice | solution.py:159
  14.5 1.3 %select_negate_fusion = f32[1024]{0:T(1024)S(1)} fusion(f32[1024]{0:T(1024)} %bitcast.92, s32[]{:T(128)} %bitcast), kind=kLoop, calls=%fused_computation.85 | loop fusion | flops 3072 | bytes 8196 | tf_op jit(solution)/shard_map/neg | solution.py:95
  15.8 0.7 %compare_or_fusion = (pred[1024]{0:T(1024)(128)(4,1)S(1)}, pred[1024]{0:T(1024)(128)(4,1)S(1)}) fusion(pred[]{:T(512)} %bitcast.1, s32[]{:T(128)} %bitcast), kind=kLoop, calls=%fused_computation.91 | loop fusion | flops 4096 | bytes 2053 | tf_op jit(solution)/shard_map/or | solution.py:62
  16.5 1.8 %copy.20 = bf16[1,512,256]{1,2,0:T(8,128)(2,1)} copy(bf16[1,512,256]{2,1,0:T(8,128)(2,1)} %param.14) | data formatting | bytes 524288 | tf_op args[1]
  18.3 3.4 %all-to-all-start = ((bf16[512,2,128]{0,2,1:T(8,128)(2,1)}), bf16[512,2,128]{0,2,1:T(8,128)(2,1)S(1)}, u32[]{:S(2)}, u32[]{:S(2)}) async-start(bf16[512,2,128]{0,2,1:T(8,128)(2,1)} %bitcast.2), calls=%async_computation | async-start | bytes 524288 | tf_op jit(solution)/shard_map/all_to_all | solution.py:166
  21.7 0.7 %iota_compare_fusion.5 = pred[1024]{0:T(1024)(128)(4,1)S(1)} fusion(s32[]{:T(128)} %bitcast), kind=kLoop, calls=%fused_computation.89 | loop fusion | flops 1024 | bytes 1028 | tf_op jit(solution)/shard_map/lt | solution.py:61
  22.4 0.8 %copy.22 = bf16[1,512,256]{1,2,0:T(8,128)(2,1)} copy(bf16[1,512,256]{2,1,0:T(8,128)(2,1)S(1)} %copy-done.1) | data formatting | bytes 524288 | tf_op args[0]
  24.1 3.5 %all-to-all-done = bf16[512,2,128]{0,2,1:T(8,128)(2,1)S(1)} async-done(((bf16[512,2,128]{0,2,1:T(8,128)(2,1)}), bf16[512,2,128]{0,2,1:T(8,128)(2,1)S(1)}, u32[]{:S(2)}, u32[]{:S(2)}) %all-to-all-start) | async-done | bytes 262176 | tf_op jit(solution)/shard_map/all_to_all | solution.py:166
  27.6 3.4 %all-to-all-start.1 = ((bf16[512,2,128]{0,2,1:T(8,128)(2,1)}), bf16[512,2,128]{0,2,1:T(8,128)(2,1)S(1)}, u32[]{:S(2)}, u32[]{:S(2)}) async-start(bf16[512,2,128]{0,2,1:T(8,128)(2,1)} %bitcast.5), calls=%async_computation.1 | async-start | bytes 524288 | tf_op jit(solution)/shard_map/all_to_all | solution.py:165
  31.3 4.9 %all-to-all-done.1 = bf16[512,2,128]{0,2,1:T(8,128)(2,1)S(1)} async-done(((bf16[512,2,128]{0,2,1:T(8,128)(2,1)}), bf16[512,2,128]{0,2,1:T(8,128)(2,1)S(1)}, u32[]{:S(2)}, u32[]{:S(2)}) %all-to-all-start.1) | async-done | bytes 262176 | tf_op jit(solution)/shard_map/all_to_all | solution.py:165
  36.2 0.8 %fusion.55 = (f32[512]{0:T(512)S(1)}, f32[512,1024]{0,1:T(8,128)S(1)}) fusion(bf16[1024,128]{1,0:T(8,128)(2,1)S(1)} %bitcast.88, bf16[2,512,128]{1,2,0:T(8,128)(2,1)S(1)} %bitcast.80, pred[1024]{0:T(1024)(128)(4,1)S(1)} %iota_compare_fusion.5, s32[512]{0:T(512)S(1)} %iota_add_fusion.1), kind=kOutput, calls=%fused_computation.109 | convolution fusion | flops 138935808 | bytes 2495488 | tf_op jit(solution)/shard_map/qd,kd->qk/dot_general | solution.py:64
  38.0 1.1 %fusion.56 = (f32[512]{0:T(512)S(1)}, f32[512,1024]{0,1:T(8,128)S(1)}) fusion(bf16[2,512,128]{1,2,0:T(8,128)(2,1)S(1)} %bitcast.81, bf16[1024,128]{1,0:T(8,128)(2,1)S(1)} %bitcast.89, bf16[512,128]{1,0:T(8,128)(2,1)S(1)} %collective-permute-done, pred[1024]{0:T(1024)(128)(4,1)S(1)} %get-tuple-element.23, pred[1024]{0:T(1024)(128)(4,1)S(1)} %get-tuple-element.24, ...), kind=kOutput, calls=%fused_computation.110 | convolution fusion | flops 139984384 | bytes 2631680 | tf_op jit(solution)/shard_map/qd,kd->qk/dot_general | solution.py:64
  41.4 1.0 %fusion.31 = f32[1024,256]{1,0:T(8,128)S(1)} fusion(f32[256,128]{1,0:T(8,128)S(1)} %get-tuple-element.6, bf16[1024,128]{1,0:T(8,128)(2,1)S(1)} %bitcast.86, f32[1024]{0:T(1024)S(1)} %select_negate_fusion), kind=kOutput, calls=%fused_computation.52 | convolution fusion | flops 402915328 | bytes 1445888 | tf_op jit(solution)/shard_map/dot_general | solution.py:17
  42.4 1.0 %bitcast_select_fusion.1 = f32[2,128,256]{2,1,0:T(8,128)S(1)} fusion(f32[2,128,256]{2,1,0:T(8,128)} %collective-permute-done.2, f32[1,2,128,256]{3,2,1,0:T(8,128)S(1)} %copy-done.2, pred[]{:T(512)} %bitcast.1), kind=kLoop, calls=%fused_computation.62 | loop fusion | flops 65536 | bytes 786433 | tf_op jit(solution)/shard_map/jit(_where)/select_n | solution.py:48
  43.4 1.0 %fusion.42 = f32[1024,256]{1,0:T(8,128)S(1)} fusion(f32[1024,128]{1,0:T(8,128)S(1)} %bitcast.77, f32[2,128,256]{2,1,0:T(8,128)S(1)} %bitcast_select_fusion.1), kind=kOutput, calls=%fused_computation.81 | convolution fusion | flops 402653184 | bytes 1703936 | tf_op jit(solution)/shard_map/dot_general | solution.py:17
  44.4 1.0 %fusion.44 = f32[1024,256]{1,0:T(8,128)S(1)} fusion(f32[1024,128]{1,0:T(8,128)S(1)} %bitcast.78, f32[2,128,256]{2,1,0:T(8,128)S(1)} %bitcast_select_fusion.1), kind=kOutput, calls=%fused_computation.83 | convolution fusion | flops 402653184 | bytes 1703936 | tf_op jit(solution)/shard_map/dot_general | solution.py:17
  45.4 2.1 %multiply_reduce_fusion.1 = (f32[128]{0:T(128)S(1)}, f32[256,128]{1,0:T(8,128)S(1)}) fusion(f32[256,128]{1,0:T(8,128)S(1)} %get-tuple-element.6, bf16[1024,128]{1,0:T(8,128)(2,1)S(1)} %bitcast.87, f32[1024]{0:T(1024)S(1)} %select_negate_fusion, f32[1024,256]{1,0:T(8,128)S(1)} %fusion.44, f32[1024,256]{1,0:T(8,128)S(1)} %fusion.42), kind=kOutput, calls=%fused_computation.73 | convolution fusion | flops 404324224 | bytes 2626048 | tf_op jit(solution)/shard_map/dot_general | solution.py:17
  47.5 1.5 %multiply_reduce_fusion.5 = (f32[256]{0:T(256)S(1)}, f32[128,256]{1,0:T(8,128)S(1)}) fusion(f32[1024,256]{1,0:T(8,128)S(1)} %fusion.42, f32[1024,256]{1,0:T(8,128)S(1)} %fusion.31, f32[1024,256]{1,0:T(8,128)S(1)} %fusion.44, bf16[1024,128]{1,0:T(8,128)(2,1)S(1)} %bitcast.90, f32[1024]{0:T(1024)S(1)} %bitcast.93, f32[2,128,256]{2,1,0:T(8,128)S(1)} %bitcast_select_fusion.1), kind=kOutput, calls=%fused_computation.79 | convolution fusion | flops 405372672 | bytes 3675136 | tf_op jit(solution)/shard_map/dot_general | solution.py:17
  48.9 1.4 %multiply_reduce_fusion.3 = (f32[256]{0:T(256)S(1)}, f32[128,256]{1,0:T(8,128)S(1)}) fusion(f32[1024,256]{1,0:T(8,128)S(1)} %fusion.31, f32[1024,256]{1,0:T(8,128)S(1)} %fusion.42, bf16[1024,128]{1,0:T(8,128)(2,1)S(1)} %bitcast.91, f32[1024]{0:T(1024)S(1)} %bitcast.94, f32[2,128,256]{2,1,0:T(8,128)S(1)} %bitcast_select_fusion.1), kind=kOutput, calls=%fused_computation.76 | convolution fusion | flops 404324096 | bytes 2626560 | tf_op jit(solution)/shard_map/dot_general | solution.py:17
  50.3 1.1 %fusion.43 = f32[1024,256]{1,0:T(8,128)S(1)} fusion(f32[1024,128]{1,0:T(8,128)S(1)} %bitcast.75, f32[2,128,256]{2,1,0:T(8,128)S(1)} %bitcast_select_fusion.1), kind=kOutput, calls=%fused_computation.82 | convolution fusion | flops 402653184 | bytes 1703936 | tf_op jit(solution)/shard_map/dot_general | solution.py:17
  51.5 1.0 %fusion.45 = f32[1024,256]{1,0:T(8,128)S(1)} fusion(f32[1024,128]{1,0:T(8,128)S(1)} %bitcast.76, f32[2,128,256]{2,1,0:T(8,128)S(1)} %bitcast_select_fusion.1), kind=kOutput, calls=%fused_computation.84 | convolution fusion | flops 402653184 | bytes 1703936 | tf_op jit(solution)/shard_map/dot_general | solution.py:17
  52.5 1.2 %multiply_reduce_fusion = (f32[1024]{0:T(1024)S(1)}, f32[1024,128]{1,0:T(8,128)S(1)}) fusion(f32[256,128]{1,0:T(8,128)S(1)} %get-tuple-element.6, f32[1024,256]{1,0:T(8,128)S(1)} %fusion.45, f32[1024,256]{1,0:T(8,128)S(1)} %fusion.43), kind=kOutput, calls=%fused_computation.54 | convolution fusion | flops 404225024 | bytes 2756608 | tf_op jit(solution)/shard_map/dot_general | solution.py:17
  53.7 1.1 %fusion.30 = bf16[1024,128]{1,0:T(8,128)(2,1)} fusion(f32[512,128]{1,0:T(8,128)S(1)} %fusion.26, f32[512,128]{1,0:T(8,128)S(1)} %fusion.25, f32[1024,128]{1,0:T(8,128)S(1)} %get-tuple-element.16, f32[1024]{0:T(1024)S(1)} %fusion.47, f32[128]{0:T(128)S(1)} %copy-done.4, f32[1024]{0:T(1024)S(1)} %add_sqrt_fusion.1), kind=kLoop, calls=%fused_computation.50 | loop fusion | flops 786432 | bytes 1319424 | tf_op jit(solution)/shard_map/convert_element_type | solution.py:90
  54.8 3.4 %all-to-all-start.3 = ((bf16[2,512,128]{2,1,0:T(8,128)(2,1)}), bf16[2,512,128]{2,1,0:T(8,128)(2,1)S(1)}, u32[]{:S(2)}, u32[]{:S(2)}) async-start(bf16[2,512,128]{2,1,0:T(8,128)(2,1)} %bitcast.20), calls=%async_computation.3 | async-start | bytes 524288 | tf_op jit(solution)/shard_map/all_to_all | solution.py:185
  58.4 0.7 %multiply_bitcast_fusion = f32[1,1,256,128]{3,2,1,0:T(8,128)} fusion(f32[256,128]{1,0:T(8,128)S(1)} %get-tuple-element.22, f32[128]{0:T(128)S(1)} %rsqrt_multiply_fusion.2), kind=kLoop, calls=%fused_computation.72 | loop fusion | flops 32768 | bytes 262656 | tf_op jit(solution)/shard_map/broadcast_in_dim | solution.py:187
  59.0 0.7 %maximum_bitcast_fusion = f32[1,1,2,128,256]{4,3,2,1,0:T(8,128)} fusion(f32[1,128,256]{2,1,0:T(8,128)S(1)} %multiply_bitcast_fusion.1, f32[1,128,256]{2,1,0:T(8,128)S(1)} %multiply_bitcast_fusion.2), kind=kLoop, calls=%fused_computation.61 | loop fusion | flops 65536 | bytes 524288 | tf_op jit(solution)/shard_map/broadcast_in_dim | solution.py:187
  59.7 3.7 %all-to-all-done.3 = bf16[2,512,128]{2,1,0:T(8,128)(2,1)S(1)} async-done(((bf16[2,512,128]{2,1,0:T(8,128)(2,1)}), bf16[2,512,128]{2,1,0:T(8,128)(2,1)S(1)}, u32[]{:S(2)}, u32[]{:S(2)}) %all-to-all-start.3) | async-done | bytes 262176 | tf_op jit(solution)/shard_map/all_to_all | solution.py:185
  63.7 0.9 %stack.12 = bf16[1,512,256]{2,1,0:T(8,128)(2,1)} reshape(bf16[512,2,128]{2,1,0:T(2,128)(2,1)S(1)} %copy.29) | data formatting | bytes 524288 | tf_op jit(solution)/shard_map/stack | solution.py:186
  (49 shorter events, 6.9 us)
Async XLA Ops:
  0.6 12.0 %copy-start = (s32[16,1]{0,1:T(1,128)S(1)}, s32[16,1]{0,1:T(1,128)}, u32[]{:S(2)}) copy-start(s32[16,1]{0,1:T(1,128)} %param.25) | copy-start | bytes 196
  0.6 21.8 %copy-start.1 = (bf16[1,512,256]{2,1,0:T(8,128)(2,1)S(1)}, bf16[1,512,256]{2,1,0:T(8,128)(2,1)}, u32[]{:S(2)}) copy-start(bf16[1,512,256]{2,1,0:T(8,128)(2,1)} %param.13) | copy-start | bytes 786436
  0.7 41.7 %collective-permute-start.2 = (f32[2,128,256]{2,1,0:T(8,128)}, f32[2,128,256]{2,1,0:T(8,128)}, u32[]{:S(2)}, u32[]{:S(2)}) collective-permute-start(f32[2,128,256]{2,1,0:T(8,128)} %bitcast.95), channel_id=1, source_target_pairs={{0,2},{2,4},{4,6},{6,8},{8,10},{10,12},{12,14},{14,16},{16,18},{18... | collective-permute-start | bytes 786440 | tf_op jit(solution)/shard_map/ppermute | solution.py:13
  1.2 39.0 %collective-permute-start.3 = (f32[256,128]{1,0:T(8,128)}, f32[256,128]{1,0:T(8,128)S(1)}, u32[]{:S(2)}, u32[]{:S(2)}) collective-permute-start(f32[256,128]{1,0:T(8,128)} %bitcast.96), channel_id=1, source_target_pairs={{0,2},{2,4},{4,6},{6,8},{8,10},{10,12},{12,14},{14,16},{16,18},{18... | collective-permute-start | bytes 393224 | tf_op jit(solution)/shard_map/ppermute | solution.py:13
  5.6 12.7 %all-to-all-start.2 = ((bf16[512,2,128]{0,2,1:T(8,128)(2,1)}), bf16[512,2,128]{0,2,1:T(8,128)(2,1)S(1)}, u32[]{:S(2)}, u32[]{:S(2)}) async-start(bf16[512,2,128]{0,2,1:T(8,128)(2,1)} %bitcast.9), calls=%async_computation.2 | async-start | bytes 524288 | tf_op jit(solution)/shard_map/all_to_all | solution.py:167
  9.0 29.0 %collective-permute-start = (bf16[512,128]{1,0:T(8,128)(2,1)}, bf16[512,128]{1,0:T(8,128)(2,1)S(1)}, u32[]{:S(2)}, u32[]{:S(2)}) collective-permute-start(bf16[512,128]{1,0:T(8,128)(2,1)} %param.17), channel_id=1, source_target_pairs={{0,2},{2,4},{4,6},{6,8},{8,10},{10,12},{12,14},{14,16},{16,18},{18... | collective-permute-start | bytes 393224 | tf_op jit(solution)/shard_map/ppermute | solution.py:13
  9.2 30.3 %collective-permute-start.1 = (bf16[512,128]{1,0:T(8,128)(2,1)}, bf16[512,128]{1,0:T(8,128)(2,1)S(1)}, u32[]{:S(2)}, u32[]{:S(2)}) collective-permute-start(bf16[512,128]{1,0:T(8,128)(2,1)} %param.18), channel_id=1, source_target_pairs={{0,2},{2,4},{4,6},{6,8},{8,10},{10,12},{12,14},{14,16},{16,18},{18... | collective-permute-start | bytes 393224 | tf_op jit(solution)/shard_map/ppermute | solution.py:13
  18.3 9.3 %all-to-all-start = ((bf16[512,2,128]{0,2,1:T(8,128)(2,1)}), bf16[512,2,128]{0,2,1:T(8,128)(2,1)S(1)}, u32[]{:S(2)}, u32[]{:S(2)}) async-start(bf16[512,2,128]{0,2,1:T(8,128)(2,1)} %bitcast.2), calls=%async_computation | async-start | bytes 524288 | tf_op jit(solution)/shard_map/all_to_all | solution.py:166
  27.6 8.6 %all-to-all-start.1 = ((bf16[512,2,128]{0,2,1:T(8,128)(2,1)}), bf16[512,2,128]{0,2,1:T(8,128)(2,1)S(1)}, u32[]{:S(2)}, u32[]{:S(2)}) async-start(bf16[512,2,128]{0,2,1:T(8,128)(2,1)} %bitcast.5), calls=%async_computation.1 | async-start | bytes 524288 | tf_op jit(solution)/shard_map/all_to_all | solution.py:165
  39.5 0.9 %copy-start.3 = (f32[1,256,128]{2,1,0:T(8,128)S(1)}, f32[1,256,128]{2,1,0:T(8,128)}, u32[]{:S(2)}) copy-start(f32[1,256,128]{2,1,0:T(8,128)} %param.22) | copy-start | bytes 393220
  40.1 2.3 %copy-start.2 = (f32[1,2,128,256]{3,2,1,0:T(8,128)S(1)}, f32[1,2,128,256]{3,2,1,0:T(8,128)}, u32[]{:S(2)}) copy-start(f32[1,2,128,256]{3,2,1,0:T(8,128)} %param.21) | copy-start | bytes 786436
  52.5 1.2 %copy-start.4 = (f32[128]{0:T(128)S(1)}, f32[128]{0:T(128)}, u32[]{:S(2)}) copy-start(f32[128]{0:T(128)} %param.23) | copy-start | bytes 1540
  52.5 5.8 %copy-start.5 = (f32[128]{0:T(128)S(1)}, f32[128]{0:T(128)}, u32[]{:S(2)}) copy-start(f32[128]{0:T(128)} %get-tuple-element.5) | copy-start | bytes 1540
  54.8 8.6 %all-to-all-start.3 = ((bf16[2,512,128]{2,1,0:T(8,128)(2,1)}), bf16[2,512,128]{2,1,0:T(8,128)(2,1)S(1)}, u32[]{:S(2)}, u32[]{:S(2)}) async-start(bf16[2,512,128]{2,1,0:T(8,128)(2,1)} %bitcast.20), calls=%async_computation.3 | async-start | bytes 524288 | tf_op jit(solution)/shard_map/all_to_all | solution.py:185
where the time goes:
time: 65.1 us; the launch traced here: 64.6 us
  starting transfers between devices  18.6 us (29%)
  matrix products  14.1 us (22%)
  waiting for transfers between devices  12.1 us (19%)
  local copies, waits for them, and re-layouts  9.09 us (14%)
  other arithmetic  8.43 us (13%)
  between operations  2.26 us (3%)
    dot_general x9, matrix products, highest(): return jnp.dot(left, right, precision=lax.Precision.HIGHEST)  11.2 us
    all_to_all x1, waiting for transfers between devices, on_device(): lax.all_to_all(queries[0], 'head', split_axis=1, concat_axis=0, tiled=True)  4.88 us
    ppermute x4, starting transfers between devices, from_behind(): lax.ppermute(shard, axis, [(i, (i + by) % size) for i in range(size)])  4.82 us
    unnamed x16, local copies, waits for them, and re-layouts  4.76 us
    all_to_all x1, waiting for transfers between devices, on_device(): lax.all_to_all(mixed_step, 'head', split_axis=0, concat_axis=1, tiled=True)  3.68 us
    all_to_all x1, waiting for transfers between devices, on_device(): lax.all_to_all(keys[0], 'head', split_axis=1, concat_axis=0, tiled=True)  3.49 us
    all_to_all x1, starting transfers between devices, on_device(): lax.all_to_all(keys[0], 'head', split_axis=1, concat_axis=0, tiled=True)  3.44 us
    all_to_all x1, starting transfers between devices, on_device(): lax.all_to_all(queries[0], 'head', split_axis=1, concat_axis=0, tiled=True)  3.44 us
  transfers between devices with their start and end apart: 8, of which 3 were waited for; matrix products, arithmetic and copies ran while one was open for 28% of the time, Pallas kernels for 0%

commit v1 on v0

v1 whole, which is shorter than its diff:
```python
import functools
import math

import jax
import jax.numpy as jnp
from jax import lax
from jax.experimental import pallas as pl
from jax.experimental.pallas import tpu as pltpu
from jax.sharding import PartitionSpec as P

epsilon = 1e-06
masked = -1e30
f32 = jnp.float32
bf16 = jnp.bfloat16

VMEM = pltpu.VMEM
in_vmem = pl.BlockSpec(memory_space=pltpu.VMEM)
in_smem = pl.BlockSpec(memory_space=pltpu.SMEM)
in_hbm = pl.BlockSpec(memory_space=pltpu.HBM)


def from_behind(shard, axis, by):
    size = lax.axis_size(axis)
    return lax.ppermute(shard, axis, [(i, (i + by) % size) for i in range(size)])


def local(array):
    return pltpu.with_memory_space_constraint(array, pltpu.VMEM)


def in_main(array):
    return pltpu.with_memory_space_constraint(array, pltpu.HBM)


def scalars(array):
    return pltpu.with_memory_space_constraint(array, pltpu.SMEM)


def run_copies(pairs, sems):
    copies = [
        pltpu.make_async_copy(source, target, sems.at[i]) for i, (source, target) in enumerate(pairs)
    ]
    for copy in copies:
        copy.start()
    for copy in copies:
        copy.wait()


def head_columns(index, width):
    return pl.ds(pl.multiple_of(index * width, width), width)


def wide(array):
    return jnp.concatenate([array, array], axis=1)


def halves(array):
    high = array.astype(bf16)
    low = (array - high.astype(f32)).astype(bf16)
    return high, low


def dot(left, right):
    return jnp.dot(left, right, preferred_element_type=f32)


def dot_nt(left, right):
    return lax.dot_general(left, right, (((1,), (1,)), ((), ())), preferred_element_type=f32)


def sigmoid(x):
    return 1.0 / (1.0 + jnp.exp(-x))


def pack_query(count, q_ref, *refs):
    outs, sems = refs[:-1], refs[-1]
    head = lax.axis_index("head")
    width = outs[0].shape[1]
    run_copies(
        [
            (q_ref.at[0, :, head_columns(lax.rem(head + s, count), width)], outs[s - 1])
            for s in range(1, count)
        ],
        sems,
    )


def pack_rest(count, q_ref, k_ref, v_ref, gu_ref, dn_ref, ids_ref, len_ref, *refs):
    own_q, own_k, own_v, packed, flags = refs[:5]
    sent_k, sent_v = refs[5 : 4 + count], refs[4 + count : 3 + 2 * count]
    ids, lens, sems = refs[-3:]
    head = lax.axis_index("head")
    here = lax.axis_index("ctx")
    width = own_q.shape[1]
    pairs = []
    for s in range(1, count):
        columns = head_columns(lax.rem(head + s, count), width)
        pairs.append((k_ref.at[0, :, columns], sent_k[s - 1]))
        pairs.append((v_ref.at[0, :, columns], sent_v[s - 1]))
    columns = head_columns(head, width)
    for whole_ref, own in ((q_ref, own_q), (k_ref, own_k), (v_ref, own_v)):
        pairs.append((whole_ref.at[0, :, columns], own))
    pairs.append((gu_ref.at[0, 0, 0], packed.at[0:width]))
    pairs.append((gu_ref.at[0, 0, 1], packed.at[width : 2 * width]))
    for group in range(dn_ref.shape[2] // width):
        rows = slice(group * width, (group + 1) * width)
        pairs.append((dn_ref.at[0, 0, rows], packed.at[2 * width : 3 * width, rows]))
    pairs.append((ids_ref, ids))
    pairs.append((len_ref, lens))
    run_copies(pairs, sems)
    size = ids.shape[1]
    before = lax.rem(here + size - 1, size)
    flags[0] = (ids[1, here] == ids[0, before]).astype(jnp.int32)
    flags[1] = lens[0, here]


def fast_forward(
    count, flags, packed, fresh_gu, fresh_dn, gain, rates, own_q, *refs
):
    got_q = refs[: count - 1]
    all_q, normed, weights, rate_row = refs[count - 1 :]
    rows, width = own_q.shape
    hidden = packed.shape[1]
    head = lax.axis_index("head")
    linked = flags[0] == 1
    length = flags[1]
    all_q[pl.ds(pl.multiple_of(head * rows, rows), rows), :] = own_q[...]
    for s in range(1, count):
        source = lax.rem(head + count - s, count)
        all_q[pl.ds(pl.multiple_of(source * rows, rows), rows), :] = got_q[s - 1][...]
    w_gate = jnp.where(linked, packed[0:width], fresh_gu[0, 0])
    w_up = jnp.where(linked, packed[width : 2 * width], fresh_gu[0, 1])
    down = [
        jnp.where(
            linked,
            packed[2 * width : 3 * width, g * width : (g + 1) * width],
            fresh_dn[0, g * width : (g + 1) * width],
        )
        for g in range(hidden // width)
    ]
    w_down = jnp.concatenate(down, axis=0)
    weights[0:width] = w_gate
    weights[width : 2 * width] = w_up
    for g in range(hidden // width):
        weights[2 * width : 3 * width, g * width : (g + 1) * width] = down[g]
    total = all_q.shape[0]
    token = lax.broadcasted_iota(jnp.int32, (1, total), 1)
    rate_row[...] = jnp.where(token < length, -rates[0], 0.0)
    gate2 = jnp.concatenate(halves(w_gate), axis=0)
    up2 = jnp.concatenate(halves(w_up), axis=0)
    down_high, down_low = halves(w_down)
    down2 = jnp.concatenate([down_high, down_low], axis=1)
    step = min(256, total)
    for start in range(0, total, step):
        block = all_q[start : start + step, :]
        block32 = block.astype(f32)
        unit = lax.rsqrt(jnp.mean(block32 * block32, axis=-1, keepdims=True) + epsilon)
        block2 = wide(block)
        gate = dot(block2, gate2) * unit
        up = dot(block2, up2) * unit
        high, low = halves(gate * sigmoid(gate) * up)
        both = dot(high, down2)
        fast = both[:, :width] + both[:, width:] + dot(low, down_high)
        scale = lax.rsqrt(jnp.mean(fast * fast, axis=-1, keepdims=True) + epsilon)
        row = start + lax.broadcasted_iota(jnp.int32, (step, 1), 0)
        scale = jnp.where(row < length, scale, 0.0)
        normed[start : start + step, :] = fast * scale * gain[...]


def attention_weights(count, tile, flags, all_q, tail_k, own_k, *refs):
    got_k = refs[: count - 1]
    keys, weights = refs[count - 1 :]
    rows, width = own_k.shape
    window = tail_k.shape[0]
    total = all_q.shape[0]
    head = lax.axis_index("head")
    linked = flags[0] == 1
    length = flags[1]
    keys[0:window, :] = tail_k[...]
    keys[pl.ds(pl.multiple_of(window + head * rows, 128), rows), :] = own_k[...]
    for s in range(1, count):
        source = lax.rem(head + count - s, count)
        keys[pl.ds(pl.multiple_of(window + source * rows, 128), rows), :] = got_k[s - 1][...]
    place = lax.broadcasted_iota(jnp.int32, (1, window + total), 1) - window
    open_key = (place < length) & ((place >= 0) | linked)
    bias = jnp.where(open_key, 0.0, masked)
    row = lax.broadcasted_iota(jnp.int32, (tile, tile), 0)
    column = lax.broadcasted_iota(jnp.int32, (tile, tile), 1)
    later = column > row
    same = column == row
    factor = math.log2(math.e) / math.sqrt(width)
    for index in range(total // tile):
        start = index * tile
        scores = dot_nt(all_q[start : start + tile, :], keys[start : start + tile + window, :])
        scores = scores * factor
        here = bias[:, start : start + tile + window]
        first = jnp.where(later, scores[:, :tile] + here[:, :tile], masked)
        middle = scores[:, tile:window] + here[:, tile:window]
        last = scores[:, window:]
        last = jnp.where(same, last, last + here[:, window:])
        last = jnp.where(later, masked, last)
        parts = [(0, first), (window, last)]
        if tile < window:
            parts.append((tile, middle))
        largest = functools.reduce(
            jnp.maximum, [jnp.max(part, axis=-1, keepdims=True) for _, part in parts]
        )
        parts = [(offset, jnp.exp2(part - largest)) for offset, part in parts]
        total_weight = sum(jnp.sum(part, axis=-1, keepdims=True) for _, part in parts)
        place_row = start + lax.broadcasted_iota(jnp.int32, (tile, 1), 0)
        scale = jnp.where(place_row < length, 1.0 / total_weight, 0.0)
        for offset, part in parts:
            weights[index, :, offset : offset + part.shape[1]] = (part * scale).astype(bf16)


def mixed_rows(tile, device, rows, weights, values, normed, out):
    window = weights.shape[2] - tile
    for t in range(rows // tile):
        start = pl.multiple_of(device * rows + t * tile, tile)
        index = device * (rows // tile) + t
        attended = dot(weights[index], values[pl.ds(start, tile + window), :])
        out[t * tile : (t + 1) * tile, :] = (attended + normed[pl.ds(start, tile), :]).astype(bf16)


def mix_sent(count, tile, weights, normed, tail_v, own_v, *refs):
    got_v = refs[: count - 1]
    values = refs[count - 1]
    outs = refs[count:]
    rows, width = own_v.shape
    window = tail_v.shape[0]
    head = lax.axis_index("head")
    values[0:window, :] = tail_v[...]
    values[pl.ds(pl.multiple_of(window + head * rows, 128), rows), :] = own_v[...]
    for s in range(1, count):
        source = lax.rem(head + count - s, count)
        values[pl.ds(pl.multiple_of(window + source * rows, 128), rows), :] = got_v[s - 1][...]
    for s in range(1, count):
        mixed_rows(
            tile, lax.rem(head + s, count), rows, weights, values, normed, outs[s - 1]
        )


def renormed(old_weight, gradient, axis):
    new_weight = old_weight - gradient
    old_square = jnp.mean(old_weight * old_weight, axis=axis, keepdims=True) + epsilon
    new_square = jnp.mean(new_weight * new_weight, axis=axis, keepdims=True) + epsilon
    return new_weight * (jnp.sqrt(old_square) / jnp.sqrt(new_square))


def update(
    tile, rows, weights, normed, values, keys, fast_weights, rate_row, mixed, new_gu, new_dn, own,
    gu, dn, sems,
):
    width = keys.shape[1]
    window = weights.shape[2] - tile
    hidden = fast_weights.shape[1]
    total = keys.shape[0] - window
    head = lax.axis_index("head")
    mixed_rows(tile, head, rows, weights, values, normed, own)
    out_copy = pltpu.make_async_copy(own, mixed.at[0, :, head_columns(head, width)], sems.at[0])
    out_copy.start()
    w_gate = fast_weights[0:width].T
    w_up = fast_weights[width : 2 * width].T
    w_down = jnp.concatenate(
        [
            fast_weights[2 * width : 3 * width, g * width : (g + 1) * width]
            for g in range(hidden // width)
        ],
        axis=0,
    )
    gate_up = jnp.concatenate(
        [
            jnp.concatenate(halves(w_gate), axis=1),
            jnp.concatenate(halves(w_up), axis=1),
        ],
        axis=0,
    )
    down = jnp.concatenate(halves(w_down), axis=1)
    ones = jnp.ones((8, 2 * width), bf16)
    grad_pair = jnp.zeros((2 * hidden, width), f32)
    grad_down = jnp.zeros((hidden, width), f32)
    step = min(256, total)
    for start in range(0, total, step):
        block_k = keys[window + start : window + start + step, :]
        block_v = values[window + start : window + start + step, :]
        block32 = block_k.astype(f32)
        square = jnp.concatenate(halves(block32 * block32), axis=1)
        unit = lax.rsqrt(dot_nt(ones, square)[:1] * (1.0 / width) + epsilon)
        both = dot_nt(gate_up, wide(block_k))
        gate = both[:hidden] * unit
        up = both[hidden:] * unit
        rate = rate_row[:, start : start + step]
        hidden_grad = dot_nt(down, wide(block_v)) * (rate * unit)
        share = sigmoid(gate)
        act = gate * share
        high_down, low_down = halves(act * up * rate)
        high_up, low_up = halves(hidden_grad * act)
        high_gate, low_gate = halves(hidden_grad * up * (share * (1.0 + gate * (1.0 - share))))
        stacked = jnp.concatenate([high_gate, high_up, low_gate, low_up], axis=0)
        pair = dot(stacked, block_k)
        grad_pair = grad_pair + (pair[: 2 * hidden] + pair[2 * hidden :])
        lower = dot(jnp.concatenate([high_down, low_down], axis=0), block_v)
        grad_down = grad_down + (lower[:hidden] + lower[hidden:])
    gu[0] = renormed(w_gate, grad_pair[:hidden], 1).T
    gu[1] = renormed(w_up, grad_pair[hidden:], 1).T
    dn[...] = renormed(w_down, grad_down, 0)
    first = pltpu.make_async_copy(gu, new_gu.at[0, 0], sems.at[1])
    second = pltpu.make_async_copy(dn, new_dn.at[0, 0], sems.at[2])
    first.start()
    second.start()
    out_copy.wait()
    first.wait()
    second.wait()


def place_received(count, *refs):
    got = refs[1:count]
    mixed, sems = refs[count:]
    width = got[0].shape[1]
    head = lax.axis_index("head")
    run_copies(
        [
            (got[s - 1], mixed.at[0, :, head_columns(lax.rem(head + count - s, count), width)])
            for s in range(1, count)
        ],
        sems,
    )


def params():
    return pltpu.CompilerParams(vmem_limit_bytes=24 * 1024 * 1024)


def on_device(
    queries,
    keys,
    values,
    rates,
    tail_keys,
    tail_values,
    state_in_gu,
    state_in_down,
    fresh_gu,
    fresh_down,
    out_gain,
    seq_ids,
    live_lengths,
):
    count = lax.axis_size("head")
    rows = queries.shape[1]
    width = queries.shape[2] // count
    window = tail_keys.shape[0]
    hidden = state_in_down.shape[2]
    total = rows * count
    tile = min(256, rows)
    piece = VMEM((rows, width), bf16)
    shifts = range(1, count)
    dma = pltpu.SemaphoreType.DMA

    sent_q = pl.pallas_call(
        functools.partial(pack_query, count),
        out_shape=[piece] * (count - 1),
        in_specs=[in_hbm],
        out_specs=[in_vmem] * (count - 1),
        scratch_shapes=[dma((count - 1,))],
        compiler_params=params(),
        name="pack_query",
    )(in_main(queries))
    got_q = [from_behind(sent_q[s - 1], "head", s) for s in shifts]
    packed_shape = VMEM((3 * width, hidden), f32)
    outs = pl.pallas_call(
        functools.partial(pack_rest, count),
        out_shape=[piece] * 3
        + [packed_shape, pltpu.SMEM((2,), jnp.int32)]
        + [piece] * (2 * count - 2),
        in_specs=[in_hbm] * 7,
        out_specs=[in_vmem] * 4 + [in_smem] + [in_vmem] * (2 * count - 2),
        scratch_shapes=[
            pltpu.SMEM(seq_ids.shape[::-1], jnp.int32),
            pltpu.SMEM(live_lengths.shape[::-1], jnp.int32),
            dma((2 * count + 5 + hidden // width,)),
        ],
        compiler_params=params(),
        name="pack_rest",
    )(
        *map(
            in_main,
            (queries, keys, values, state_in_gu, state_in_down, seq_ids.T, live_lengths.T),
        )
    )
    own_q, own_k, own_v, packed, flags = outs[:5]
    sent_k, sent_v = outs[5 : 4 + count], outs[4 + count :]
    moved = from_behind(packed, "ctx", 1)
    got_k = [from_behind(sent_k[s - 1], "head", s) for s in shifts]
    prior_keys = from_behind(tail_keys, "ctx", 1)
    got_v = [from_behind(sent_v[s - 1], "head", s) for s in shifts]
    prior_values = from_behind(tail_values, "ctx", 1)

    all_q, normed, fast_weights, rate_row = pl.pallas_call(
        functools.partial(fast_forward, count),
        out_shape=[
            VMEM((total, width), bf16),
            VMEM((total, width), f32),
            packed_shape,
            VMEM((1, total), f32),
        ],
        in_specs=[in_smem] + [in_vmem] * (5 + count),
        out_specs=[in_vmem] * 4,
        compiler_params=params(),
        name="fast_forward",
    )(
        scalars(flags),
        *map(local, (moved, fresh_gu, fresh_down, out_gain[None], rates, own_q, *got_q)),
    )
    joined = VMEM((window + total, width), bf16)
    all_keys, weights = pl.pallas_call(
        functools.partial(attention_weights, count, tile),
        out_shape=[joined, VMEM((total // tile, tile, tile + window), bf16)],
        in_specs=[in_smem] + [in_vmem] * (2 + count),
        out_specs=[in_vmem] * 2,
        compiler_params=params(),
        name="attention_weights",
    )(scalars(flags), *map(local, (all_q, prior_keys, own_k, *got_k)))
    all_values, *mixed_out = pl.pallas_call(
        functools.partial(mix_sent, count, tile),
        out_shape=[joined] + [piece] * (count - 1),
        in_specs=[in_vmem] * (3 + count),
        out_specs=[in_vmem] * count,
        compiler_params=params(),
        name="mix_sent",
    )(*map(local, (weights, normed, prior_values, own_v, *got_v)))
    mixed_in = [from_behind(mixed_out[s - 1], "head", s) for s in shifts]
    mixed, new_gu, new_down = pl.pallas_call(
        functools.partial(update, tile, rows),
        out_shape=[
            jax.ShapeDtypeStruct(queries.shape, bf16),
            jax.ShapeDtypeStruct(state_in_gu.shape, f32),
            jax.ShapeDtypeStruct(state_in_down.shape, f32),
        ],
        in_specs=[in_vmem] * 6,
        out_specs=[in_hbm] * 3,
        scratch_shapes=[
            VMEM((rows, width), bf16),
            VMEM(state_in_gu.shape[2:], f32),
            VMEM(state_in_down.shape[2:], f32),
            dma((3,)),
        ],
        compiler_params=params(),
        name="update",
    )(*map(local, (weights, normed, all_values, all_keys, fast_weights, rate_row)))
    mixed = pl.pallas_call(
        functools.partial(place_received, count),
        out_shape=jax.ShapeDtypeStruct(queries.shape, bf16),
        in_specs=[in_hbm] + [in_vmem] * (count - 1),
        out_specs=in_hbm,
        scratch_shapes=[dma((count - 1,))],
        input_output_aliases={0: 0},
        compiler_params=params(),
        name="place_received",
    )(in_main(mixed), *map(local, mixed_in))
    return (mixed, new_gu, new_down)


def solution(mesh):
    placed = (
        P(None, ("ctx", "head"), None),
        P(None, ("ctx", "head"), None),
        P(None, ("ctx", "head"), None),
        P(None, "head", "ctx"),
        P("ctx", "head"),
        P("ctx", "head"),
        P("ctx", "head", None, None, None),
        P("ctx", "head", None, None),
        P("head", None, None, None),
        P("head", None, None),
        P("head"),
        P(),
        P(),
    )
    return jax.shard_map(
        on_device,
        mesh=mesh,
        in_specs=placed,
        out_specs=(
            P(None, ("ctx", "head"), None),
            P("ctx", "head", None, None, None),
            P("ctx", "head", None, None),
        ),
        check_vma=False,
    )
```

time: 65.1 us -> 23.1 us (0.35)
  matrix products: 14.1 us -> 0 us
  Pallas kernels: 0 us -> 9.49 us
  local copies, waits for them, and re-layouts: 9.09 us -> 0.03 us
  starting transfers between devices: 18.6 us -> 9.58 us
  waiting for transfers between devices: 12.1 us -> 3.13 us
  other arithmetic: 8.43 us -> 0 us
  between operations: 2.26 us -> 0.75 us
    dot_general x13 -> x0, matrix products: 14.1 us -> none  [the longest x9 11.2 us: highest(): return jnp.dot(left, right, precision=lax.Precision.HIGHEST)]
    all_to_all x4 -> x0, starting transfers between devices: 13.8 us -> none  [the longest x1 3.44 us: on_device(): lax.all_to_all(keys[0], 'head', split_axis=1, concat_axis=0, tiled=True)]
    all_to_all x4 -> x0, waiting for transfers between devices: 12.1 us -> none  [the longest x1 4.88 us: on_device(): lax.all_to_all(queries[0], 'head', split_axis=1, concat_axis=0, tiled=True)]
    pallas_call x0 -> x7, Pallas kernels: none -> 9.49 us  [the longest x1 3.33 us: on_device(): pl.pallas_call(functools.partial(update, tile, rows), out_shape=[jax.Shap...]
    ppermute x4 -> x7, starting transfers between devices: 4.82 us -> 9.58 us  [from_behind(): lax.ppermute(shard, axis, [(i, (i + by) % size) for i in range(size)])]
    unnamed x16 -> x12, local copies, waits for them, and re-layouts: 4.76 us -> 0.03 us
    ppermute x4 -> x7, waiting for transfers between devices: 0.01 us -> 3.13 us  [from_behind(): lax.ppermute(shard, axis, [(i, (i + by) % size) for i in range(size)])]
    convert_element_type x2 -> x0, other arithmetic: 1.73 us -> none  [the longest x1 1.09 us: fast_block(): ((attended + rms_rows(fast_out) * head_gain) * live_rows).astype(jnp.bflo...]
  transfers between devices with their start and end apart: 8 -> 7, of which waited for: 3 -> 3; matrix products, arithmetic and copies ran while one was open for 28% -> 0% of each run, Pallas kernels for 0% -> 30%
where the time goes in v1:
time: 23.1 us; the launch traced here: 23 us
  starting transfers between devices  9.58 us (41%)
  Pallas kernels  9.49 us (41%)
  waiting for transfers between devices  3.13 us (14%)
  between operations  0.75 us (3%)
    ppermute x7, starting transfers between devices, from_behind(): lax.ppermute(shard, axis, [(i, (i + by) % size) for i in range(size)])  9.58 us
    pallas_call x1, Pallas kernels, on_device(): pl.pallas_call(functools.partial(update, tile, rows), out_shape=[jax.Shap...  3.33 us
    ppermute x7, waiting for transfers between devices, from_behind(): lax.ppermute(shard, axis, [(i, (i + by) % size) for i in range(size)])  3.13 us
    pallas_call x1, Pallas kernels, on_device(): pl.pallas_call(functools.partial(pack_rest, count), out_shape=[piece] * 3...  1.49 us
    pallas_call x1, Pallas kernels, on_device(): pl.pallas_call(functools.partial(attention_weights, count, tile), out_sha...  1.35 us
    pallas_call x1, Pallas kernels, on_device(): pl.pallas_call(functools.partial(fast_forward, count), out_shape=[VMEM((t...  1.34 us
    pallas_call x1, Pallas kernels, on_device(): pl.pallas_call(functools.partial(pack_query, count), out_shape=[piece] *...  0.91 us
    pallas_call x1, Pallas kernels, on_device(): pl.pallas_call(functools.partial(place_received, count), out_shape=jax.Sh...  0.66 us
  transfers between devices with their start and end apart: 7, of which 3 were waited for; matrix products, arithmetic and copies ran while one was open for 0% of the time, Pallas kernels for 30%

profile of v1, /device:TPU:0, one launch (start us, length us, event | category | flops | bytes accessed | tf_op | source)
XLA Modules:
  0.0 23.0 jit_solution(11951773543583727470)
XLA Ops:
  0.6 0.0 copy-start.4
  0.6 0.0 copy-start.5
  0.7 0.0 copy-start.3
  0.7 0.0 copy-start.1
  0.7 0.0 copy-start
  0.7 0.0 copy-start.2
  0.7 1.5 %pack_rest.1 = (bf16[512,128]{1,0:T(8,128)(2,1)S(1)}, bf16[512,128]{1,0:T(8,128)(2,1)S(1)}, bf16[512,128]{1,0:T(8,128)(2,1)S(1)}, f32[384,256]{1,0:T(8,128)S(1)}...) custom-call(bf16[1,512,256]{2,1,0:T(8,128)(2,1)} %q_ref.3, bf16[1,512,256]{2,1,0:T(8,128)(2,1)} %k_ref.1, ...), custom_call_target="tpu_custom_call" | custom-call | tf_op jit(solution)/shard_map/pack_rest/pallas_call | solution.py:371
  2.2 0.5 %collective-permute-start = (f32[384,256]{1,0:T(8,128)S(1)}, f32[384,256]{1,0:T(8,128)S(1)}, u32[]{:S(2)}, u32[]{:S(2)}) collective-permute-start(f32[384,256]{1,0:T(8,128)S(1)} %get-tuple-element.22), channel_id=1, source_target_pairs={{0,2},{2,4},{4,6},{6,8},{8,10},{10,12},{12,14},{14,16},{16,18},{18... | collective-permute-start | bytes 1179656 | tf_op jit(solution)/shard_map/ppermute | solution.py:24
  2.7 0.9 %pack_query.1 = bf16[512,128]{1,0:T(8,128)(2,1)S(1)} custom-call(bf16[1,512,256]{2,1,0:T(8,128)(2,1)} %q_ref.3), custom_call_target="tpu_custom_call" | custom-call | tf_op jit(solution)/shard_map/pack_query/pallas_call | solution.py:360
  3.6 2.6 %collective-permute-start.1 = (bf16[512,128]{1,0:T(8,128)(2,1)S(1)}, bf16[512,128]{1,0:T(8,128)(2,1)S(1)}, u32[]{:S(2)}, u32[]{:S(2)}) collective-permute-start(bf16[512,128]{1,0:T(8,128)(2,1)S(1)} %pack_query.1), channel_id=1, source_target_pairs={{0,1},{1,0},{2,3},{3,2},{4,5},{5,4},{6,7},{7,6},{8,9},{9,8},{10,11... | collective-permute-start | bytes 393224 | tf_op jit(solution)/shard_map/ppermute | solution.py:24
  6.2 0.0 copy-done.4
  6.2 1.3 %collective-permute-start.2 = (bf16[512,128]{1,0:T(8,128)(2,1)S(1)}, bf16[512,128]{1,0:T(8,128)(2,1)S(1)}, u32[]{:S(2)}, u32[]{:S(2)}) collective-permute-start(bf16[512,128]{1,0:T(8,128)(2,1)S(1)} %copy-done.4), channel_id=1, source_target_pairs={{0,2},{2,4},{4,6},{6,8},{8,10},{10,12},{12,14},{14,16},{16,18},{18... | collective-permute-start | bytes 393224 | tf_op jit(solution)/shard_map/ppermute | solution.py:24
  7.5 0.5 %collective-permute-start.3 = (bf16[512,128]{1,0:T(8,128)(2,1)S(1)}, bf16[512,128]{1,0:T(8,128)(2,1)S(1)}, u32[]{:S(2)}, u32[]{:S(2)}) collective-permute-start(bf16[512,128]{1,0:T(8,128)(2,1)S(1)} %get-tuple-element.26), channel_id=1, source_target_pairs={{0,1},{1,0},{2,3},{3,2},{4,5},{5,4},{6,7},{7,6},{8,9},{9,8},{10,11... | collective-permute-start | bytes 393224 | tf_op jit(solution)/shard_map/ppermute | solution.py:24
  8.1 0.0 copy-done.5
  8.1 0.0 collective-permute-start.4
  8.1 1.4 %collective-permute-done.1.refs_0_ = bf16[512,128]{1,0:T(8,128)(2,1)S(1)} collective-permute-done((bf16[512,128]{1,0:T(8,128)(2,1)S(1)}, bf16[512,128]{1,0:T(8,128)(2,1)S(1)}, u32[]{:S(2)}, u32[]{:S(2)}) %collective-permute-start.1) | collective-permute-done | bytes 131104 | tf_op jit(solution)/shard_map/ppermute | solution.py:24
  9.5 2.5 %collective-permute-start.5 = (bf16[512,128]{1,0:T(8,128)(2,1)S(1)}, bf16[512,128]{1,0:T(8,128)(2,1)S(1)}, u32[]{:S(2)}, u32[]{:S(2)}) collective-permute-start(bf16[512,128]{1,0:T(8,128)(2,1)S(1)} %get-tuple-element.30), channel_id=1, source_target_pairs={{0,1},{1,0},{2,3},{3,2},{4,5},{5,4},{6,7},{7,6},{8,9},{9,8},{10,11... | collective-permute-start | bytes 393224 | tf_op jit(solution)/shard_map/ppermute | solution.py:24
  12.0 1.2 %collective-permute-done.packed = f32[384,256]{1,0:T(8,128)S(1)} collective-permute-done((f32[384,256]{1,0:T(8,128)S(1)}, f32[384,256]{1,0:T(8,128)S(1)}, u32[]{:S(2)}, u32[]{:S(2)}) %collective-permute-start) | collective-permute-done | bytes 393248 | tf_op jit(solution)/shard_map/ppermute | solution.py:24
  13.2 0.0 copy-done.3
  13.2 0.0 copy-done.1
  13.2 0.0 copy-done
  13.2 1.3 %fast_forward.1 = (bf16[1024,128]{1,0:T(8,128)(2,1)S(1)}, f32[1024,128]{1,0:T(8,128)S(1)}, f32[384,256]{1,0:T(8,128)S(1)}, f32[1,1024]{1,0:T(1,128)S(1)}) custom-call(s32[2]{0:T(128)S(4)} %get-tuple-element.21.flags, f32[384,256]{1,0:T(8,128)S(1)} %collective-permute-done.packed, f32[1,2,128,256]{3,2,1,0:T(8,128)S(1)} %copy-done, ...), custom_call_target="tpu_custom_call" | custom-call | tf_op jit(solution)/shard_map/fast_forward/pallas_call | solution.py:399
  14.5 0.0 collective-permute-done.2.tail_k
  14.6 0.0 collective-permute-done.3.refs_0_
  14.6 1.3 %attention_weights.1 = (bf16[1536,128]{1,0:T(8,128)(2,1)S(1)}, bf16[4,256,768]{2,1,0:T(8,128)(2,1)S(1)}) custom-call(s32[2]{0:T(128)S(4)} %get-tuple-element.21.flags, bf16[1024,128]{1,0:T(8,128)(2,1)S(1)} %get-tuple-element.24.all_q, bf16[512,128]{1,0:T(8,128)(2,1)S(1)} %collective-permute-done.2.tail_k, bf16[512,128]{1,0:T(8,128)(2,1)S(1)} %get-tuple-element.25.own_k, ...), custom_call_target="tpu_custom_call" | custom-call | tf_op jit(solution)/shard_map/attention_weights/pallas_call | solution.py:416
  15.9 0.0 collective-permute-done.4.tail_v
  16.0 0.0 collective-permute-done.5.refs_0_
  16.0 0.4 %mix_sent.1 = (bf16[1536,128]{1,0:T(8,128)(2,1)S(1)}, bf16[512,128]{1,0:T(8,128)(2,1)S(1)}) custom-call(bf16[4,256,768]{2,1,0:T(8,128)(2,1)S(1)} %get-tuple-element.27.weights, f32[1024,128]{1,0:T(8,128)S(1)} %get-tuple-element.28.normed, bf16[512,128]{1,0:T(8,128)(2,1)S(1)} %collective-permute-done.4.tail_v, bf16[512,128]{1,0:T(8,128)(2,1)S(1)} %get-tuple-element.29.own_v, ...), custom_call_target="tpu_custom_call" | custom-call | tf_op jit(solution)/shard_map/mix_sent/pallas_call | solution.py:424
  16.4 2.1 %collective-permute-start.6 = (bf16[512,128]{1,0:T(8,128)(2,1)S(1)}, bf16[512,128]{1,0:T(8,128)(2,1)S(1)}, u32[]{:S(2)}, u32[]{:S(2)}) collective-permute-start(bf16[512,128]{1,0:T(8,128)(2,1)S(1)} %get-tuple-element.36), channel_id=1, source_target_pairs={{0,1},{1,0},{2,3},{3,2},{4,5},{5,4},{6,7},{7,6},{8,9},{9,8},{10,11... | collective-permute-start | bytes 393224 | tf_op jit(solution)/shard_map/ppermute | solution.py:24
  18.5 3.3 %update.1 = (bf16[1,512,256]{2,1,0:T(8,128)(2,1)}, f32[1,1,2,128,256]{4,3,2,1,0:T(8,128)}, f32[1,1,256,128]{3,2,1,0:T(8,128)}) custom-call(bf16[4,256,768]{2,1,0:T(8,128)(2,1)S(1)} %get-tuple-element.27.weights, f32[1024,128]{1,0:T(8,128)S(1)} %get-tuple-element.28.normed, bf16[1536,128]{1,0:T(8,128)(2,1)S(1)} %get-tuple-element.31.values, ...), custom_call_target="tpu_custom_call" | custom-call | tf_op jit(solution)/shard_map/update/pallas_call | solution.py:433
  21.8 0.5 %collective-permute-done.6.refs_1_ = bf16[512,128]{1,0:T(8,128)(2,1)S(1)} collective-permute-done((bf16[512,128]{1,0:T(8,128)(2,1)S(1)}, bf16[512,128]{1,0:T(8,128)(2,1)S(1)}, u32[]{:S(2)}, u32[]{:S(2)}) %collective-permute-start.6) | collective-permute-done | bytes 131104 | tf_op jit(solution)/shard_map/ppermute | solution.py:24
  22.3 0.7 %place_received.1 = bf16[1,512,256]{2,1,0:T(8,128)(2,1)} custom-call(bf16[1,512,256]{2,1,0:T(8,128)(2,1)} %get-tuple-element.35.refs_0_, bf16[512,128]{1,0:T(8,128)(2,1)S(1)} %collective-permute-done.6.refs_1_), custom_call_target="tpu_custom_call", output_to_operand_aliasing={{}: (0, {})} | custom-call | tf_op jit(solution)/shard_map/place_received/pallas_call | solution.py:451
  (1 shorter events, 0.0 us)
Async XLA Ops:
  0.6 5.6 %copy-start.4 = (bf16[512,128]{1,0:T(8,128)(2,1)S(1)}, bf16[512,128]{1,0:T(8,128)(2,1)}, u32[]{:S(2)}) copy-start(bf16[512,128]{1,0:T(8,128)(2,1)} %param.17) | copy-start | bytes 393220
  0.6 7.4 %copy-start.5 = (bf16[512,128]{1,0:T(8,128)(2,1)S(1)}, bf16[512,128]{1,0:T(8,128)(2,1)}, u32[]{:S(2)}) copy-start(bf16[512,128]{1,0:T(8,128)(2,1)} %param.18) | copy-start | bytes 393220
  0.7 12.5 %copy-start.3 = (f32[128]{0:T(128)S(1)}, f32[128]{0:T(128)}, u32[]{:S(2)}) copy-start(f32[128]{0:T(128)} %param.23) | copy-start | bytes 1540
  0.7 12.5 %copy-start.1 = (f32[1,256,128]{2,1,0:T(8,128)S(1)}, f32[1,256,128]{2,1,0:T(8,128)}, u32[]{:S(2)}) copy-start(f32[1,256,128]{2,1,0:T(8,128)} %fresh_dn.1) | copy-start | bytes 393220
  0.7 12.5 %copy-start = (f32[1,2,128,256]{3,2,1,0:T(8,128)S(1)}, f32[1,2,128,256]{3,2,1,0:T(8,128)}, u32[]{:S(2)}) copy-start(f32[1,2,128,256]{3,2,1,0:T(8,128)} %fresh_gu.1) | copy-start | bytes 786436
  0.7 12.5 %copy-start.2 = (f32[1,1,1024]{2,1,0:T(1,128)S(1)}, f32[1,1,1024]{2,1,0:T(1,128)}, u32[]{:S(2)}) copy-start(f32[1,1,1024]{2,1,0:T(1,128)} %rates.1) | copy-start | bytes 12292
  2.2 11.0 %collective-permute-start = (f32[384,256]{1,0:T(8,128)S(1)}, f32[384,256]{1,0:T(8,128)S(1)}, u32[]{:S(2)}, u32[]{:S(2)}) collective-permute-start(f32[384,256]{1,0:T(8,128)S(1)} %get-tuple-element.22), channel_id=1, source_target_pairs={{0,2},{2,4},{4,6},{6,8},{8,10},{10,12},{12,14},{14,16},{16,18},{18... | collective-permute-start | bytes 1179656 | tf_op jit(solution)/shard_map/ppermute | solution.py:24
  3.6 5.9 %collective-permute-start.1 = (bf16[512,128]{1,0:T(8,128)(2,1)S(1)}, bf16[512,128]{1,0:T(8,128)(2,1)S(1)}, u32[]{:S(2)}, u32[]{:S(2)}) collective-permute-start(bf16[512,128]{1,0:T(8,128)(2,1)S(1)} %pack_query.1), channel_id=1, source_target_pairs={{0,1},{1,0},{2,3},{3,2},{4,5},{5,4},{6,7},{7,6},{8,9},{9,8},{10,11... | collective-permute-start | bytes 393224 | tf_op jit(solution)/shard_map/ppermute | solution.py:24
  6.2 8.4 %collective-permute-start.2 = (bf16[512,128]{1,0:T(8,128)(2,1)S(1)}, bf16[512,128]{1,0:T(8,128)(2,1)S(1)}, u32[]{:S(2)}, u32[]{:S(2)}) collective-permute-start(bf16[512,128]{1,0:T(8,128)(2,1)S(1)} %copy-done.4), channel_id=1, source_target_pairs={{0,2},{2,4},{4,6},{6,8},{8,10},{10,12},{12,14},{14,16},{16,18},{18... | collective-permute-start | bytes 393224 | tf_op jit(solution)/shard_map/ppermute | solution.py:24
  7.5 7.0 %collective-permute-start.3 = (bf16[512,128]{1,0:T(8,128)(2,1)S(1)}, bf16[512,128]{1,0:T(8,128)(2,1)S(1)}, u32[]{:S(2)}, u32[]{:S(2)}) collective-permute-start(bf16[512,128]{1,0:T(8,128)(2,1)S(1)} %get-tuple-element.26), channel_id=1, source_target_pairs={{0,1},{1,0},{2,3},{3,2},{4,5},{5,4},{6,7},{7,6},{8,9},{9,8},{10,11... | collective-permute-start | bytes 393224 | tf_op jit(solution)/shard_map/ppermute | solution.py:24
  8.1 7.9 %collective-permute-start.4 = (bf16[512,128]{1,0:T(8,128)(2,1)S(1)}, bf16[512,128]{1,0:T(8,128)(2,1)S(1)}, u32[]{:S(2)}, u32[]{:S(2)}) collective-permute-start(bf16[512,128]{1,0:T(8,128)(2,1)S(1)} %copy-done.5), channel_id=1, source_target_pairs={{0,2},{2,4},{4,6},{6,8},{8,10},{10,12},{12,14},{14,16},{16,18},{18... | collective-permute-start | bytes 393224 | tf_op jit(solution)/shard_map/ppermute | solution.py:24
  9.5 6.5 %collective-permute-start.5 = (bf16[512,128]{1,0:T(8,128)(2,1)S(1)}, bf16[512,128]{1,0:T(8,128)(2,1)S(1)}, u32[]{:S(2)}, u32[]{:S(2)}) collective-permute-start(bf16[512,128]{1,0:T(8,128)(2,1)S(1)} %get-tuple-element.30), channel_id=1, source_target_pairs={{0,1},{1,0},{2,3},{3,2},{4,5},{5,4},{6,7},{7,6},{8,9},{9,8},{10,11... | collective-permute-start | bytes 393224 | tf_op jit(solution)/shard_map/ppermute | solution.py:24
  16.4 5.9 %collective-permute-start.6 = (bf16[512,128]{1,0:T(8,128)(2,1)S(1)}, bf16[512,128]{1,0:T(8,128)(2,1)S(1)}, u32[]{:S(2)}, u32[]{:S(2)}) collective-permute-start(bf16[512,128]{1,0:T(8,128)(2,1)S(1)} %get-tuple-element.36), channel_id=1, source_target_pairs={{0,1},{1,0},{2,3},{3,2},{4,5},{5,4},{6,7},{7,6},{8,9},{9,8},{10,11... | collective-permute-start | bytes 393224 | tf_op jit(solution)/shard_map/ppermute | solution.py:24

commit v2 on v0

v2 whole, which is shorter than its diff:
```python
import functools
import math

import jax
import jax.numpy as jnp
from jax import lax
from jax.experimental import pallas as pl
from jax.experimental.pallas import tpu as pltpu
from jax.sharding import PartitionSpec as P

epsilon = 1e-06
masked = -1e30
f32 = jnp.float32
bf16 = jnp.bfloat16

VMEM = pltpu.VMEM
in_vmem = pl.BlockSpec(memory_space=pltpu.VMEM)
in_smem = pl.BlockSpec(memory_space=pltpu.SMEM)
in_hbm = pl.BlockSpec(memory_space=pltpu.HBM)


def from_behind(shard, axis, by):
    size = lax.axis_size(axis)
    return lax.ppermute(shard, axis, [(i, (i + by) % size) for i in range(size)])


def local(array):
    return pltpu.with_memory_space_constraint(array, pltpu.VMEM)


def in_main(array):
    return pltpu.with_memory_space_constraint(array, pltpu.HBM)


def scalars(array):
    return pltpu.with_memory_space_constraint(array, pltpu.SMEM)


def run_copies(pairs, sems):
    copies = [
        pltpu.make_async_copy(source, target, sems.at[i]) for i, (source, target) in enumerate(pairs)
    ]
    for copy in copies:
        copy.start()
    for copy in copies:
        copy.wait()


def head_columns(index, width):
    return pl.ds(pl.multiple_of(index * width, width), width)


def wide(array):
    return jnp.concatenate([array, array], axis=1)


def halves(array):
    high = array.astype(bf16)
    low = (array - high.astype(f32)).astype(bf16)
    return high, low


def dot(left, right):
    return jnp.dot(left, right, preferred_element_type=f32)


def dot_nt(left, right):
    return lax.dot_general(left, right, (((1,), (1,)), ((), ())), preferred_element_type=f32)


def sigmoid(x):
    return 0.5 * jnp.tanh(0.5 * x) + 0.5


def row_block(index, rows):
    return pl.ds(pl.multiple_of(index * rows, rows), rows)


def fast_rows(high, low, first_row, length, down2, gain):
    count = high.shape[0]
    width = down2.shape[1] // 2
    both = dot(high, down2[...])
    fast = both[:, :width] + both[:, width:] + dot(low, down2[:, :width])
    scale = lax.rsqrt(jnp.mean(fast * fast, axis=-1, keepdims=True) + epsilon)
    row = first_row + lax.broadcasted_iota(jnp.int32, (count, 1), 0)
    return fast * jnp.where(row < length, scale, 0.0) * gain[...]


def store_weights(queries, keys, first_row, length, linked, out):
    tile, width = queries.shape
    window = keys.shape[0] - tile
    place = first_row - window + lax.broadcasted_iota(jnp.int32, (1, tile + window), 1)
    bias = jnp.where((place < length) & ((place >= 0) | linked), 0.0, masked)
    row = lax.broadcasted_iota(jnp.int32, (tile, tile), 0)
    column = lax.broadcasted_iota(jnp.int32, (tile, tile), 1)
    later = column > row
    factor = math.log2(math.e) / math.sqrt(width)
    scores = dot_nt(queries, keys) * factor
    first = jnp.where(later, scores[:, :tile] + bias[:, :tile], masked)
    last = scores[:, window:]
    last = jnp.where(column == row, last, last + bias[:, window:])
    last = jnp.where(later, masked, last)
    parts = [(0, first), (window, last)]
    if tile < window:
        parts.append((tile, scores[:, tile:window] + bias[:, tile:window]))
    largest = functools.reduce(
        jnp.maximum, [jnp.max(part, axis=-1, keepdims=True) for _, part in parts]
    )
    parts = [(offset, jnp.exp2(part - largest)) for offset, part in parts]
    total = sum(jnp.sum(part, axis=-1, keepdims=True) for _, part in parts)
    token = first_row + lax.broadcasted_iota(jnp.int32, (tile, 1), 0)
    scale = jnp.where(token < length, 1.0 / total, 0.0)
    for offset, part in parts:
        out[:, offset : offset + part.shape[1]] = (part * scale).astype(bf16)


def join(count, window, own, got, joined):
    rows = own.shape[0]
    head = lax.axis_index("head")
    joined[pl.ds(pl.multiple_of(window + head * rows, rows), rows), :] = own[...]
    for s in range(1, count):
        source = lax.rem(head + count - s, count)
        joined[pl.ds(pl.multiple_of(window + source * rows, rows), rows), :] = got[s - 1][...]


def pack(count, k_ref, v_ref, dn_ref, tail_k, tail_v, *refs):
    down_keys, last_v = refs[:2]
    sent_k, sent_v = refs[2 : 1 + count], refs[1 + count : 2 * count]
    down, sems = refs[-2:]
    head = lax.axis_index("head")
    hidden, width = down.shape
    pairs = [(dn_ref.at[0, 0], down)]
    for s in range(1, count):
        columns = head_columns(lax.rem(head + s, count), width)
        pairs.append((k_ref.at[0, :, columns], sent_k[s - 1]))
        pairs.append((v_ref.at[0, :, columns], sent_v[s - 1]))
    pairs += [(tail_k, down_keys.at[2 * hidden :]), (tail_v, last_v)]
    run_copies(pairs, sems)
    high, low = halves(down[...])
    down_keys[0:hidden] = high
    down_keys[hidden : 2 * hidden] = low


def load(
    count, k_ref, v_ref, fresh_gu, fresh_dn, gain, rates, ids_ref, len_ref, _, own_k, own_v, fresh,
    gain_row, rate_row, flags, ids, lens, sems
):
    head = lax.axis_index("head")
    here = lax.axis_index("ctx")
    width = own_k.shape[1]
    columns = head_columns(head, width)
    pairs = [
        (k_ref.at[0, :, columns], own_k),
        (v_ref.at[0, :, columns], own_v),
        (fresh_gu.at[0, 0], fresh.at[0:width]),
        (fresh_gu.at[0, 1], fresh.at[width : 2 * width]),
    ]
    for group in range(fresh_dn.shape[1] // width):
        part = slice(group * width, (group + 1) * width)
        pairs.append((fresh_dn.at[0, part], fresh.at[2 * width : 3 * width, part]))
    pairs += [(gain, gain_row), (rates.at[0], rate_row), (ids_ref, ids), (len_ref, lens)]
    run_copies(pairs, sems)
    size = ids.shape[1]
    before = lax.rem(here + size - 1, size)
    flags[0] = (ids[1, here] == ids[0, before]).astype(jnp.int32)
    flags[1] = lens[0, here]


def join_queries(*refs):
    joined = refs[-1]
    rows = refs[0].shape[0]
    for index, part in enumerate(refs[:-1]):
        joined[index * rows : (index + 1) * rows, :] = part[...]


def query_hidden(queries, gate2, up2, highs, lows):
    total, width = queries.shape
    step = min(256, total)
    for start in range(0, total, step):
        block = queries[start : start + step, :]
        block32 = block.astype(f32)
        unit = lax.rsqrt(jnp.mean(block32 * block32, axis=-1, keepdims=True) + epsilon)
        doubled = wide(block)
        gate = dot(doubled, gate2[...]) * unit
        up = dot(doubled, up2[...]) * unit
        high, low = halves(gate * sigmoid(gate) * up)
        highs[start : start + step, :] = high
        lows[start : start + step, :] = low


def choose_gate_up(flags, _, got_gu, fresh, rates, gate2, up2, turned2, turned, rate_row):
    hidden = fresh.shape[1]
    width = got_gu.shape[0] // 2
    linked = flags[0] == 1
    length = flags[1]
    for index, split in enumerate((gate2, up2)):
        rows = slice(index * width, (index + 1) * width)
        weight = jnp.where(linked, got_gu[rows], fresh[rows])
        split[...] = jnp.concatenate(halves(weight), axis=0)
        part = slice(index * hidden, (index + 1) * hidden)
        weight = weight.T
        turned[part] = weight
        turned2[part] = jnp.concatenate(halves(weight), axis=1)
    token = lax.broadcasted_iota(jnp.int32, rates.shape, 1)
    rate_row[...] = jnp.where(token < length, -rates[...], 0.0)


def key_hidden(
    count, window, _, turned2, rate_row, own_k, *refs
):
    got_k, (keys, gate_part, up_part, down_steps) = refs[: count - 1], refs[count - 1 :]
    rows, width = own_k.shape
    hidden = turned2.shape[0] // 2
    total = count * rows
    join(count, window, own_k, got_k, keys)
    ones = jnp.ones((8, 2 * width), bf16)
    step = min(256, total)
    for start in range(0, total, step):
        block = keys[window + start : window + start + step, :]
        block32 = block.astype(f32)
        square = jnp.concatenate(halves(block32 * block32), axis=1)
        unit = lax.rsqrt(dot_nt(ones, square)[:1] * (1.0 / width) + epsilon)
        rate = rate_row[:, start : start + step]
        scale = rate * unit
        both = dot_nt(turned2[...], wide(block))
        gate = both[:hidden] * unit
        up = both[hidden:] * unit
        share = sigmoid(gate)
        act = gate * share
        gate_part[:, start : start + step] = up * (share + act * (1.0 - share)) * scale
        up_part[:, start : start + step] = act * scale
        down_steps[:, start : start + step] = (act * up * rate).astype(bf16)


def choose_down(flags, down_keys, fresh, keys, down2, down, joined):
    hidden, width = down.shape
    window = down_keys.shape[0] - 2 * hidden
    linked = flags[0] == 1
    fresh_down = jnp.concatenate(
        [fresh[2 * width :, g * width : (g + 1) * width] for g in range(hidden // width)], axis=0
    )
    got_down = down_keys[0:hidden].astype(f32) + down_keys[hidden : 2 * hidden].astype(f32)
    w_down = jnp.where(linked, got_down, fresh_down)
    down[...] = w_down
    down2[...] = jnp.concatenate(halves(w_down), axis=1)
    joined[0:window] = down_keys[2 * hidden :]


def sent_rows(count, tile, flags, down2, gain, keys, queries, highs, lows, weights, normed):
    rows = queries.shape[0] // count
    window = keys.shape[0] - count * rows
    linked = flags[0] == 1
    length = flags[1]
    head = lax.axis_index("head")
    for s in range(1, count):
        device = lax.rem(head + s, count)
        for t in range(rows // tile):
            place = (s - 1) * rows + t * tile
            start = pl.multiple_of(device * rows + t * tile, tile)
            span = slice(place, place + tile)
            normed[span, :] = fast_rows(highs[span, :], lows[span, :], start, length, down2, gain)
            store_weights(
                queries[span, :],
                keys[pl.ds(start, tile + window), :],
                start,
                length,
                linked,
                weights.at[place // tile],
            )


def start_values(_, tail_v, own_v, values):
    window = tail_v.shape[0]
    values[0:window, :] = tail_v[...]
    join(1, window, own_v, [], values)


def mix_sent(count, weights, normed, _, *refs):
    got_v, values, outs = refs[: count - 1], refs[count - 1], refs[count:]
    rows = got_v[0].shape[0]
    tile, span = weights.shape[1:]
    head = lax.axis_index("head")
    for s in range(1, count):
        source = lax.rem(head + count - s, count)
        start = span - tile + source * rows
        values[pl.ds(pl.multiple_of(start, rows), rows), :] = got_v[s - 1][...]
    for s in range(1, count):
        device = lax.rem(head + s, count)
        for t in range(rows // tile):
            place = (s - 1) * rows + t * tile
            start = pl.multiple_of(device * rows + t * tile, tile)
            attended = dot(weights[place // tile], values[pl.ds(start, span), :])
            outs[s - 1][t * tile : (t + 1) * tile, :] = (
                attended + normed[place : place + tile, :]
            ).astype(bf16)


def renormed(old_weight, gradient, axis):
    new_weight = old_weight - gradient
    old_square = jnp.mean(old_weight * old_weight, axis=axis, keepdims=True) + epsilon
    new_square = jnp.mean(new_weight * new_weight, axis=axis, keepdims=True) + epsilon
    return new_weight * (jnp.sqrt(old_square) / jnp.sqrt(new_square))


def own_rows_and_update(
    tile,
    flags,
    down2,
    gain,
    queries,
    highs,
    lows,
    keys,
    values,
    turned,
    down,
    gate_part,
    up_part,
    down_steps,
    mixed,
    new_gu,
    new_dn,
    weights,
    own,
    steps,
    gu,
    dn,
    sems,
):
    rows, width = own.shape
    hidden = down.shape[0]
    window = weights.shape[1] - tile
    total = keys.shape[0] - window
    linked = flags[0] == 1
    length = flags[1]
    head = lax.axis_index("head")
    for t in range(rows // tile):
        start = pl.multiple_of(head * rows + t * tile, tile)
        place = total - rows + t * tile
        span = slice(place, place + tile)
        normed = fast_rows(highs[span, :], lows[span, :], start, length, down2, gain)
        store_weights(
            queries[span, :], keys[pl.ds(start, tile + window), :], start, length, linked, weights
        )
        attended = dot(weights[...], values[pl.ds(start, tile + window), :])
        own[t * tile : (t + 1) * tile, :] = (attended + normed).astype(bf16)
    out_copy = pltpu.make_async_copy(own, mixed.at[0, :, head_columns(head, width)], sems.at[0])
    out_copy.start()
    step = min(256, total)
    for start in range(0, total, step):
        block_v = values[window + start : window + start + step, :]
        hidden_grad = dot_nt(down2[...], wide(block_v))
        part = slice(start, start + step)
        steps[0:hidden, part] = (hidden_grad * gate_part[:, part]).astype(bf16)
        steps[hidden : 2 * hidden, part] = (hidden_grad * up_part[:, part]).astype(bf16)
    both = dot(steps[...], keys[window:, :])
    for index in range(2):
        part = slice(index * hidden, (index + 1) * hidden)
        gu[index] = renormed(turned[part], both[part], 1).T
    first = pltpu.make_async_copy(gu, new_gu.at[0, 0], sems.at[1])
    first.start()
    dn[...] = renormed(down[...], dot(down_steps[...], values[window:, :]), 0)
    second = pltpu.make_async_copy(dn, new_dn.at[0, 0], sems.at[2])
    second.start()
    out_copy.wait()
    first.wait()
    second.wait()


def place_received(count, *refs):
    got = refs[1:count]
    mixed, sems = refs[count:]
    width = got[0].shape[1]
    head = lax.axis_index("head")
    run_copies(
        [
            (got[s - 1], mixed.at[0, :, head_columns(lax.rem(head + count - s, count), width)])
            for s in range(1, count)
        ],
        sems,
    )


def params():
    return pltpu.CompilerParams(vmem_limit_bytes=24 * 1024 * 1024)


def call(body, name, outs, ins, scratch=(), cost=1, aliases={}):
    spec = {local: in_vmem, in_main: in_hbm, scalars: in_smem}
    return pl.pallas_call(
        body,
        out_shape=[shape for _, shape in outs],
        in_specs=[spec[where] for where, _ in ins],
        out_specs=[spec[where] for where, _ in outs],
        scratch_shapes=list(scratch),
        input_output_aliases=aliases,
        compiler_params=params(),
        cost_estimate=pl.CostEstimate(
            flops=int(cost * 1e6), bytes_accessed=1024, transcendentals=0
        ),
        name=name,
    )(*[where(array) for where, array in ins])


def on_device(
    queries,
    keys,
    values,
    rates,
    tail_keys,
    tail_values,
    state_in_gu,
    state_in_down,
    fresh_gu,
    fresh_down,
    out_gain,
    seq_ids,
    live_lengths,
):
    count = lax.axis_size("head")
    rows = queries.shape[1]
    width = queries.shape[2] // count
    window = tail_keys.shape[0]
    hidden = state_in_down.shape[2]
    total = rows * count
    sent = total - rows
    tile = min(256, rows)
    span = tile + window
    shifts = range(1, count)
    dma = pltpu.SemaphoreType.DMA

    def on_chip(shape, kind):
        return (local, VMEM(shape, kind))

    def in_hbm_out(shape, kind):
        return (in_main, jax.ShapeDtypeStruct(shape, kind))

    def all_local(*arrays):
        return [(local, array) for array in arrays]

    piece = on_chip((rows, width), bf16)

    def columns(array, shift):
        start = lax.rem(lax.axis_index("head") + shift, count) * width
        return lax.dynamic_slice_in_dim(array[0], start, width, 1)

    sent_q = [columns(queries, s) for s in shifts]
    got_q = [from_behind(sent_q[s - 1], "head", s) for s in shifts]
    own_q = columns(lax.optimization_barrier((queries, *sent_q))[0], 0)
    got_gu = from_behind(state_in_gu[0, 0].reshape(2 * width, hidden), "ctx", 1)
    down_keys, last_v, *packed = call(
        functools.partial(pack, count),
        "pack",
        [on_chip((2 * hidden + window, width), bf16), on_chip((window, width), bf16)]
        + [piece] * (2 * count - 2),
        [(in_main, array) for array in (keys, values, state_in_down, tail_keys, tail_values)],
        scratch=[VMEM((hidden, width), f32), dma((2 * count + 1,))],
    )
    sent_k, sent_v = packed[: count - 1], packed[count - 1 :]
    got_k = [from_behind(sent_k[s - 1], "head", s) for s in shifts]
    got_dk = from_behind(down_keys, "ctx", 1)
    prior_v = from_behind(last_v, "ctx", 1)
    got_v = [from_behind(sent_v[s - 1], "head", s) for s in shifts]

    own_k, own_v, fresh, gain, rate_row, flags = call(
        functools.partial(load, count),
        "load",
        [
            piece,
            piece,
            on_chip((3 * width, hidden), f32),
            on_chip((1, width), f32),
            on_chip((1, total), f32),
            (scalars, pltpu.SMEM((2,), jnp.int32)),
        ],
        [
            (in_main, array)
            for array in (
                keys,
                values,
                fresh_gu,
                fresh_down,
                out_gain[None],
                rates,
                seq_ids.T,
                live_lengths.T,
            )
        ]
        + all_local(got_q[0]),
        scratch=[
            pltpu.SMEM(seq_ids.shape[::-1], jnp.int32),
            pltpu.SMEM(live_lengths.shape[::-1], jnp.int32),
            dma((8 + hidden // width,)),
        ],
    )
    (all_q,) = call(
        join_queries,
        "join_queries",
        [on_chip((total, width), bf16)],
        all_local(*got_q[::-1], own_q),
        cost=90,
    )
    gate2, up2, turned2, turned, live_rates = call(
        choose_gate_up,
        "choose_gate_up",
        [
            on_chip((2 * width, hidden), bf16),
            on_chip((2 * width, hidden), bf16),
            on_chip((2 * hidden, 2 * width), bf16),
            on_chip((2 * hidden, width), f32),
            on_chip((1, total), f32),
        ],
        [(scalars, flags)] + all_local(all_q, got_gu, fresh, rate_row),
        cost=90,
    )
    highs, lows = call(
        query_hidden,
        "query_hidden",
        [on_chip((total, hidden), bf16)] * 2,
        all_local(all_q, gate2, up2),
    )
    all_keys_shape = on_chip((window + total, width), bf16)
    all_keys, gate_part, up_part, down_steps = call(
        functools.partial(key_hidden, count, window),
        "key_hidden",
        [
            all_keys_shape,
            on_chip((hidden, total), f32),
            on_chip((hidden, total), f32),
            on_chip((hidden, total), bf16),
        ],
        all_local(highs, turned2, live_rates, own_k, *got_k),
        cost=1300,
    )
    down2, down, all_keys = call(
        choose_down,
        "choose_down",
        [on_chip((hidden, 2 * width), bf16), on_chip((hidden, width), f32), all_keys_shape],
        [(scalars, flags)] + all_local(got_dk, fresh, all_keys),
        aliases={3: 2},
    )
    weights, normed = call(
        functools.partial(sent_rows, count, tile),
        "sent_rows",
        [on_chip((sent // tile, tile, span), bf16), on_chip((sent, width), f32)],
        [(scalars, flags)] + all_local(down2, gain, all_keys, all_q, highs, lows),
        cost=50,
    )
    (all_values,) = call(
        start_values,
        "start_values",
        [on_chip((window + total, width), bf16)],
        all_local(normed, prior_v, own_v),
        cost=50,
    )
    all_values, *mixed_out = call(
        functools.partial(mix_sent, count),
        "mix_sent",
        [on_chip((window + total, width), bf16)] + [piece] * (count - 1),
        all_local(weights, normed, all_values, *got_v),
        aliases={2: 0},
    )
    mixed_in = [from_behind(mixed_out[s - 1], "head", s) for s in shifts]
    mixed, new_gu, new_down = call(
        functools.partial(own_rows_and_update, tile),
        "own_rows_and_update",
        [
            in_hbm_out(queries.shape, bf16),
            in_hbm_out(state_in_gu.shape, f32),
            in_hbm_out(state_in_down.shape, f32),
        ],
        [(scalars, flags)]
        + all_local(
            down2,
            gain,
            all_q,
            highs,
            lows,
            all_keys,
            all_values,
            turned,
            down,
            gate_part,
            up_part,
            down_steps,
        ),
        scratch=[
            VMEM((tile, span), bf16),
            VMEM((rows, width), bf16),
            VMEM((2 * hidden, total), bf16),
            VMEM(state_in_gu.shape[2:], f32),
            VMEM(state_in_down.shape[2:], f32),
            dma((3,)),
        ],
    )
    (mixed,) = call(
        functools.partial(place_received, count),
        "place_received",
        [in_hbm_out(queries.shape, bf16)],
        [(in_main, mixed)] + all_local(*mixed_in),
        scratch=[dma((count - 1,))],
        aliases={0: 0},
    )
    return (mixed, new_gu, new_down)


def solution(mesh):
    placed = (
        P(None, ("ctx", "head"), None),
        P(None, ("ctx", "head"), None),
        P(None, ("ctx", "head"), None),
        P(None, "head", "ctx"),
        P("ctx", "head"),
        P("ctx", "head"),
        P("ctx", "head", None, None, None),
        P("ctx", "head", None, None),
        P("head", None, None, None),
        P("head", None, None),
        P("head"),
        P(),
        P(),
    )
    return jax.shard_map(
        on_device,
        mesh=mesh,
        in_specs=placed,
        out_specs=(
            P(None, ("ctx", "head"), None),
            P("ctx", "head", None, None, None),
            P("ctx", "head", None, None),
        ),
        check_vma=False,
    )
```

time: 65.1 us -> 22.4 us (0.34)
  matrix products: 14.1 us -> 0 us
  starting transfers between devices: 18.6 us -> 8.43 us
  Pallas kernels: 0 us -> 9.07 us
  waiting for transfers between devices: 12.1 us -> 3.44 us
  local copies, waits for them, and re-layouts: 9.09 us -> 0.46 us
  other arithmetic: 8.43 us -> 0 us
  between operations: 2.26 us -> 0.75 us
    dot_general x13 -> x0, matrix products: 14.1 us -> none  [the longest x9 11.2 us: highest(): return jnp.dot(left, right, precision=lax.Precision.HIGHEST)]
    all_to_all x4 -> x0, starting transfers between devices: 13.8 us -> none  [the longest x1 3.44 us: on_device(): lax.all_to_all(keys[0], 'head', split_axis=1, concat_axis=0, tiled=True)]
    all_to_all x4 -> x0, waiting for transfers between devices: 12.1 us -> none  [the longest x1 4.88 us: on_device(): lax.all_to_all(queries[0], 'head', split_axis=1, concat_axis=0, tiled=True)]
    pallas_call x0 -> x12, Pallas kernels: none -> 9.07 us  [call(): pl.pallas_call(body, out_shape=[shape for _, shape in outs], in_specs=[sp...]
    unnamed x16 -> x2, local copies, waits for them, and re-layouts: 4.76 us -> 0.44 us
    ppermute x4 -> x7, starting transfers between devices: 4.82 us -> 8.43 us  [from_behind(): lax.ppermute(shard, axis, [(i, (i + by) % size) for i in range(size)])]
    ppermute x4 -> x7, waiting for transfers between devices: 0.01 us -> 3.44 us  [from_behind(): lax.ppermute(shard, axis, [(i, (i + by) % size) for i in range(size)])]
    convert_element_type x2 -> x0, other arithmetic: 1.73 us -> none  [the longest x1 1.09 us: fast_block(): ((attended + rms_rows(fast_out) * head_gain) * live_rows).astype(jnp.bflo...]
  transfers between devices with their start and end apart: 8 -> 7, of which waited for: 3 -> 4; matrix products, arithmetic and copies ran while one was open for 28% -> 0% of each run, Pallas kernels for 0% -> 36%
where the time goes in v2:
time: 22.4 us; the launch traced here: 22.2 us
  Pallas kernels  9.07 us (40%)
  starting transfers between devices  8.43 us (38%)
  waiting for transfers between devices  3.44 us (15%)
  between operations  0.75 us (3%)
  local copies, waits for them, and re-layouts  0.46 us (2%)
    pallas_call x12, Pallas kernels, call(): pl.pallas_call(body, out_shape=[shape for _, shape in outs], in_specs=[sp...  9.07 us
    ppermute x7, starting transfers between devices, from_behind(): lax.ppermute(shard, axis, [(i, (i + by) % size) for i in range(size)])  8.43 us
    ppermute x7, waiting for transfers between devices, from_behind(): lax.ppermute(shard, axis, [(i, (i + by) % size) for i in range(size)])  3.44 us
  transfers between devices with their start and end apart: 7, of which 4 were waited for; matrix products, arithmetic and copies ran while one was open for 0% of the time, Pallas kernels for 36%

profile of v2, /device:TPU:0, one launch (start us, length us, event | category | flops | bytes accessed | tf_op | source)
XLA Modules:
  0.0 22.2 jit_solution(5900580752447396299)
XLA Ops:
  0.6 0.0 copy-start
  0.6 0.5 %collective-permute-start.2 = (f32[256,256]{1,0:T(8,128)}, f32[256,256]{1,0:T(8,128)S(1)}, u32[]{:S(2)}, u32[]{:S(2)}) collective-permute-start(f32[256,256]{1,0:T(8,128)} %bitcast.11), channel_id=1, source_target_pairs={{0,2},{2,4},{4,6},{6,8},{8,10},{10,12},{12,14},{14,16},{16,18},{18... | collective-permute-start | bytes 786440 | tf_op jit(solution)/shard_map/ppermute | solution.py:24
  1.1 0.4 %copy-done = bf16[1,512,256]{2,1,0:T(8,128)(2,1)S(1)} copy-done((bf16[1,512,256]{2,1,0:T(8,128)(2,1)S(1)}, bf16[1,512,256]{2,1,0:T(8,128)(2,1)}, u32[]{:S(2)}) %copy-start) | copy-done | bytes 262168
  1.6 3.0 %collective-permute-start = (bf16[512,128]{1,0:T(8,128)(2,1)S(1)}, bf16[512,128]{1,0:T(8,128)(2,1)S(1)}, u32[]{:S(2)}, u32[]{:S(2)}) collective-permute-start(bf16[512,128]{1,0:T(8,128)(2,1)S(1)} %dynamic-slice_bitcast_fusion.1), channel_id=1, source_target_pairs={{0,1},{1,0},{2,3},{3,2},{4,5},{5,4},{6,7},{7,6},{8,9},{9,8},{10,11... | collective-permute-start | bytes 393224 | tf_op jit(solution)/shard_map/ppermute | solution.py:24
  4.6 1.2 %pack.1 = (bf16[1024,128]{1,0:T(8,128)(2,1)S(1)}, bf16[512,128]{1,0:T(8,128)(2,1)S(1)}, bf16[512,128]{1,0:T(8,128)(2,1)S(1)}, bf16[512,128]{1,0:T(8,128)(2,1)S(1)}) custom-call(bf16[1,512,256]{2,1,0:T(8,128)(2,1)} %k_ref.3, bf16[1,512,256]{2,1,0:T(8,128)(2,1)} %v_ref.3, f32[1,1,256,128]{3,2,1,0:T(8,128)} %dn_ref.1, bf16[512,128]{1,0:T(8,128)(2,1)} %tail_k.1, ...), custom_call_target="tpu_custom_call" | custom-call | flops 1000000 | bytes 1024 | tf_op jit(solution)/shard_map/pack/pallas_call | solution.py:390
  5.8 0.5 %collective-permute-start.1 = (bf16[1024,128]{1,0:T(8,128)(2,1)S(1)}, bf16[1024,128]{1,0:T(8,128)(2,1)S(1)}, u32[]{:S(2)}, u32[]{:S(2)}) collective-permute-start(bf16[1024,128]{1,0:T(8,128)(2,1)S(1)} %get-tuple-element.36), channel_id=1, source_target_pairs={{0,2},{2,4},{4,6},{6,8},{8,10},{10,12},{12,14},{14,16},{16,18},{18... | collective-permute-start | bytes 786440 | tf_op jit(solution)/shard_map/ppermute | solution.py:24
  6.4 0.5 %collective-permute-start.3 = (bf16[512,128]{1,0:T(8,128)(2,1)S(1)}, bf16[512,128]{1,0:T(8,128)(2,1)S(1)}, u32[]{:S(2)}, u32[]{:S(2)}) collective-permute-start(bf16[512,128]{1,0:T(8,128)(2,1)S(1)} %get-tuple-element.46), channel_id=1, source_target_pairs={{0,1},{1,0},{2,3},{3,2},{4,5},{5,4},{6,7},{7,6},{8,9},{9,8},{10,11... | collective-permute-start | bytes 393224 | tf_op jit(solution)/shard_map/ppermute | solution.py:24
  6.9 0.9 %collective-permute-start.4 = (bf16[512,128]{1,0:T(8,128)(2,1)S(1)}, bf16[512,128]{1,0:T(8,128)(2,1)S(1)}, u32[]{:S(2)}, u32[]{:S(2)}) collective-permute-start(bf16[512,128]{1,0:T(8,128)(2,1)S(1)} %get-tuple-element.54), channel_id=1, source_target_pairs={{0,2},{2,4},{4,6},{6,8},{8,10},{10,12},{12,14},{14,16},{16,18},{18... | collective-permute-start | bytes 393224 | tf_op jit(solution)/shard_map/ppermute | solution.py:24
  7.8 0.9 %collective-permute-done._.refs_0_ = bf16[512,128]{1,0:T(8,128)(2,1)S(1)} collective-permute-done((bf16[512,128]{1,0:T(8,128)(2,1)S(1)}, bf16[512,128]{1,0:T(8,128)(2,1)S(1)}, u32[]{:S(2)}, u32[]{:S(2)}) %collective-permute-start) | collective-permute-done | bytes 131104 | tf_op jit(solution)/shard_map/ppermute | solution.py:24
  8.6 2.1 %collective-permute-start.5 = (bf16[512,128]{1,0:T(8,128)(2,1)S(1)}, bf16[512,128]{1,0:T(8,128)(2,1)S(1)}, u32[]{:S(2)}, u32[]{:S(2)}) collective-permute-start(bf16[512,128]{1,0:T(8,128)(2,1)S(1)} %get-tuple-element.56), channel_id=1, source_target_pairs={{0,1},{1,0},{2,3},{3,2},{4,5},{5,4},{6,7},{7,6},{8,9},{9,8},{10,11... | collective-permute-start | bytes 393224 | tf_op jit(solution)/shard_map/ppermute | solution.py:24
  10.8 1.2 %load.1 = (bf16[512,128]{1,0:T(8,128)(2,1)S(1)}, bf16[512,128]{1,0:T(8,128)(2,1)S(1)}, f32[384,256]{1,0:T(8,128)S(1)}, f32[1,128]{1,0:T(1,128)S(1)}, f32[1,1024]{1,0:T(1,128)S(1)}, /*index=5*/s32[2]{0:T(128)S(4)}) custom-call(bf16[1,512,256]{2,1,0:T(8,128)(2,1)} %k_ref.3, bf16[1,512,256]{2,1,0:T(8,128)(2,1)} %v_ref.3, f32[1,2,128,256]{3,2,1,0:T(8,128)} %fresh_gu.1, ...), custom_call_target="tpu_custom_call" | custom-call | flops 1000000 | bytes 1024 | tf_op jit(solution)/shard_map/load/pallas_call | solution.py:390
  12.1 0.0 collective-permute-done.2.got_gu
  12.1 0.1 choose_gate_up.1
  12.2 0.7 %query_hidden.1 = (bf16[1024,256]{1,0:T(8,128)(2,1)S(1)}, bf16[1024,256]{1,0:T(8,128)(2,1)S(1)}) custom-call(bf16[1024,128]{1,0:T(8,128)(2,1)S(1)} %join_queries.1._.queries, bf16[256,256]{1,0:T(8,128)(2,1)S(1)} %get-tuple-element.40.gate2, bf16[256,256]{1,0:T(8,128)(2,1)S(1)} %get-tuple-element.41.up2), custom_call_target="tpu_custom_call" | custom-call | flops 1000000 | bytes 1024 | tf_op jit(solution)/shard_map/query_hidden/pallas_call | solution.py:390
  12.9 0.0 collective-permute-done.3.refs_0_
  12.9 0.9 %key_hidden.1 = (bf16[1536,128]{1,0:T(8,128)(2,1)S(1)}, f32[256,1024]{1,0:T(8,128)S(1)}, f32[256,1024]{1,0:T(8,128)S(1)}, bf16[256,1024]{1,0:T(8,128)(2,1)S(1)}) custom-call(bf16[1024,256]{1,0:T(8,128)(2,1)S(1)} %get-tuple-element.42._.highs, bf16[512,256]{1,0:T(8,128)(2,1)S(1)} %get-tuple-element.43.turned2, f32[1,1024]{1,0:T(1,128)S(1)} %get-tuple-element.44.rate_row, ...), custom_call_target="tpu_custom_call" | custom-call | flops 1300000000 | bytes 1024 | tf_op jit(solution)/shard_map/key_hidden/pallas_call | solution.py:390
  13.9 0.5 %collective-permute-done.1.down_keys = bf16[1024,128]{1,0:T(8,128)(2,1)S(1)} collective-permute-done((bf16[1024,128]{1,0:T(8,128)(2,1)S(1)}, bf16[1024,128]{1,0:T(8,128)(2,1)S(1)}, u32[]{:S(2)}, u32[]{:S(2)}) %collective-permute-start.1) | collective-permute-done | bytes 262176 | tf_op jit(solution)/shard_map/ppermute | solution.py:24
  14.4 0.9 %sent_rows.1 = (bf16[2,256,768]{2,1,0:T(8,128)(2,1)S(1)}, f32[512,128]{1,0:T(8,128)S(1)}) custom-call(s32[2]{0:T(128)S(4)} %get-tuple-element.35.flags, bf16[256,256]{1,0:T(8,128)(2,1)S(1)} %get-tuple-element.48.down2, f32[1,128]{1,0:T(1,128)S(1)} %get-tuple-element.49.gain, bf16[1536,128]{1,0:T(8,128)(2,1)S(1)} %get-tuple-element.51.keys, ...), custom_call_target="tpu_custom_call" | custom-call | flops 50000000 | bytes 1024 | tf_op jit(solution)/shard_map/sent_rows/pallas_call | solution.py:390
  15.3 0.5 %collective-permute-done.4.tail_v = bf16[512,128]{1,0:T(8,128)(2,1)S(1)} collective-permute-done((bf16[512,128]{1,0:T(8,128)(2,1)S(1)}, bf16[512,128]{1,0:T(8,128)(2,1)S(1)}, u32[]{:S(2)}, u32[]{:S(2)}) %collective-permute-start.4) | collective-permute-done | bytes 131104 | tf_op jit(solution)/shard_map/ppermute | solution.py:24
  15.8 0.0 collective-permute-done.5.refs_0_
  15.8 0.4 %mix_sent.1 = (bf16[1536,128]{1,0:T(8,128)(2,1)S(1)}, bf16[512,128]{1,0:T(8,128)(2,1)S(1)}) custom-call(bf16[2,256,768]{2,1,0:T(8,128)(2,1)S(1)} %get-tuple-element.52.weights, f32[512,128]{1,0:T(8,128)S(1)} %get-tuple-element.53._.normed, bf16[1536,128]{1,0:T(8,128)(2,1)S(1)} %start_values.1._, ...), custom_call_target="tpu_custom_call", output_to_operand_aliasing={{0}: (2, {})} | custom-call | flops 1000000 | bytes 1024 | tf_op jit(solution)/shard_map/mix_sent/pallas_call | solution.py:390
  16.2 0.8 %collective-permute-start.6 = (bf16[512,128]{1,0:T(8,128)(2,1)S(1)}, bf16[512,128]{1,0:T(8,128)(2,1)S(1)}, u32[]{:S(2)}, u32[]{:S(2)}) collective-permute-start(bf16[512,128]{1,0:T(8,128)(2,1)S(1)} %get-tuple-element.64), channel_id=1, source_target_pairs={{0,1},{1,0},{2,3},{3,2},{4,5},{5,4},{6,7},{7,6},{8,9},{9,8},{10,11... | collective-permute-start | bytes 393224 | tf_op jit(solution)/shard_map/ppermute | solution.py:24
  17.0 2.9 %own_rows_and_update.1 = (bf16[1,512,256]{2,1,0:T(8,128)(2,1)}, f32[1,1,2,128,256]{4,3,2,1,0:T(8,128)}, f32[1,1,256,128]{3,2,1,0:T(8,128)}) custom-call(s32[2]{0:T(128)S(4)} %get-tuple-element.35.flags, bf16[256,256]{1,0:T(8,128)(2,1)S(1)} %get-tuple-element.48.down2, f32[1,128]{1,0:T(1,128)S(1)} %get-tuple-element.49.gain, ...), custom_call_target="tpu_custom_call" | custom-call | flops 1000000 | bytes 1024 | tf_op jit(solution)/shard_map/own_rows_and_update/pallas_call | solution.py:390
  19.9 1.6 %collective-permute-done.6.refs_1_ = bf16[512,128]{1,0:T(8,128)(2,1)S(1)} collective-permute-done((bf16[512,128]{1,0:T(8,128)(2,1)S(1)}, bf16[512,128]{1,0:T(8,128)(2,1)S(1)}, u32[]{:S(2)}, u32[]{:S(2)}) %collective-permute-start.6) | collective-permute-done | bytes 131104 | tf_op jit(solution)/shard_map/ppermute | solution.py:24
  21.5 0.7 %place_received.1 = bf16[1,512,256]{2,1,0:T(8,128)(2,1)} custom-call(bf16[1,512,256]{2,1,0:T(8,128)(2,1)} %get-tuple-element.63.refs_0_, bf16[512,128]{1,0:T(8,128)(2,1)S(1)} %collective-permute-done.6.refs_1_), custom_call_target="tpu_custom_call", output_to_operand_aliasing={{}: (0, {})} | custom-call | flops 1000000 | bytes 1024 | tf_op jit(solution)/shard_map/place_received/pallas_call | solution.py:390
  (5 shorter events, 0.1 us)
Async XLA Ops:
  0.6 1.0 %copy-start = (bf16[1,512,256]{2,1,0:T(8,128)(2,1)S(1)}, bf16[1,512,256]{2,1,0:T(8,128)(2,1)}, u32[]{:S(2)}) copy-start(bf16[1,512,256]{2,1,0:T(8,128)(2,1)} %param.13) | copy-start | bytes 786436
  0.6 11.4 %collective-permute-start.2 = (f32[256,256]{1,0:T(8,128)}, f32[256,256]{1,0:T(8,128)S(1)}, u32[]{:S(2)}, u32[]{:S(2)}) collective-permute-start(f32[256,256]{1,0:T(8,128)} %bitcast.11), channel_id=1, source_target_pairs={{0,2},{2,4},{4,6},{6,8},{8,10},{10,12},{12,14},{14,16},{16,18},{18... | collective-permute-start | bytes 786440 | tf_op jit(solution)/shard_map/ppermute | solution.py:24
  1.6 7.0 %collective-permute-start = (bf16[512,128]{1,0:T(8,128)(2,1)S(1)}, bf16[512,128]{1,0:T(8,128)(2,1)S(1)}, u32[]{:S(2)}, u32[]{:S(2)}) collective-permute-start(bf16[512,128]{1,0:T(8,128)(2,1)S(1)} %dynamic-slice_bitcast_fusion.1), channel_id=1, source_target_pairs={{0,1},{1,0},{2,3},{3,2},{4,5},{5,4},{6,7},{7,6},{8,9},{9,8},{10,11... | collective-permute-start | bytes 393224 | tf_op jit(solution)/shard_map/ppermute | solution.py:24
  5.8 8.5 %collective-permute-start.1 = (bf16[1024,128]{1,0:T(8,128)(2,1)S(1)}, bf16[1024,128]{1,0:T(8,128)(2,1)S(1)}, u32[]{:S(2)}, u32[]{:S(2)}) collective-permute-start(bf16[1024,128]{1,0:T(8,128)(2,1)S(1)} %get-tuple-element.36), channel_id=1, source_target_pairs={{0,2},{2,4},{4,6},{6,8},{8,10},{10,12},{12,14},{14,16},{16,18},{18... | collective-permute-start | bytes 786440 | tf_op jit(solution)/shard_map/ppermute | solution.py:24
  6.4 6.5 %collective-permute-start.3 = (bf16[512,128]{1,0:T(8,128)(2,1)S(1)}, bf16[512,128]{1,0:T(8,128)(2,1)S(1)}, u32[]{:S(2)}, u32[]{:S(2)}) collective-permute-start(bf16[512,128]{1,0:T(8,128)(2,1)S(1)} %get-tuple-element.46), channel_id=1, source_target_pairs={{0,1},{1,0},{2,3},{3,2},{4,5},{5,4},{6,7},{7,6},{8,9},{9,8},{10,11... | collective-permute-start | bytes 393224 | tf_op jit(solution)/shard_map/ppermute | solution.py:24
  6.9 8.9 %collective-permute-start.4 = (bf16[512,128]{1,0:T(8,128)(2,1)S(1)}, bf16[512,128]{1,0:T(8,128)(2,1)S(1)}, u32[]{:S(2)}, u32[]{:S(2)}) collective-permute-start(bf16[512,128]{1,0:T(8,128)(2,1)S(1)} %get-tuple-element.54), channel_id=1, source_target_pairs={{0,2},{2,4},{4,6},{6,8},{8,10},{10,12},{12,14},{14,16},{16,18},{18... | collective-permute-start | bytes 393224 | tf_op jit(solution)/shard_map/ppermute | solution.py:24
  8.6 7.2 %collective-permute-start.5 = (bf16[512,128]{1,0:T(8,128)(2,1)S(1)}, bf16[512,128]{1,0:T(8,128)(2,1)S(1)}, u32[]{:S(2)}, u32[]{:S(2)}) collective-permute-start(bf16[512,128]{1,0:T(8,128)(2,1)S(1)} %get-tuple-element.56), channel_id=1, source_target_pairs={{0,1},{1,0},{2,3},{3,2},{4,5},{5,4},{6,7},{7,6},{8,9},{9,8},{10,11... | collective-permute-start | bytes 393224 | tf_op jit(solution)/shard_map/ppermute | solution.py:24
  16.2 5.3 %collective-permute-start.6 = (bf16[512,128]{1,0:T(8,128)(2,1)S(1)}, bf16[512,128]{1,0:T(8,128)(2,1)S(1)}, u32[]{:S(2)}, u32[]{:S(2)}) collective-permute-start(bf16[512,128]{1,0:T(8,128)(2,1)S(1)} %get-tuple-element.64), channel_id=1, source_target_pairs={{0,1},{1,0},{2,3},{3,2},{4,5},{5,4},{6,7},{7,6},{8,9},{9,8},{10,11... | collective-permute-start | bytes 393224 | tf_op jit(solution)/shard_map/ppermute | solution.py:24

commit v3 on v2

--- a/solution.py
+++ b/solution.py
@@ -123,16 +123,18 @@
         joined[pl.ds(pl.multiple_of(window + source * rows, rows), rows), :] = got[s - 1][...]
 
 
-def pack(count, k_ref, v_ref, dn_ref, tail_k, tail_v, *refs):
+def pack(count, q_ref, k_ref, v_ref, dn_ref, tail_k, tail_v, *refs):
     down_keys, last_v = refs[:2]
-    sent_k, sent_v = refs[2 : 1 + count], refs[1 + count : 2 * count]
+    sent_qk, sent_v = refs[2 : 1 + count], refs[1 + count : 2 * count]
     down, sems = refs[-2:]
     head = lax.axis_index("head")
     hidden, width = down.shape
+    rows = sent_v[0].shape[0]
     pairs = [(dn_ref.at[0, 0], down)]
     for s in range(1, count):
         columns = head_columns(lax.rem(head + s, count), width)
-        pairs.append((k_ref.at[0, :, columns], sent_k[s - 1]))
+        pairs.append((q_ref.at[0, :, columns], sent_qk[s - 1].at[0:rows]))
+        pairs.append((k_ref.at[0, :, columns], sent_qk[s - 1].at[rows : 2 * rows]))
         pairs.append((v_ref.at[0, :, columns], sent_v[s - 1]))
     pairs += [(tail_k, down_keys.at[2 * hidden :]), (tail_v, last_v)]
     run_copies(pairs, sems)
@@ -142,7 +144,8 @@
 
 
 def load(
-    count, k_ref, v_ref, fresh_gu, fresh_dn, gain, rates, ids_ref, len_ref, _, own_k, own_v, fresh,
+    count, q_ref, k_ref, v_ref, fresh_gu, fresh_dn, gain, rates, ids_ref, len_ref, _, own_q, own_k,
+    own_v, fresh,
     gain_row, rate_row, flags, ids, lens, sems
 ):
     head = lax.axis_index("head")
@@ -150,6 +153,7 @@
     width = own_k.shape[1]
     columns = head_columns(head, width)
     pairs = [
+        (q_ref.at[0, :, columns], own_q),
         (k_ref.at[0, :, columns], own_k),
         (v_ref.at[0, :, columns], own_v),
         (fresh_gu.at[0, 0], fresh.at[0:width]),
@@ -166,29 +170,31 @@
     flags[1] = lens[0, here]
 
 
-def join_queries(*refs):
-    joined = refs[-1]
-    rows = refs[0].shape[0]
-    for index, part in enumerate(refs[:-1]):
-        joined[index * rows : (index + 1) * rows, :] = part[...]
-
-
-def query_hidden(queries, gate2, up2, highs, lows):
-    total, width = queries.shape
-    step = min(256, total)
-    for start in range(0, total, step):
-        block = queries[start : start + step, :]
-        block32 = block.astype(f32)
-        unit = lax.rsqrt(jnp.mean(block32 * block32, axis=-1, keepdims=True) + epsilon)
-        doubled = wide(block)
-        gate = dot(doubled, gate2[...]) * unit
-        up = dot(doubled, up2[...]) * unit
-        high, low = halves(gate * sigmoid(gate) * up)
-        highs[start : start + step, :] = high
-        lows[start : start + step, :] = low
-
-
-def choose_gate_up(flags, _, got_gu, fresh, rates, gate2, up2, turned2, turned, rate_row):
+def hidden_rows(queries, gate2, up2):
+    queries32 = queries.astype(f32)
+    unit = lax.rsqrt(jnp.mean(queries32 * queries32, axis=-1, keepdims=True) + epsilon)
+    doubled = wide(queries)
+    gate = dot(doubled, gate2[...]) * unit
+    up = dot(doubled, up2[...]) * unit
+    return halves(gate * sigmoid(gate) * up)
+
+
+def sent_hidden(count, tile, window, gate2, up2, own_k, *refs):
+    got_qk, (queries, highs, lows, keys) = refs[: count - 1], refs[count - 1 :]
+    rows, width = own_k.shape
+    for s in range(1, count):
+        source = got_qk[count - s - 1]
+        for t in range(rows // tile):
+            span = slice((s - 1) * rows + t * tile, (s - 1) * rows + (t + 1) * tile)
+            block = source[t * tile : (t + 1) * tile, :]
+            queries[span, :] = block
+            high, low = hidden_rows(block, gate2, up2)
+            highs[span, :] = high
+            lows[span, :] = low
+    join(count, window, own_k, [got.at[rows : 2 * rows] for got in got_qk], keys)
+
+
+def choose_gate_up(flags, got_gu, fresh, rates, gate2, up2, turned2, turned, rate_row):
     hidden = fresh.shape[1]
     width = got_gu.shape[0] // 2
     linked = flags[0] == 1
@@ -205,33 +211,6 @@
     rate_row[...] = jnp.where(token < length, -rates[...], 0.0)
 
 
-def key_hidden(
-    count, window, _, turned2, rate_row, own_k, *refs
-):
-    got_k, (keys, gate_part, up_part, down_steps) = refs[: count - 1], refs[count - 1 :]
-    rows, width = own_k.shape
-    hidden = turned2.shape[0] // 2
-    total = count * rows
-    join(count, window, own_k, got_k, keys)
-    ones = jnp.ones((8, 2 * width), bf16)
-    step = min(256, total)
-    for start in range(0, total, step):
-        block = keys[window + start : window + start + step, :]
-        block32 = block.astype(f32)
-        square = jnp.concatenate(halves(block32 * block32), axis=1)
-        unit = lax.rsqrt(dot_nt(ones, square)[:1] * (1.0 / width) + epsilon)
-        rate = rate_row[:, start : start + step]
-        scale = rate * unit
-        both = dot_nt(turned2[...], wide(block))
-        gate = both[:hidden] * unit
-        up = both[hidden:] * unit
-        share = sigmoid(gate)
-        act = gate * share
-        gate_part[:, start : start + step] = up * (share + act * (1.0 - share)) * scale
-        up_part[:, start : start + step] = act * scale
-        down_steps[:, start : start + step] = (act * up * rate).astype(bf16)
-
-
 def choose_down(flags, down_keys, fresh, keys, down2, down, joined):
     hidden, width = down.shape
     window = down_keys.shape[0] - 2 * hidden
@@ -247,7 +226,7 @@
 
 
 def sent_rows(count, tile, flags, down2, gain, keys, queries, highs, lows, weights, normed):
-    rows = queries.shape[0] // count
+    rows = queries.shape[0] // (count - 1)
     window = keys.shape[0] - count * rows
     linked = flags[0] == 1
     length = flags[1]
@@ -305,18 +284,17 @@
 def own_rows_and_update(
     tile,
     flags,
+    gate2,
+    up2,
     down2,
     gain,
-    queries,
-    highs,
-    lows,
+    own_q,
     keys,
     values,
+    turned2,
     turned,
     down,
-    gate_part,
-    up_part,
-    down_steps,
+    rate_row,
     mixed,
     new_gu,
     new_dn,
@@ -327,39 +305,51 @@
     dn,
     sems,
 ):
-    rows, width = own.shape
+    rows, width = own_q.shape
     hidden = down.shape[0]
-    window = weights.shape[1] - tile
+    window = weights.shape[2] - tile
     total = keys.shape[0] - window
     linked = flags[0] == 1
     length = flags[1]
     head = lax.axis_index("head")
     for t in range(rows // tile):
         start = pl.multiple_of(head * rows + t * tile, tile)
-        place = total - rows + t * tile
-        span = slice(place, place + tile)
-        normed = fast_rows(highs[span, :], lows[span, :], start, length, down2, gain)
+        block = own_q[t * tile : (t + 1) * tile, :]
+        high, low = hidden_rows(block, gate2, up2)
+        normed = fast_rows(high, low, start, length, down2, gain)
         store_weights(
-            queries[span, :], keys[pl.ds(start, tile + window), :], start, length, linked, weights
+            block, keys[pl.ds(start, tile + window), :], start, length, linked, weights.at[t]
         )
-        attended = dot(weights[...], values[pl.ds(start, tile + window), :])
+        attended = dot(weights[t], values[pl.ds(start, tile + window), :])
         own[t * tile : (t + 1) * tile, :] = (attended + normed).astype(bf16)
     out_copy = pltpu.make_async_copy(own, mixed.at[0, :, head_columns(head, width)], sems.at[0])
     out_copy.start()
+    ones = jnp.ones((8, 2 * width), bf16)
     step = min(256, total)
     for start in range(0, total, step):
+        block_k = keys[window + start : window + start + step, :]
         block_v = values[window + start : window + start + step, :]
-        hidden_grad = dot_nt(down2[...], wide(block_v))
+        block32 = block_k.astype(f32)
+        square = jnp.concatenate(halves(block32 * block32), axis=1)
+        unit = lax.rsqrt(dot_nt(ones, square)[:1] * (1.0 / width) + epsilon)
+        rate = rate_row[:, start : start + step]
+        both = dot_nt(turned2[...], wide(block_k))
+        gate = both[:hidden] * unit
+        up = both[hidden:] * unit
+        share = sigmoid(gate)
+        act = gate * share
+        hidden_grad = dot_nt(down2[...], wide(block_v)) * (rate * unit)
         part = slice(start, start + step)
-        steps[0:hidden, part] = (hidden_grad * gate_part[:, part]).astype(bf16)
-        steps[hidden : 2 * hidden, part] = (hidden_grad * up_part[:, part]).astype(bf16)
-    both = dot(steps[...], keys[window:, :])
+        steps[0:hidden, part] = (hidden_grad * up * (share + act * (1.0 - share))).astype(bf16)
+        steps[hidden : 2 * hidden, part] = (hidden_grad * act).astype(bf16)
+        steps[2 * hidden : 3 * hidden, part] = (act * up * rate).astype(bf16)
+    both = dot(steps[0 : 2 * hidden, :], keys[window:, :])
     for index in range(2):
         part = slice(index * hidden, (index + 1) * hidden)
         gu[index] = renormed(turned[part], both[part], 1).T
     first = pltpu.make_async_copy(gu, new_gu.at[0, 0], sems.at[1])
     first.start()
-    dn[...] = renormed(down[...], dot(down_steps[...], values[window:, :]), 0)
+    dn[...] = renormed(down[...], dot(steps[2 * hidden :, :], values[window:, :]), 0)
     second = pltpu.make_async_copy(dn, new_dn.at[0, 0], sems.at[2])
     second.start()
     out_copy.wait()
@@ -440,32 +430,30 @@
 
     piece = on_chip((rows, width), bf16)
 
-    def columns(array, shift):
-        start = lax.rem(lax.axis_index("head") + shift, count) * width
-        return lax.dynamic_slice_in_dim(array[0], start, width, 1)
-
-    sent_q = [columns(queries, s) for s in shifts]
-    got_q = [from_behind(sent_q[s - 1], "head", s) for s in shifts]
-    own_q = columns(lax.optimization_barrier((queries, *sent_q))[0], 0)
     got_gu = from_behind(state_in_gu[0, 0].reshape(2 * width, hidden), "ctx", 1)
     down_keys, last_v, *packed = call(
         functools.partial(pack, count),
         "pack",
         [on_chip((2 * hidden + window, width), bf16), on_chip((window, width), bf16)]
-        + [piece] * (2 * count - 2),
-        [(in_main, array) for array in (keys, values, state_in_down, tail_keys, tail_values)],
-        scratch=[VMEM((hidden, width), f32), dma((2 * count + 1,))],
-    )
-    sent_k, sent_v = packed[: count - 1], packed[count - 1 :]
-    got_k = [from_behind(sent_k[s - 1], "head", s) for s in shifts]
+        + [on_chip((2 * rows, width), bf16)] * (count - 1)
+        + [piece] * (count - 1),
+        [
+            (in_main, array)
+            for array in (queries, keys, values, state_in_down, tail_keys, tail_values)
+        ],
+        scratch=[VMEM((hidden, width), f32), dma((3 * count,))],
+    )
+    sent_qk, sent_v = packed[: count - 1], packed[count - 1 :]
+    got_qk = [from_behind(sent_qk[s - 1], "head", s) for s in shifts]
     got_dk = from_behind(down_keys, "ctx", 1)
     prior_v = from_behind(last_v, "ctx", 1)
     got_v = [from_behind(sent_v[s - 1], "head", s) for s in shifts]
 
-    own_k, own_v, fresh, gain, rate_row, flags = call(
+    own_q, own_k, own_v, fresh, gain, rate_row, flags = call(
         functools.partial(load, count),
         "load",
         [
+            piece,
             piece,
             piece,
             on_chip((3 * width, hidden), f32),
@@ -476,6 +464,7 @@
         [
             (in_main, array)
             for array in (
+                queries,
                 keys,
                 values,
                 fresh_gu,
@@ -486,19 +475,12 @@
                 live_lengths.T,
             )
         ]
-        + all_local(got_q[0]),
+        + all_local(sent_qk[0]),
         scratch=[
             pltpu.SMEM(seq_ids.shape[::-1], jnp.int32),
             pltpu.SMEM(live_lengths.shape[::-1], jnp.int32),
-            dma((8 + hidden // width,)),
-        ],
-    )
-    (all_q,) = call(
-        join_queries,
-        "join_queries",
-        [on_chip((total, width), bf16)],
-        all_local(*got_q[::-1], own_q),
-        cost=90,
+            dma((9 + hidden // width,)),
+        ],
     )
     gate2, up2, turned2, turned, live_rates = call(
         choose_gate_up,
@@ -510,27 +492,18 @@
             on_chip((2 * hidden, width), f32),
             on_chip((1, total), f32),
         ],
-        [(scalars, flags)] + all_local(all_q, got_gu, fresh, rate_row),
-        cost=90,
-    )
-    highs, lows = call(
-        query_hidden,
-        "query_hidden",
-        [on_chip((total, hidden), bf16)] * 2,
-        all_local(all_q, gate2, up2),
+        [(scalars, flags)] + all_local(got_gu, fresh, rate_row),
+        cost=500,
     )
     all_keys_shape = on_chip((window + total, width), bf16)
-    all_keys, gate_part, up_part, down_steps = call(
-        functools.partial(key_hidden, count, window),
-        "key_hidden",
-        [
-            all_keys_shape,
-            on_chip((hidden, total), f32),
-            on_chip((hidden, total), f32),
-            on_chip((hidden, total), bf16),
-        ],
-        all_local(highs, turned2, live_rates, own_k, *got_k),
-        cost=1300,
+    sent_q, highs, lows, all_keys = call(
+        functools.partial(sent_hidden, count, tile, window),
+        "sent_hidden",
+        [on_chip((sent, width), bf16)]
+        + [on_chip((sent, hidden), bf16)] * 2
+        + [all_keys_shape],
+        all_local(gate2, up2, own_k, *got_qk),
+        cost=500,
     )
     down2, down, all_keys = call(
         choose_down,
@@ -543,15 +516,15 @@
         functools.partial(sent_rows, count, tile),
         "sent_rows",
         [on_chip((sent // tile, tile, span), bf16), on_chip((sent, width), f32)],
-        [(scalars, flags)] + all_local(down2, gain, all_keys, all_q, highs, lows),
-        cost=50,
+        [(scalars, flags)] + all_local(down2, gain, all_keys, sent_q, highs, lows),
+        cost=1,
     )
     (all_values,) = call(
         start_values,
         "start_values",
         [on_chip((window + total, width), bf16)],
         all_local(normed, prior_v, own_v),
-        cost=50,
+        cost=1,
     )
     all_values, *mixed_out = call(
         functools.partial(mix_sent, count),
@@ -571,23 +544,12 @@
         ],
         [(scalars, flags)]
         + all_local(
-            down2,
-            gain,
-            all_q,
-            highs,
-            lows,
-            all_keys,
-            all_values,
-            turned,
-            down,
-            gate_part,
-            up_part,
-            down_steps,
+            gate2, up2, down2, gain, own_q, all_keys, all_values, turned2, turned, down, live_rates
         ),
         scratch=[
-            VMEM((tile, span), bf16),
+            VMEM((rows // tile, tile, span), bf16),
             VMEM((rows, width), bf16),
-            VMEM((2 * hidden, total), bf16),
+            VMEM((3 * hidden, total), bf16),
             VMEM(state_in_gu.shape[2:], f32),
             VMEM(state_in_down.shape[2:], f32),
             dma((3,)),

time: 22.4 us -> 21.8 us (0.973)
  waiting for transfers between devices: 3.44 us -> 4.92 us
  starting transfers between devices: 8.43 us -> 6.97 us
  local copies, waits for them, and re-layouts: 0.46 us -> 0 us
    ppermute x7 -> x6, waiting for transfers between devices: 3.44 us -> 4.92 us  [from_behind(): lax.ppermute(shard, axis, [(i, (i + by) % size) for i in range(size)])]
    ppermute x7 -> x6, starting transfers between devices: 8.43 us -> 6.97 us  [from_behind(): lax.ppermute(shard, axis, [(i, (i + by) % size) for i in range(size)])]
    unnamed x2 -> x0, local copies, waits for them, and re-layouts: 0.44 us -> none
    pallas_call x12 -> x10, Pallas kernels: 9.07 us -> 9 us  [call(): pl.pallas_call(body, out_shape=[shape for _, shape in outs], in_specs=[sp...]
  transfers between devices with their start and end apart: 7 -> 6, of which waited for: 4 -> 4; matrix products, arithmetic and copies ran while one was open for 0% -> 0% of each run, Pallas kernels for 36% -> 37%
where the time goes in v3:
time: 21.8 us; the launch traced here: 21.6 us
  Pallas kernels  9 us (41%)
  starting transfers between devices  6.97 us (32%)
  waiting for transfers between devices  4.92 us (23%)
  between operations  0.71 us (3%)
    pallas_call x10, Pallas kernels, call(): pl.pallas_call(body, out_shape=[shape for _, shape in outs], in_specs=[sp...  9 us
    ppermute x6, starting transfers between devices, from_behind(): lax.ppermute(shard, axis, [(i, (i + by) % size) for i in range(size)])  6.97 us
    ppermute x6, waiting for transfers between devices, from_behind(): lax.ppermute(shard, axis, [(i, (i + by) % size) for i in range(size)])  4.92 us
  transfers between devices with their start and end apart: 6, of which 4 were waited for; matrix products, arithmetic and copies ran while one was open for 0% of the time, Pallas kernels for 37%

profile of v3, /device:TPU:0, one launch (start us, length us, event | category | flops | bytes accessed | tf_op | source)
XLA Modules:
  0.0 21.6 jit_solution(8672604301134336936)
XLA Ops:
  0.6 0.5 %collective-permute-start = (f32[256,256]{1,0:T(8,128)}, f32[256,256]{1,0:T(8,128)S(1)}, u32[]{:S(2)}, u32[]{:S(2)}) collective-permute-start(f32[256,256]{1,0:T(8,128)} %bitcast.7), channel_id=1, source_target_pairs={{0,2},{2,4},{4,6},{6,8},{8,10},{10,12},{12,14},{14,16},{16,18},{18... | collective-permute-start | bytes 786440 | tf_op jit(solution)/shard_map/ppermute | solution.py:24
  1.1 1.3 %pack.1 = (bf16[1024,128]{1,0:T(8,128)(2,1)S(1)}, bf16[512,128]{1,0:T(8,128)(2,1)S(1)}, bf16[1024,128]{1,0:T(8,128)(2,1)S(1)}, bf16[512,128]{1,0:T(8,128)(2,1)S(1)}) custom-call(bf16[1,512,256]{2,1,0:T(8,128)(2,1)} %q_ref.3, bf16[1,512,256]{2,1,0:T(8,128)(2,1)} %k_ref.3, bf16[1,512,256]{2,1,0:T(8,128)(2,1)} %v_ref.3, f32[1,1,256,128]{3,2,1,0:T(8,128)} %dn_ref.1, ...), custom_call_target="tpu_custom_call" | custom-call | flops 1000000 | bytes 1024 | tf_op jit(solution)/shard_map/pack/pallas_call | solution.py:380
  2.4 2.6 %collective-permute-start.2 = (bf16[1024,128]{1,0:T(8,128)(2,1)S(1)}, bf16[1024,128]{1,0:T(8,128)(2,1)S(1)}, u32[]{:S(2)}, u32[]{:S(2)}) collective-permute-start(bf16[1024,128]{1,0:T(8,128)(2,1)S(1)} %get-tuple-element.33._), channel_id=1, source_target_pairs={{0,1},{1,0},{2,3},{3,2},{4,5},{5,4},{6,7},{7,6},{8,9},{9,8},{10,11... | collective-permute-start | bytes 786440 | tf_op jit(solution)/shard_map/ppermute | solution.py:24
  5.0 1.3 %collective-permute-start.1 = (bf16[1024,128]{1,0:T(8,128)(2,1)S(1)}, bf16[1024,128]{1,0:T(8,128)(2,1)S(1)}, u32[]{:S(2)}, u32[]{:S(2)}) collective-permute-start(bf16[1024,128]{1,0:T(8,128)(2,1)S(1)} %get-tuple-element.39), channel_id=1, source_target_pairs={{0,2},{2,4},{4,6},{6,8},{8,10},{10,12},{12,14},{14,16},{16,18},{18... | collective-permute-start | bytes 786440 | tf_op jit(solution)/shard_map/ppermute | solution.py:24
  6.3 0.3 %collective-permute-start.3 = (bf16[512,128]{1,0:T(8,128)(2,1)S(1)}, bf16[512,128]{1,0:T(8,128)(2,1)S(1)}, u32[]{:S(2)}, u32[]{:S(2)}) collective-permute-start(bf16[512,128]{1,0:T(8,128)(2,1)S(1)} %get-tuple-element.51), channel_id=1, source_target_pairs={{0,2},{2,4},{4,6},{6,8},{8,10},{10,12},{12,14},{14,16},{16,18},{18... | collective-permute-start | bytes 393224 | tf_op jit(solution)/shard_map/ppermute | solution.py:24
  6.6 0.5 %collective-permute-start.4 = (bf16[512,128]{1,0:T(8,128)(2,1)S(1)}, bf16[512,128]{1,0:T(8,128)(2,1)S(1)}, u32[]{:S(2)}, u32[]{:S(2)}) collective-permute-start(bf16[512,128]{1,0:T(8,128)(2,1)S(1)} %get-tuple-element.53), channel_id=1, source_target_pairs={{0,1},{1,0},{2,3},{3,2},{4,5},{5,4},{6,7},{7,6},{8,9},{9,8},{10,11... | collective-permute-start | bytes 393224 | tf_op jit(solution)/shard_map/ppermute | solution.py:24
  7.2 1.3 %load.1 = (bf16[512,128]{1,0:T(8,128)(2,1)S(1)}, bf16[512,128]{1,0:T(8,128)(2,1)S(1)}, bf16[512,128]{1,0:T(8,128)(2,1)S(1)}, f32[384,256]{1,0:T(8,128)S(1)}, f32...) custom-call(bf16[1,512,256]{2,1,0:T(8,128)(2,1)} %q_ref.3, bf16[1,512,256]{2,1,0:T(8,128)(2,1)} %k_ref.3, ...), custom_call_target="tpu_custom_call" | custom-call | flops 1000000 | bytes 1024 | tf_op jit(solution)/shard_map/load/pallas_call | solution.py:380
  8.5 1.9 %collective-permute-done.got_gu = f32[256,256]{1,0:T(8,128)S(1)} collective-permute-done((f32[256,256]{1,0:T(8,128)}, f32[256,256]{1,0:T(8,128)S(1)}, u32[]{:S(2)}, u32[]{:S(2)}) %collective-permute-start) | collective-permute-done | bytes 262176 | tf_op jit(solution)/shard_map/ppermute | solution.py:24
  10.4 0.1 choose_gate_up.1
  10.6 0.5 %collective-permute-done.2.refs_0_ = bf16[1024,128]{1,0:T(8,128)(2,1)S(1)} collective-permute-done((bf16[1024,128]{1,0:T(8,128)(2,1)S(1)}, bf16[1024,128]{1,0:T(8,128)(2,1)S(1)}, u32[]{:S(2)}, u32[]{:S(2)}) %collective-permute-start.2) | collective-permute-done | bytes 262176 | tf_op jit(solution)/shard_map/ppermute | solution.py:24
  11.1 0.4 %sent_hidden.1 = (bf16[512,128]{1,0:T(8,128)(2,1)S(1)}, bf16[512,256]{1,0:T(8,128)(2,1)S(1)}, bf16[512,256]{1,0:T(8,128)(2,1)S(1)}, bf16[1536,128]{1,0:T(8,128)(2,1)S(1)}) custom-call(bf16[256,256]{1,0:T(8,128)(2,1)S(1)} %get-tuple-element.37.gate2, bf16[256,256]{1,0:T(8,128)(2,1)S(1)} %get-tuple-element.38.up2, ...), custom_call_target="tpu_custom_call" | custom-call | flops 500000000 | bytes 1024 | tf_op jit(solution)/shard_map/sent_hidden/pallas_call | solution.py:380
  11.5 2.0 %collective-permute-done.1.down_keys = bf16[1024,128]{1,0:T(8,128)(2,1)S(1)} collective-permute-done((bf16[1024,128]{1,0:T(8,128)(2,1)S(1)}, bf16[1024,128]{1,0:T(8,128)(2,1)S(1)}, u32[]{:S(2)}, u32[]{:S(2)}) %collective-permute-start.1) | collective-permute-done | bytes 262176 | tf_op jit(solution)/shard_map/ppermute | solution.py:24
  13.5 0.9 %sent_rows.1 = (bf16[2,256,768]{2,1,0:T(8,128)(2,1)S(1)}, f32[512,128]{1,0:T(8,128)S(1)}) custom-call(s32[2]{0:T(128)S(4)} %get-tuple-element.34.flags, bf16[256,256]{1,0:T(8,128)(2,1)S(1)} %get-tuple-element.42.down2, f32[1,128]{1,0:T(1,128)S(1)} %get-tuple-element.43.gain, bf16[1536,128]{1,0:T(8,128)(2,1)S(1)} %get-tuple-element.45.keys, ...), custom_call_target="tpu_custom_call" | custom-call | flops 1000000 | bytes 1024 | tf_op jit(solution)/shard_map/sent_rows/pallas_call | solution.py:380
  14.4 0.5 %collective-permute-done.3.tail_v = bf16[512,128]{1,0:T(8,128)(2,1)S(1)} collective-permute-done((bf16[512,128]{1,0:T(8,128)(2,1)S(1)}, bf16[512,128]{1,0:T(8,128)(2,1)S(1)}, u32[]{:S(2)}, u32[]{:S(2)}) %collective-permute-start.3) | collective-permute-done | bytes 131104 | tf_op jit(solution)/shard_map/ppermute | solution.py:24
  14.9 0.0 collective-permute-done.4.refs_0_
  14.9 0.4 %mix_sent.1 = (bf16[1536,128]{1,0:T(8,128)(2,1)S(1)}, bf16[512,128]{1,0:T(8,128)(2,1)S(1)}) custom-call(bf16[2,256,768]{2,1,0:T(8,128)(2,1)S(1)} %get-tuple-element.49.weights, f32[512,128]{1,0:T(8,128)S(1)} %get-tuple-element.50._.normed, bf16[1536,128]{1,0:T(8,128)(2,1)S(1)} %start_values.1._, ...), custom_call_target="tpu_custom_call", output_to_operand_aliasing={{0}: (2, {})} | custom-call | flops 1000000 | bytes 1024 | tf_op jit(solution)/shard_map/mix_sent/pallas_call | solution.py:380
  15.3 1.7 %collective-permute-start.5 = (bf16[512,128]{1,0:T(8,128)(2,1)S(1)}, bf16[512,128]{1,0:T(8,128)(2,1)S(1)}, u32[]{:S(2)}, u32[]{:S(2)}) collective-permute-start(bf16[512,128]{1,0:T(8,128)(2,1)S(1)} %get-tuple-element.60), channel_id=1, source_target_pairs={{0,1},{1,0},{2,3},{3,2},{4,5},{5,4},{6,7},{7,6},{8,9},{9,8},{10,11... | collective-permute-start | bytes 393224 | tf_op jit(solution)/shard_map/ppermute | solution.py:24
  17.0 3.9 %own_rows_and_update.1 = (bf16[1,512,256]{2,1,0:T(8,128)(2,1)}, f32[1,1,2,128,256]{4,3,2,1,0:T(8,128)}, f32[1,1,256,128]{3,2,1,0:T(8,128)}) custom-call(s32[2]{0:T(128)S(4)} %get-tuple-element.34.flags, bf16[256,256]{1,0:T(8,128)(2,1)S(1)} %get-tuple-element.37.gate2, bf16[256,256]{1,0:T(8,128)(2,1)S(1)} %get-tuple-element.38.up2, ...), custom_call_target="tpu_custom_call" | custom-call | flops 1000000 | bytes 1024 | tf_op jit(solution)/shard_map/own_rows_and_update/pallas_call | solution.py:380
  20.9 0.0 collective-permute-done.5.refs_1_
  20.9 0.7 %place_received.1 = bf16[1,512,256]{2,1,0:T(8,128)(2,1)} custom-call(bf16[1,512,256]{2,1,0:T(8,128)(2,1)} %get-tuple-element.59.refs_0_, bf16[512,128]{1,0:T(8,128)(2,1)S(1)} %collective-permute-done.5.refs_1_), custom_call_target="tpu_custom_call", output_to_operand_aliasing={{}: (0, {})} | custom-call | flops 1000000 | bytes 1024 | tf_op jit(solution)/shard_map/place_received/pallas_call | solution.py:380
  (2 shorter events, 0.1 us)
Async XLA Ops:
  0.6 9.8 %collective-permute-start = (f32[256,256]{1,0:T(8,128)}, f32[256,256]{1,0:T(8,128)S(1)}, u32[]{:S(2)}, u32[]{:S(2)}) collective-permute-start(f32[256,256]{1,0:T(8,128)} %bitcast.7), channel_id=1, source_target_pairs={{0,2},{2,4},{4,6},{6,8},{8,10},{10,12},{12,14},{14,16},{16,18},{18... | collective-permute-start | bytes 786440 | tf_op jit(solution)/shard_map/ppermute | solution.py:24
  2.4 8.7 %collective-permute-start.2 = (bf16[1024,128]{1,0:T(8,128)(2,1)S(1)}, bf16[1024,128]{1,0:T(8,128)(2,1)S(1)}, u32[]{:S(2)}, u32[]{:S(2)}) collective-permute-start(bf16[1024,128]{1,0:T(8,128)(2,1)S(1)} %get-tuple-element.33._), channel_id=1, source_target_pairs={{0,1},{1,0},{2,3},{3,2},{4,5},{5,4},{6,7},{7,6},{8,9},{9,8},{10,11... | collective-permute-start | bytes 786440 | tf_op jit(solution)/shard_map/ppermute | solution.py:24
  5.0 8.5 %collective-permute-start.1 = (bf16[1024,128]{1,0:T(8,128)(2,1)S(1)}, bf16[1024,128]{1,0:T(8,128)(2,1)S(1)}, u32[]{:S(2)}, u32[]{:S(2)}) collective-permute-start(bf16[1024,128]{1,0:T(8,128)(2,1)S(1)} %get-tuple-element.39), channel_id=1, source_target_pairs={{0,2},{2,4},{4,6},{6,8},{8,10},{10,12},{12,14},{14,16},{16,18},{18... | collective-permute-start | bytes 786440 | tf_op jit(solution)/shard_map/ppermute | solution.py:24
  6.3 8.6 %collective-permute-start.3 = (bf16[512,128]{1,0:T(8,128)(2,1)S(1)}, bf16[512,128]{1,0:T(8,128)(2,1)S(1)}, u32[]{:S(2)}, u32[]{:S(2)}) collective-permute-start(bf16[512,128]{1,0:T(8,128)(2,1)S(1)} %get-tuple-element.51), channel_id=1, source_target_pairs={{0,2},{2,4},{4,6},{6,8},{8,10},{10,12},{12,14},{14,16},{16,18},{18... | collective-permute-start | bytes 393224 | tf_op jit(solution)/shard_map/ppermute | solution.py:24
  6.6 8.3 %collective-permute-start.4 = (bf16[512,128]{1,0:T(8,128)(2,1)S(1)}, bf16[512,128]{1,0:T(8,128)(2,1)S(1)}, u32[]{:S(2)}, u32[]{:S(2)}) collective-permute-start(bf16[512,128]{1,0:T(8,128)(2,1)S(1)} %get-tuple-element.53), channel_id=1, source_target_pairs={{0,1},{1,0},{2,3},{3,2},{4,5},{5,4},{6,7},{7,6},{8,9},{9,8},{10,11... | collective-permute-start | bytes 393224 | tf_op jit(solution)/shard_map/ppermute | solution.py:24
  15.3 5.6 %collective-permute-start.5 = (bf16[512,128]{1,0:T(8,128)(2,1)S(1)}, bf16[512,128]{1,0:T(8,128)(2,1)S(1)}, u32[]{:S(2)}, u32[]{:S(2)}) collective-permute-start(bf16[512,128]{1,0:T(8,128)(2,1)S(1)} %get-tuple-element.60), channel_id=1, source_target_pairs={{0,1},{1,0},{2,3},{3,2},{4,5},{5,4},{6,7},{7,6},{8,9},{9,8},{10,11... | collective-permute-start | bytes 393224 | tf_op jit(solution)/shard_map/ppermute | solution.py:24

commit v4 on v3

--- a/solution.py
+++ b/solution.py
@@ -179,11 +179,11 @@
     return halves(gate * sigmoid(gate) * up)
 
 
-def sent_hidden(count, tile, window, gate2, up2, own_k, *refs):
+def query_hidden(count, tile, window, gate2, up2, own_q, own_k, *refs):
     got_qk, (queries, highs, lows, keys) = refs[: count - 1], refs[count - 1 :]
     rows, width = own_k.shape
-    for s in range(1, count):
-        source = got_qk[count - s - 1]
+    for s in range(1, count + 1):
+        source = own_q if s == count else got_qk[count - s - 1]
         for t in range(rows // tile):
             span = slice((s - 1) * rows + t * tile, (s - 1) * rows + (t + 1) * tile)
             block = source[t * tile : (t + 1) * tile, :]
@@ -226,7 +226,7 @@
 
 
 def sent_rows(count, tile, flags, down2, gain, keys, queries, highs, lows, weights, normed):
-    rows = queries.shape[0] // (count - 1)
+    rows = queries.shape[0] // count
     window = keys.shape[0] - count * rows
     linked = flags[0] == 1
     length = flags[1]
@@ -284,11 +284,11 @@
 def own_rows_and_update(
     tile,
     flags,
-    gate2,
-    up2,
     down2,
     gain,
-    own_q,
+    queries,
+    highs,
+    lows,
     keys,
     values,
     turned2,
@@ -305,7 +305,7 @@
     dn,
     sems,
 ):
-    rows, width = own_q.shape
+    rows, width = own.shape
     hidden = down.shape[0]
     window = weights.shape[2] - tile
     total = keys.shape[0] - window
@@ -314,12 +314,11 @@
     head = lax.axis_index("head")
     for t in range(rows // tile):
         start = pl.multiple_of(head * rows + t * tile, tile)
-        block = own_q[t * tile : (t + 1) * tile, :]
-        high, low = hidden_rows(block, gate2, up2)
-        normed = fast_rows(high, low, start, length, down2, gain)
-        store_weights(
-            block, keys[pl.ds(start, tile + window), :], start, length, linked, weights.at[t]
-        )
+        place = total - rows + t * tile
+        span = slice(place, place + tile)
+        normed = fast_rows(highs[span, :], lows[span, :], start, length, down2, gain)
+        keys_here = keys[pl.ds(start, tile + window), :]
+        store_weights(queries[span, :], keys_here, start, length, linked, weights.at[t])
         attended = dot(weights[t], values[pl.ds(start, tile + window), :])
         own[t * tile : (t + 1) * tile, :] = (attended + normed).astype(bf16)
     out_copy = pltpu.make_async_copy(own, mixed.at[0, :, head_columns(head, width)], sems.at[0])
@@ -447,7 +446,6 @@
     got_qk = [from_behind(sent_qk[s - 1], "head", s) for s in shifts]
     got_dk = from_behind(down_keys, "ctx", 1)
     prior_v = from_behind(last_v, "ctx", 1)
-    got_v = [from_behind(sent_v[s - 1], "head", s) for s in shifts]
 
     own_q, own_k, own_v, fresh, gain, rate_row, flags = call(
         functools.partial(load, count),
@@ -482,6 +480,8 @@
             dma((9 + hidden // width,)),
         ],
     )
+    held_v = lax.optimization_barrier((fresh, *sent_v))[1:]
+    got_v = [from_behind(held_v[s - 1], "head", s) for s in shifts]
     gate2, up2, turned2, turned, live_rates = call(
         choose_gate_up,
         "choose_gate_up",
@@ -496,13 +496,13 @@
         cost=500,
     )
     all_keys_shape = on_chip((window + total, width), bf16)
-    sent_q, highs, lows, all_keys = call(
-        functools.partial(sent_hidden, count, tile, window),
-        "sent_hidden",
-        [on_chip((sent, width), bf16)]
-        + [on_chip((sent, hidden), bf16)] * 2
+    all_q, highs, lows, all_keys = call(
+        functools.partial(query_hidden, count, tile, window),
+        "query_hidden",
+        [on_chip((total, width), bf16)]
+        + [on_chip((total, hidden), bf16)] * 2
         + [all_keys_shape],
-        all_local(gate2, up2, own_k, *got_qk),
+        all_local(gate2, up2, own_q, own_k, *got_qk),
         cost=500,
     )
     down2, down, all_keys = call(
@@ -516,7 +516,7 @@
         functools.partial(sent_rows, count, tile),
         "sent_rows",
         [on_chip((sent // tile, tile, span), bf16), on_chip((sent, width), f32)],
-        [(scalars, flags)] + all_local(down2, gain, all_keys, sent_q, highs, lows),
+        [(scalars, flags)] + all_local(down2, gain, all_keys, all_q, highs, lows),
         cost=1,
     )
     (all_values,) = call(
@@ -544,7 +544,17 @@
         ],
         [(scalars, flags)]
         + all_local(
-            gate2, up2, down2, gain, own_q, all_keys, all_values, turned2, turned, down, live_rates
+            down2,
+            gain,
+            all_q,
+            highs,
+            lows,
+            all_keys,
+            all_values,
+            turned2,
+            turned,
+            down,
+            live_rates,
         ),
         scratch=[
             VMEM((rows // tile, tile, span), bf16),

time: 21.8 us -> 21.7 us (level)
  Pallas kernels: 9 us -> 8.78 us
    pallas_call x10, Pallas kernels: 9 us -> 8.78 us  [call(): pl.pallas_call(body, out_shape=[shape for _, shape in outs], in_specs=[sp...]
  transfers between devices with their start and end apart: 6 -> 6, of which waited for: 4 -> 5; matrix products, arithmetic and copies ran while one was open for 0% -> 0% of each run, Pallas kernels for 37% -> 36%
where the time goes in v4:
time: 21.7 us; the launch traced here: 21.6 us
  Pallas kernels  8.78 us (40%)
  starting transfers between devices  7.03 us (32%)
  waiting for transfers between devices  5.05 us (23%)
  between operations  0.7 us (3%)
    pallas_call x10, Pallas kernels, call(): pl.pallas_call(body, out_shape=[shape for _, shape in outs], in_specs=[sp...  8.78 us
    ppermute x6, starting transfers between devices, from_behind(): lax.ppermute(shard, axis, [(i, (i + by) % size) for i in range(size)])  7.03 us
    ppermute x6, waiting for transfers between devices, from_behind(): lax.ppermute(shard, axis, [(i, (i + by) % size) for i in range(size)])  5.05 us
  transfers between devices with their start and end apart: 6, of which 5 were waited for; matrix products, arithmetic and copies ran while one was open for 0% of the time, Pallas kernels for 36%

profile of v4, /device:TPU:0, one launch (start us, length us, event | category | flops | bytes accessed | tf_op | source)
XLA Modules:
  0.0 21.6 jit_solution(13963401024167736486)
XLA Ops:
  0.6 0.5 %collective-permute-start.1 = (f32[256,256]{1,0:T(8,128)}, f32[256,256]{1,0:T(8,128)S(1)}, u32[]{:S(2)}, u32[]{:S(2)}) collective-permute-start(f32[256,256]{1,0:T(8,128)} %bitcast.7), channel_id=1, source_target_pairs={{0,2},{2,4},{4,6},{6,8},{8,10},{10,12},{12,14},{14,16},{16,18},{18... | collective-permute-start | bytes 786440 | tf_op jit(solution)/shard_map/ppermute | solution.py:24
  1.1 1.3 %pack.1 = (bf16[1024,128]{1,0:T(8,128)(2,1)S(1)}, bf16[512,128]{1,0:T(8,128)(2,1)S(1)}, bf16[1024,128]{1,0:T(8,128)(2,1)S(1)}, bf16[512,128]{1,0:T(8,128)(2,1)S(1)}) custom-call(bf16[1,512,256]{2,1,0:T(8,128)(2,1)} %q_ref.3, bf16[1,512,256]{2,1,0:T(8,128)(2,1)} %k_ref.3, bf16[1,512,256]{2,1,0:T(8,128)(2,1)} %v_ref.3, f32[1,1,256,128]{3,2,1,0:T(8,128)} %dn_ref.1, ...), custom_call_target="tpu_custom_call" | custom-call | flops 1000000 | bytes 1024 | tf_op jit(solution)/shard_map/pack/pallas_call | solution.py:379
  2.4 2.6 %collective-permute-start.2 = (bf16[1024,128]{1,0:T(8,128)(2,1)S(1)}, bf16[1024,128]{1,0:T(8,128)(2,1)S(1)}, u32[]{:S(2)}, u32[]{:S(2)}) collective-permute-start(bf16[1024,128]{1,0:T(8,128)(2,1)S(1)} %get-tuple-element.34._), channel_id=1, source_target_pairs={{0,1},{1,0},{2,3},{3,2},{4,5},{5,4},{6,7},{7,6},{8,9},{9,8},{10,11... | collective-permute-start | bytes 786440 | tf_op jit(solution)/shard_map/ppermute | solution.py:24
  5.0 1.3 %collective-permute-start = (bf16[1024,128]{1,0:T(8,128)(2,1)S(1)}, bf16[1024,128]{1,0:T(8,128)(2,1)S(1)}, u32[]{:S(2)}, u32[]{:S(2)}) collective-permute-start(bf16[1024,128]{1,0:T(8,128)(2,1)S(1)} %get-tuple-element.36), channel_id=1, source_target_pairs={{0,2},{2,4},{4,6},{6,8},{8,10},{10,12},{12,14},{14,16},{16,18},{18... | collective-permute-start | bytes 786440 | tf_op jit(solution)/shard_map/ppermute | solution.py:24
  6.3 0.3 %collective-permute-start.3 = (bf16[512,128]{1,0:T(8,128)(2,1)S(1)}, bf16[512,128]{1,0:T(8,128)(2,1)S(1)}, u32[]{:S(2)}, u32[]{:S(2)}) collective-permute-start(bf16[512,128]{1,0:T(8,128)(2,1)S(1)} %get-tuple-element.52), channel_id=1, source_target_pairs={{0,2},{2,4},{4,6},{6,8},{8,10},{10,12},{12,14},{14,16},{16,18},{18... | collective-permute-start | bytes 393224 | tf_op jit(solution)/shard_map/ppermute | solution.py:24
  6.6 1.3 %load.1 = (bf16[512,128]{1,0:T(8,128)(2,1)S(1)}, bf16[512,128]{1,0:T(8,128)(2,1)S(1)}, bf16[512,128]{1,0:T(8,128)(2,1)S(1)}, f32[384,256]{1,0:T(8,128)S(1)}, f32...) custom-call(bf16[1,512,256]{2,1,0:T(8,128)(2,1)} %q_ref.3, bf16[1,512,256]{2,1,0:T(8,128)(2,1)} %k_ref.3, ...), custom_call_target="tpu_custom_call" | custom-call | flops 1000000 | bytes 1024 | tf_op jit(solution)/shard_map/load/pallas_call | solution.py:379
  7.9 0.6 %collective-permute-start.4 = (bf16[512,128]{1,0:T(8,128)(2,1)S(1)}, bf16[512,128]{1,0:T(8,128)(2,1)S(1)}, u32[]{:S(2)}, u32[]{:S(2)}) collective-permute-start(bf16[512,128]{1,0:T(8,128)(2,1)S(1)} %get-tuple-element.55), channel_id=1, source_target_pairs={{0,1},{1,0},{2,3},{3,2},{4,5},{5,4},{6,7},{7,6},{8,9},{9,8},{10,11... | collective-permute-start | bytes 393224 | tf_op jit(solution)/shard_map/ppermute | solution.py:24
  8.5 1.9 %collective-permute-done.1.got_gu = f32[256,256]{1,0:T(8,128)S(1)} collective-permute-done((f32[256,256]{1,0:T(8,128)}, f32[256,256]{1,0:T(8,128)S(1)}, u32[]{:S(2)}, u32[]{:S(2)}) %collective-permute-start.1) | collective-permute-done | bytes 262176 | tf_op jit(solution)/shard_map/ppermute | solution.py:24
  10.4 0.1 choose_gate_up.1
  10.6 0.5 %collective-permute-done.2.refs_0_ = bf16[1024,128]{1,0:T(8,128)(2,1)S(1)} collective-permute-done((bf16[1024,128]{1,0:T(8,128)(2,1)S(1)}, bf16[1024,128]{1,0:T(8,128)(2,1)S(1)}, u32[]{:S(2)}, u32[]{:S(2)}) %collective-permute-start.2) | collective-permute-done | bytes 262176 | tf_op jit(solution)/shard_map/ppermute | solution.py:24
  11.1 0.6 %query_hidden.1 = (bf16[1024,128]{1,0:T(8,128)(2,1)S(1)}, bf16[1024,256]{1,0:T(8,128)(2,1)S(1)}, bf16[1024,256]{1,0:T(8,128)(2,1)S(1)}, bf16[1536,128]{1,0:T(8,128)(2,1)S(1)}) custom-call(bf16[256,256]{1,0:T(8,128)(2,1)S(1)} %get-tuple-element.39.gate2, bf16[256,256]{1,0:T(8,128)(2,1)S(1)} %get-tuple-element.40.up2, ...), custom_call_target="tpu_custom_call" | custom-call | flops 500000000 | bytes 1024 | tf_op jit(solution)/shard_map/query_hidden/pallas_call | solution.py:379
  11.7 1.7 %collective-permute-done.down_keys = bf16[1024,128]{1,0:T(8,128)(2,1)S(1)} collective-permute-done((bf16[1024,128]{1,0:T(8,128)(2,1)S(1)}, bf16[1024,128]{1,0:T(8,128)(2,1)S(1)}, u32[]{:S(2)}, u32[]{:S(2)}) %collective-permute-start) | collective-permute-done | bytes 262176 | tf_op jit(solution)/shard_map/ppermute | solution.py:24
  13.5 0.9 %sent_rows.1 = (bf16[2,256,768]{2,1,0:T(8,128)(2,1)S(1)}, f32[512,128]{1,0:T(8,128)S(1)}) custom-call(s32[2]{0:T(128)S(4)} %get-tuple-element.35.flags, bf16[256,256]{1,0:T(8,128)(2,1)S(1)} %get-tuple-element.44.down2, f32[1,128]{1,0:T(1,128)S(1)} %get-tuple-element.45.gain, bf16[1536,128]{1,0:T(8,128)(2,1)S(1)} %get-tuple-element.49.keys, ...), custom_call_target="tpu_custom_call" | custom-call | flops 1000000 | bytes 1024 | tf_op jit(solution)/shard_map/sent_rows/pallas_call | solution.py:379
  14.4 0.5 %collective-permute-done.3.tail_v = bf16[512,128]{1,0:T(8,128)(2,1)S(1)} collective-permute-done((bf16[512,128]{1,0:T(8,128)(2,1)S(1)}, bf16[512,128]{1,0:T(8,128)(2,1)S(1)}, u32[]{:S(2)}, u32[]{:S(2)}) %collective-permute-start.3) | collective-permute-done | bytes 131104 | tf_op jit(solution)/shard_map/ppermute | solution.py:24
  14.9 0.0 collective-permute-done.4.refs_0_
  14.9 0.4 %mix_sent.1 = (bf16[1536,128]{1,0:T(8,128)(2,1)S(1)}, bf16[512,128]{1,0:T(8,128)(2,1)S(1)}) custom-call(bf16[2,256,768]{2,1,0:T(8,128)(2,1)S(1)} %get-tuple-element.50.weights, f32[512,128]{1,0:T(8,128)S(1)} %get-tuple-element.51._.normed, bf16[1536,128]{1,0:T(8,128)(2,1)S(1)} %start_values.1._, ...), custom_call_target="tpu_custom_call", output_to_operand_aliasing={{0}: (2, {})} | custom-call | flops 1000000 | bytes 1024 | tf_op jit(solution)/shard_map/mix_sent/pallas_call | solution.py:379
  15.3 1.7 %collective-permute-start.5 = (bf16[512,128]{1,0:T(8,128)(2,1)S(1)}, bf16[512,128]{1,0:T(8,128)(2,1)S(1)}, u32[]{:S(2)}, u32[]{:S(2)}) collective-permute-start(bf16[512,128]{1,0:T(8,128)(2,1)S(1)} %get-tuple-element.62), channel_id=1, source_target_pairs={{0,1},{1,0},{2,3},{3,2},{4,5},{5,4},{6,7},{7,6},{8,9},{9,8},{10,11... | collective-permute-start | bytes 393224 | tf_op jit(solution)/shard_map/ppermute | solution.py:24
  17.0 3.4 %own_rows_and_update.1 = (bf16[1,512,256]{2,1,0:T(8,128)(2,1)}, f32[1,1,2,128,256]{4,3,2,1,0:T(8,128)}, f32[1,1,256,128]{3,2,1,0:T(8,128)}) custom-call(s32[2]{0:T(128)S(4)} %get-tuple-element.35.flags, bf16[256,256]{1,0:T(8,128)(2,1)S(1)} %get-tuple-element.44.down2, f32[1,128]{1,0:T(1,128)S(1)} %get-tuple-element.45.gain, ...), custom_call_target="tpu_custom_call" | custom-call | flops 1000000 | bytes 1024 | tf_op jit(solution)/shard_map/own_rows_and_update/pallas_call | solution.py:379
  20.5 0.4 %collective-permute-done.5.refs_1_ = bf16[512,128]{1,0:T(8,128)(2,1)S(1)} collective-permute-done((bf16[512,128]{1,0:T(8,128)(2,1)S(1)}, bf16[512,128]{1,0:T(8,128)(2,1)S(1)}, u32[]{:S(2)}, u32[]{:S(2)}) %collective-permute-start.5) | collective-permute-done | bytes 131104 | tf_op jit(solution)/shard_map/ppermute | solution.py:24
  20.9 0.7 %place_received.1 = bf16[1,512,256]{2,1,0:T(8,128)(2,1)} custom-call(bf16[1,512,256]{2,1,0:T(8,128)(2,1)} %get-tuple-element.61.refs_0_, bf16[512,128]{1,0:T(8,128)(2,1)S(1)} %collective-permute-done.5.refs_1_), custom_call_target="tpu_custom_call", output_to_operand_aliasing={{}: (0, {})} | custom-call | flops 1000000 | bytes 1024 | tf_op jit(solution)/shard_map/place_received/pallas_call | solution.py:379
  (2 shorter events, 0.1 us)
Async XLA Ops:
  0.6 9.8 %collective-permute-start.1 = (f32[256,256]{1,0:T(8,128)}, f32[256,256]{1,0:T(8,128)S(1)}, u32[]{:S(2)}, u32[]{:S(2)}) collective-permute-start(f32[256,256]{1,0:T(8,128)} %bitcast.7), channel_id=1, source_target_pairs={{0,2},{2,4},{4,6},{6,8},{8,10},{10,12},{12,14},{14,16},{16,18},{18... | collective-permute-start | bytes 786440 | tf_op jit(solution)/shard_map/ppermute | solution.py:24
  2.4 8.7 %collective-permute-start.2 = (bf16[1024,128]{1,0:T(8,128)(2,1)S(1)}, bf16[1024,128]{1,0:T(8,128)(2,1)S(1)}, u32[]{:S(2)}, u32[]{:S(2)}) collective-permute-start(bf16[1024,128]{1,0:T(8,128)(2,1)S(1)} %get-tuple-element.34._), channel_id=1, source_target_pairs={{0,1},{1,0},{2,3},{3,2},{4,5},{5,4},{6,7},{7,6},{8,9},{9,8},{10,11... | collective-permute-start | bytes 786440 | tf_op jit(solution)/shard_map/ppermute | solution.py:24
  5.0 8.5 %collective-permute-start = (bf16[1024,128]{1,0:T(8,128)(2,1)S(1)}, bf16[1024,128]{1,0:T(8,128)(2,1)S(1)}, u32[]{:S(2)}, u32[]{:S(2)}) collective-permute-start(bf16[1024,128]{1,0:T(8,128)(2,1)S(1)} %get-tuple-element.36), channel_id=1, source_target_pairs={{0,2},{2,4},{4,6},{6,8},{8,10},{10,12},{12,14},{14,16},{16,18},{18... | collective-permute-start | bytes 786440 | tf_op jit(solution)/shard_map/ppermute | solution.py:24
  6.3 8.6 %collective-permute-start.3 = (bf16[512,128]{1,0:T(8,128)(2,1)S(1)}, bf16[512,128]{1,0:T(8,128)(2,1)S(1)}, u32[]{:S(2)}, u32[]{:S(2)}) collective-permute-start(bf16[512,128]{1,0:T(8,128)(2,1)S(1)} %get-tuple-element.52), channel_id=1, source_target_pairs={{0,2},{2,4},{4,6},{6,8},{8,10},{10,12},{12,14},{14,16},{16,18},{18... | collective-permute-start | bytes 393224 | tf_op jit(solution)/shard_map/ppermute | solution.py:24
  7.9 7.0 %collective-permute-start.4 = (bf16[512,128]{1,0:T(8,128)(2,1)S(1)}, bf16[512,128]{1,0:T(8,128)(2,1)S(1)}, u32[]{:S(2)}, u32[]{:S(2)}) collective-permute-start(bf16[512,128]{1,0:T(8,128)(2,1)S(1)} %get-tuple-element.55), channel_id=1, source_target_pairs={{0,1},{1,0},{2,3},{3,2},{4,5},{5,4},{6,7},{7,6},{8,9},{9,8},{10,11... | collective-permute-start | bytes 393224 | tf_op jit(solution)/shard_map/ppermute | solution.py:24
  15.3 5.6 %collective-permute-start.5 = (bf16[512,128]{1,0:T(8,128)(2,1)S(1)}, bf16[512,128]{1,0:T(8,128)(2,1)S(1)}, u32[]{:S(2)}, u32[]{:S(2)}) collective-permute-start(bf16[512,128]{1,0:T(8,128)(2,1)S(1)} %get-tuple-element.62), channel_id=1, source_target_pairs={{0,1},{1,0},{2,3},{3,2},{4,5},{5,4},{6,7},{7,6},{8,9},{9,8},{10,11... | collective-permute-start | bytes 393224 | tf_op jit(solution)/shard_map/ppermute | solution.py:24

commit v5 on v4

--- a/solution.py
+++ b/solution.py
@@ -281,6 +281,39 @@
     return new_weight * (jnp.sqrt(old_square) / jnp.sqrt(new_square))
 
 
+def fill_key_parts(window, keys, turned2, rate_row, gate_part, up_part, down_steps):
+    hidden, total = down_steps.shape
+    width = keys.shape[1]
+    ones = jnp.ones((8, 2 * width), bf16)
+    step = min(256, total)
+    for start in range(0, total, step):
+        block = keys[window + start : window + start + step, :]
+        block32 = block.astype(f32)
+        square = jnp.concatenate(halves(block32 * block32), axis=1)
+        unit = lax.rsqrt(dot_nt(ones, square)[:1] * (1.0 / width) + epsilon)
+        part = slice(start, start + step)
+        rate = rate_row[:, part]
+        scale = rate * unit
+        both = dot_nt(turned2[...], wide(block))
+        gate = both[:hidden] * unit
+        up = both[hidden:] * unit
+        share = sigmoid(gate)
+        act = gate * share
+        gate_part[:, part] = up * (share + act * (1.0 - share)) * scale
+        up_part[:, part] = act * scale
+        down_steps[:, part] = (act * up * rate).astype(bf16)
+
+
+def first_core():
+    return lax.rem(lax.axis_index("ctx"), 2) == 0
+
+
+def key_hidden(window, _, keys, turned2, rate_row, *parts):
+    @pl.when(first_core())
+    def _fill():
+        fill_key_parts(window, keys, turned2, rate_row, *parts)
+
+
 def own_rows_and_update(
     tile,
     flags,
@@ -295,9 +328,15 @@
     turned,
     down,
     rate_row,
+    _gate_part,
+    _up_part,
+    _down_steps,
     mixed,
     new_gu,
     new_dn,
+    gate_part,
+    up_part,
+    down_steps,
     weights,
     own,
     steps,
@@ -323,32 +362,24 @@
         own[t * tile : (t + 1) * tile, :] = (attended + normed).astype(bf16)
     out_copy = pltpu.make_async_copy(own, mixed.at[0, :, head_columns(head, width)], sems.at[0])
     out_copy.start()
-    ones = jnp.ones((8, 2 * width), bf16)
+    @pl.when(jnp.logical_not(first_core()))
+    def _fill():
+        fill_key_parts(window, keys, turned2, rate_row, gate_part, up_part, down_steps)
+
     step = min(256, total)
     for start in range(0, total, step):
-        block_k = keys[window + start : window + start + step, :]
         block_v = values[window + start : window + start + step, :]
-        block32 = block_k.astype(f32)
-        square = jnp.concatenate(halves(block32 * block32), axis=1)
-        unit = lax.rsqrt(dot_nt(ones, square)[:1] * (1.0 / width) + epsilon)
-        rate = rate_row[:, start : start + step]
-        both = dot_nt(turned2[...], wide(block_k))
-        gate = both[:hidden] * unit
-        up = both[hidden:] * unit
-        share = sigmoid(gate)
-        act = gate * share
-        hidden_grad = dot_nt(down2[...], wide(block_v)) * (rate * unit)
+        hidden_grad = dot_nt(down2[...], wide(block_v))
         part = slice(start, start + step)
-        steps[0:hidden, part] = (hidden_grad * up * (share + act * (1.0 - share))).astype(bf16)
-        steps[hidden : 2 * hidden, part] = (hidden_grad * act).astype(bf16)
-        steps[2 * hidden : 3 * hidden, part] = (act * up * rate).astype(bf16)
-    both = dot(steps[0 : 2 * hidden, :], keys[window:, :])
+        steps[0:hidden, part] = (hidden_grad * gate_part[:, part]).astype(bf16)
+        steps[hidden : 2 * hidden, part] = (hidden_grad * up_part[:, part]).astype(bf16)
+    both = dot(steps[...], keys[window:, :])
     for index in range(2):
         part = slice(index * hidden, (index + 1) * hidden)
         gu[index] = renormed(turned[part], both[part], 1).T
     first = pltpu.make_async_copy(gu, new_gu.at[0, 0], sems.at[1])
     first.start()
-    dn[...] = renormed(down[...], dot(steps[2 * hidden :, :], values[window:, :]), 0)
+    dn[...] = renormed(down[...], dot(down_steps[...], values[window:, :]), 0)
     second = pltpu.make_async_copy(dn, new_dn.at[0, 0], sems.at[2])
     second.start()
     out_copy.wait()
@@ -519,11 +550,22 @@
         [(scalars, flags)] + all_local(down2, gain, all_keys, all_q, highs, lows),
         cost=1,
     )
+    key_parts = [
+        on_chip((hidden, total), f32),
+        on_chip((hidden, total), f32),
+        on_chip((hidden, total), bf16),
+    ]
+    parts = call(
+        functools.partial(key_hidden, window),
+        "key_hidden",
+        key_parts,
+        all_local(normed, all_keys, turned2, live_rates),
+    )
     (all_values,) = call(
         start_values,
         "start_values",
         [on_chip((window + total, width), bf16)],
-        all_local(normed, prior_v, own_v),
+        all_local(parts[2], prior_v, own_v),
         cost=1,
     )
     all_values, *mixed_out = call(
@@ -534,13 +576,14 @@
         aliases={2: 0},
     )
     mixed_in = [from_behind(mixed_out[s - 1], "head", s) for s in shifts]
-    mixed, new_gu, new_down = call(
+    mixed, new_gu, new_down, *_ = call(
         functools.partial(own_rows_and_update, tile),
         "own_rows_and_update",
         [
             in_hbm_out(queries.shape, bf16),
             in_hbm_out(state_in_gu.shape, f32),
             in_hbm_out(state_in_down.shape, f32),
+            *key_parts,
         ],
         [(scalars, flags)]
         + all_local(
@@ -555,15 +598,17 @@
             turned,
             down,
             live_rates,
+            *parts,
         ),
         scratch=[
             VMEM((rows // tile, tile, span), bf16),
             VMEM((rows, width), bf16),
-            VMEM((3 * hidden, total), bf16),
+            VMEM((2 * hidden, total), bf16),
             VMEM(state_in_gu.shape[2:], f32),
             VMEM(state_in_down.shape[2:], f32),
             dma((3,)),
         ],
+        aliases={12: 3, 13: 4, 14: 5},
     )
     (mixed,) = call(
         functools.partial(place_received, count),

time: 21.7 us -> 21.7 us (level)
  waiting for transfers between devices: 5.05 us -> 4.41 us
  Pallas kernels: 8.78 us -> 9.39 us
    ppermute x6, waiting for transfers between devices: 5.05 us -> 4.41 us  [from_behind(): lax.ppermute(shard, axis, [(i, (i + by) % size) for i in range(size)])]
    pallas_call x10 -> x11, Pallas kernels: 8.78 us -> 9.39 us  [call(): pl.pallas_call(body, out_shape=[shape for _, shape in outs], in_specs=[sp...]
  transfers between devices with their start and end apart: 6 -> 6, of which waited for: 5 -> 4; matrix products, arithmetic and copies ran while one was open for 0% -> 0% of each run, Pallas kernels for 36% -> 39%
where the time goes in v5:
time: 21.7 us; the launch traced here: 21.6 us
  Pallas kernels  9.39 us (43%)
  starting transfers between devices  7.03 us (32%)
  waiting for transfers between devices  4.41 us (20%)
  between operations  0.72 us (3%)
    pallas_call x11, Pallas kernels, call(): pl.pallas_call(body, out_shape=[shape for _, shape in outs], in_specs=[sp...  9.39 us
    ppermute x6, starting transfers between devices, from_behind(): lax.ppermute(shard, axis, [(i, (i + by) % size) for i in range(size)])  7.03 us
    ppermute x6, waiting for transfers between devices, from_behind(): lax.ppermute(shard, axis, [(i, (i + by) % size) for i in range(size)])  4.41 us
  transfers between devices with their start and end apart: 6, of which 4 were waited for; matrix products, arithmetic and copies ran while one was open for 0% of the time, Pallas kernels for 39%

profile of v5, /device:TPU:0, one launch (start us, length us, event | category | flops | bytes accessed | tf_op | source)
XLA Modules:
  0.0 21.6 jit_solution(14914087661653771902)
XLA Ops:
  0.6 0.5 %collective-permute-start.1 = (f32[256,256]{1,0:T(8,128)}, f32[256,256]{1,0:T(8,128)S(1)}, u32[]{:S(2)}, u32[]{:S(2)}) collective-permute-start(f32[256,256]{1,0:T(8,128)} %bitcast.7), channel_id=1, source_target_pairs={{0,2},{2,4},{4,6},{6,8},{8,10},{10,12},{12,14},{14,16},{16,18},{18... | collective-permute-start | bytes 786440 | tf_op jit(solution)/shard_map/ppermute | solution.py:24
  1.1 1.3 %pack.1 = (bf16[1024,128]{1,0:T(8,128)(2,1)S(1)}, bf16[512,128]{1,0:T(8,128)(2,1)S(1)}, bf16[1024,128]{1,0:T(8,128)(2,1)S(1)}, bf16[512,128]{1,0:T(8,128)(2,1)S(1)}) custom-call(bf16[1,512,256]{2,1,0:T(8,128)(2,1)} %q_ref.3, bf16[1,512,256]{2,1,0:T(8,128)(2,1)} %k_ref.3, bf16[1,512,256]{2,1,0:T(8,128)(2,1)} %v_ref.3, f32[1,1,256,128]{3,2,1,0:T(8,128)} %dn_ref.1, ...), custom_call_target="tpu_custom_call" | custom-call | flops 1000000 | bytes 1024 | tf_op jit(solution)/shard_map/pack/pallas_call | solution.py:410
  2.4 2.6 %collective-permute-start.2 = (bf16[1024,128]{1,0:T(8,128)(2,1)S(1)}, bf16[1024,128]{1,0:T(8,128)(2,1)S(1)}, u32[]{:S(2)}, u32[]{:S(2)}) collective-permute-start(bf16[1024,128]{1,0:T(8,128)(2,1)S(1)} %get-tuple-element.37._), channel_id=1, source_target_pairs={{0,1},{1,0},{2,3},{3,2},{4,5},{5,4},{6,7},{7,6},{8,9},{9,8},{10,11... | collective-permute-start | bytes 786440 | tf_op jit(solution)/shard_map/ppermute | solution.py:24
  5.0 1.3 %collective-permute-start = (bf16[1024,128]{1,0:T(8,128)(2,1)S(1)}, bf16[1024,128]{1,0:T(8,128)(2,1)S(1)}, u32[]{:S(2)}, u32[]{:S(2)}) collective-permute-start(bf16[1024,128]{1,0:T(8,128)(2,1)S(1)} %get-tuple-element.39), channel_id=1, source_target_pairs={{0,2},{2,4},{4,6},{6,8},{8,10},{10,12},{12,14},{14,16},{16,18},{18... | collective-permute-start | bytes 786440 | tf_op jit(solution)/shard_map/ppermute | solution.py:24
  6.3 0.3 %collective-permute-start.3 = (bf16[512,128]{1,0:T(8,128)(2,1)S(1)}, bf16[512,128]{1,0:T(8,128)(2,1)S(1)}, u32[]{:S(2)}, u32[]{:S(2)}) collective-permute-start(bf16[512,128]{1,0:T(8,128)(2,1)S(1)} %get-tuple-element.58), channel_id=1, source_target_pairs={{0,2},{2,4},{4,6},{6,8},{8,10},{10,12},{12,14},{14,16},{16,18},{18... | collective-permute-start | bytes 393224 | tf_op jit(solution)/shard_map/ppermute | solution.py:24
  6.6 1.3 %load.1 = (bf16[512,128]{1,0:T(8,128)(2,1)S(1)}, bf16[512,128]{1,0:T(8,128)(2,1)S(1)}, bf16[512,128]{1,0:T(8,128)(2,1)S(1)}, f32[384,256]{1,0:T(8,128)S(1)}, f32...) custom-call(bf16[1,512,256]{2,1,0:T(8,128)(2,1)} %q_ref.3, bf16[1,512,256]{2,1,0:T(8,128)(2,1)} %k_ref.3, ...), custom_call_target="tpu_custom_call" | custom-call | flops 1000000 | bytes 1024 | tf_op jit(solution)/shard_map/load/pallas_call | solution.py:410
  7.9 0.6 %collective-permute-start.4 = (bf16[512,128]{1,0:T(8,128)(2,1)S(1)}, bf16[512,128]{1,0:T(8,128)(2,1)S(1)}, u32[]{:S(2)}, u32[]{:S(2)}) collective-permute-start(bf16[512,128]{1,0:T(8,128)(2,1)S(1)} %get-tuple-element.61), channel_id=1, source_target_pairs={{0,1},{1,0},{2,3},{3,2},{4,5},{5,4},{6,7},{7,6},{8,9},{9,8},{10,11... | collective-permute-start | bytes 393224 | tf_op jit(solution)/shard_map/ppermute | solution.py:24
  8.5 1.9 %collective-permute-done.1.got_gu = f32[256,256]{1,0:T(8,128)S(1)} collective-permute-done((f32[256,256]{1,0:T(8,128)}, f32[256,256]{1,0:T(8,128)S(1)}, u32[]{:S(2)}, u32[]{:S(2)}) %collective-permute-start.1) | collective-permute-done | bytes 262176 | tf_op jit(solution)/shard_map/ppermute | solution.py:24
  10.4 0.1 choose_gate_up.1
  10.6 0.5 %collective-permute-done.2.refs_0_ = bf16[1024,128]{1,0:T(8,128)(2,1)S(1)} collective-permute-done((bf16[1024,128]{1,0:T(8,128)(2,1)S(1)}, bf16[1024,128]{1,0:T(8,128)(2,1)S(1)}, u32[]{:S(2)}, u32[]{:S(2)}) %collective-permute-start.2) | collective-permute-done | bytes 262176 | tf_op jit(solution)/shard_map/ppermute | solution.py:24
  11.1 0.6 %query_hidden.1 = (bf16[1024,128]{1,0:T(8,128)(2,1)S(1)}, bf16[1024,256]{1,0:T(8,128)(2,1)S(1)}, bf16[1024,256]{1,0:T(8,128)(2,1)S(1)}, bf16[1536,128]{1,0:T(8,128)(2,1)S(1)}) custom-call(bf16[256,256]{1,0:T(8,128)(2,1)S(1)} %get-tuple-element.42.gate2, bf16[256,256]{1,0:T(8,128)(2,1)S(1)} %get-tuple-element.43.up2, ...), custom_call_target="tpu_custom_call" | custom-call | flops 500000000 | bytes 1024 | tf_op jit(solution)/shard_map/query_hidden/pallas_call | solution.py:410
  11.7 1.7 %collective-permute-done.down_keys = bf16[1024,128]{1,0:T(8,128)(2,1)S(1)} collective-permute-done((bf16[1024,128]{1,0:T(8,128)(2,1)S(1)}, bf16[1024,128]{1,0:T(8,128)(2,1)S(1)}, u32[]{:S(2)}, u32[]{:S(2)}) %collective-permute-start) | collective-permute-done | bytes 262176 | tf_op jit(solution)/shard_map/ppermute | solution.py:24
  13.5 0.9 %sent_rows.1 = (bf16[2,256,768]{2,1,0:T(8,128)(2,1)S(1)}, f32[512,128]{1,0:T(8,128)S(1)}) custom-call(s32[2]{0:T(128)S(4)} %get-tuple-element.38.flags, bf16[256,256]{1,0:T(8,128)(2,1)S(1)} %get-tuple-element.47.down2, f32[1,128]{1,0:T(1,128)S(1)} %get-tuple-element.48.gain, bf16[1536,128]{1,0:T(8,128)(2,1)S(1)} %get-tuple-element.52.keys, ...), custom_call_target="tpu_custom_call" | custom-call | flops 1000000 | bytes 1024 | tf_op jit(solution)/shard_map/sent_rows/pallas_call | solution.py:410
  14.4 0.9 %key_hidden.1 = (f32[256,1024]{1,0:T(8,128)S(1)}, f32[256,1024]{1,0:T(8,128)S(1)}, bf16[256,1024]{1,0:T(8,128)(2,1)S(1)}) custom-call(f32[512,128]{1,0:T(8,128)S(1)} %get-tuple-element.54._.normed, bf16[1536,128]{1,0:T(8,128)(2,1)S(1)} %get-tuple-element.52.keys, bf16[512,256]{1,0:T(8,128)(2,1)S(1)} %get-tuple-element.55.turned2, ...), custom_call_target="tpu_custom_call" | custom-call | flops 1000000 | bytes 1024 | tf_op jit(solution)/shard_map/key_hidden/pallas_call | solution.py:410
  15.4 0.0 collective-permute-done.3.tail_v
  15.4 0.0 collective-permute-done.4.refs_0_
  15.4 0.4 %mix_sent.1 = (bf16[1536,128]{1,0:T(8,128)(2,1)S(1)}, bf16[512,128]{1,0:T(8,128)(2,1)S(1)}) custom-call(bf16[2,256,768]{2,1,0:T(8,128)(2,1)S(1)} %get-tuple-element.53.weights, f32[512,128]{1,0:T(8,128)S(1)} %get-tuple-element.54._.normed, bf16[1536,128]{1,0:T(8,128)(2,1)S(1)} %start_values.1._, ...), custom_call_target="tpu_custom_call", output_to_operand_aliasing={{0}: (2, {})} | custom-call | flops 1000000 | bytes 1024 | tf_op jit(solution)/shard_map/mix_sent/pallas_call | solution.py:410
  15.8 1.7 %collective-permute-start.5 = (bf16[512,128]{1,0:T(8,128)(2,1)S(1)}, bf16[512,128]{1,0:T(8,128)(2,1)S(1)}, u32[]{:S(2)}, u32[]{:S(2)}) collective-permute-start(bf16[512,128]{1,0:T(8,128)(2,1)S(1)} %get-tuple-element.68), channel_id=1, source_target_pairs={{0,1},{1,0},{2,3},{3,2},{4,5},{5,4},{6,7},{7,6},{8,9},{9,8},{10,11... | collective-permute-start | bytes 393224 | tf_op jit(solution)/shard_map/ppermute | solution.py:24
  17.5 3.1 %own_rows_and_update.1 = (bf16[1,512,256]{2,1,0:T(8,128)(2,1)}, f32[1,1,2,128,256]{4,3,2,1,0:T(8,128)}, f32[1,1,256,128]{3,2,1,0:T(8,128)}, f32[256,1024]{1,0:T(...) custom-call(s32[2]{0:T(128)S(4)} %get-tuple-element.38.flags, ...), custom_call_target="tpu_custom_call", output_to_operand_aliasing={{3}: (12, {}), {4}: (13, {}), {5}: (14, {})} | custom-call | flops 1000000 | bytes 1024 | tf_op jit(solution)/shard_map/own_rows_and_update/pallas_call | solution.py:410
  20.6 0.3 %collective-permute-done.5.refs_1_ = bf16[512,128]{1,0:T(8,128)(2,1)S(1)} collective-permute-done((bf16[512,128]{1,0:T(8,128)(2,1)S(1)}, bf16[512,128]{1,0:T(8,128)(2,1)S(1)}, u32[]{:S(2)}, u32[]{:S(2)}) %collective-permute-start.5) | collective-permute-done | bytes 131104 | tf_op jit(solution)/shard_map/ppermute | solution.py:24
  20.9 0.7 %place_received.1 = bf16[1,512,256]{2,1,0:T(8,128)(2,1)} custom-call(bf16[1,512,256]{2,1,0:T(8,128)(2,1)} %get-tuple-element.67.refs_0_, bf16[512,128]{1,0:T(8,128)(2,1)S(1)} %collective-permute-done.5.refs_1_), custom_call_target="tpu_custom_call", output_to_operand_aliasing={{}: (0, {})} | custom-call | flops 1000000 | bytes 1024 | tf_op jit(solution)/shard_map/place_received/pallas_call | solution.py:410
  (2 shorter events, 0.1 us)
Async XLA Ops:
  0.6 9.8 %collective-permute-start.1 = (f32[256,256]{1,0:T(8,128)}, f32[256,256]{1,0:T(8,128)S(1)}, u32[]{:S(2)}, u32[]{:S(2)}) collective-permute-start(f32[256,256]{1,0:T(8,128)} %bitcast.7), channel_id=1, source_target_pairs={{0,2},{2,4},{4,6},{6,8},{8,10},{10,12},{12,14},{14,16},{16,18},{18... | collective-permute-start | bytes 786440 | tf_op jit(solution)/shard_map/ppermute | solution.py:24
  2.4 8.7 %collective-permute-start.2 = (bf16[1024,128]{1,0:T(8,128)(2,1)S(1)}, bf16[1024,128]{1,0:T(8,128)(2,1)S(1)}, u32[]{:S(2)}, u32[]{:S(2)}) collective-permute-start(bf16[1024,128]{1,0:T(8,128)(2,1)S(1)} %get-tuple-element.37._), channel_id=1, source_target_pairs={{0,1},{1,0},{2,3},{3,2},{4,5},{5,4},{6,7},{7,6},{8,9},{9,8},{10,11... | collective-permute-start | bytes 786440 | tf_op jit(solution)/shard_map/ppermute | solution.py:24
  5.0 8.5 %collective-permute-start = (bf16[1024,128]{1,0:T(8,128)(2,1)S(1)}, bf16[1024,128]{1,0:T(8,128)(2,1)S(1)}, u32[]{:S(2)}, u32[]{:S(2)}) collective-permute-start(bf16[1024,128]{1,0:T(8,128)(2,1)S(1)} %get-tuple-element.39), channel_id=1, source_target_pairs={{0,2},{2,4},{4,6},{6,8},{8,10},{10,12},{12,14},{14,16},{16,18},{18... | collective-permute-start | bytes 786440 | tf_op jit(solution)/shard_map/ppermute | solution.py:24
  6.3 9.0 %collective-permute-start.3 = (bf16[512,128]{1,0:T(8,128)(2,1)S(1)}, bf16[512,128]{1,0:T(8,128)(2,1)S(1)}, u32[]{:S(2)}, u32[]{:S(2)}) collective-permute-start(bf16[512,128]{1,0:T(8,128)(2,1)S(1)} %get-tuple-element.58), channel_id=1, source_target_pairs={{0,2},{2,4},{4,6},{6,8},{8,10},{10,12},{12,14},{14,16},{16,18},{18... | collective-permute-start | bytes 393224 | tf_op jit(solution)/shard_map/ppermute | solution.py:24
  7.9 7.5 %collective-permute-start.4 = (bf16[512,128]{1,0:T(8,128)(2,1)S(1)}, bf16[512,128]{1,0:T(8,128)(2,1)S(1)}, u32[]{:S(2)}, u32[]{:S(2)}) collective-permute-start(bf16[512,128]{1,0:T(8,128)(2,1)S(1)} %get-tuple-element.61), channel_id=1, source_target_pairs={{0,1},{1,0},{2,3},{3,2},{4,5},{5,4},{6,7},{7,6},{8,9},{9,8},{10,11... | collective-permute-start | bytes 393224 | tf_op jit(solution)/shard_map/ppermute | solution.py:24
  15.8 5.1 %collective-permute-start.5 = (bf16[512,128]{1,0:T(8,128)(2,1)S(1)}, bf16[512,128]{1,0:T(8,128)(2,1)S(1)}, u32[]{:S(2)}, u32[]{:S(2)}) collective-permute-start(bf16[512,128]{1,0:T(8,128)(2,1)S(1)} %get-tuple-element.68), channel_id=1, source_target_pairs={{0,1},{1,0},{2,3},{3,2},{4,5},{5,4},{6,7},{7,6},{8,9},{9,8},{10,11... | collective-permute-start | bytes 393224 | tf_op jit(solution)/shard_map/ppermute | solution.py:24

commit v6 on v4

--- a/solution.py
+++ b/solution.py
@@ -295,11 +295,10 @@
     turned,
     down,
     rate_row,
-    mixed,
+    own,
     new_gu,
     new_dn,
     weights,
-    own,
     steps,
     gu,
     dn,
@@ -312,17 +311,6 @@
     linked = flags[0] == 1
     length = flags[1]
     head = lax.axis_index("head")
-    for t in range(rows // tile):
-        start = pl.multiple_of(head * rows + t * tile, tile)
-        place = total - rows + t * tile
-        span = slice(place, place + tile)
-        normed = fast_rows(highs[span, :], lows[span, :], start, length, down2, gain)
-        keys_here = keys[pl.ds(start, tile + window), :]
-        store_weights(queries[span, :], keys_here, start, length, linked, weights.at[t])
-        attended = dot(weights[t], values[pl.ds(start, tile + window), :])
-        own[t * tile : (t + 1) * tile, :] = (attended + normed).astype(bf16)
-    out_copy = pltpu.make_async_copy(own, mixed.at[0, :, head_columns(head, width)], sems.at[0])
-    out_copy.start()
     ones = jnp.ones((8, 2 * width), bf16)
     step = min(256, total)
     for start in range(0, total, step):
@@ -346,25 +334,32 @@
     for index in range(2):
         part = slice(index * hidden, (index + 1) * hidden)
         gu[index] = renormed(turned[part], both[part], 1).T
-    first = pltpu.make_async_copy(gu, new_gu.at[0, 0], sems.at[1])
+    first = pltpu.make_async_copy(gu, new_gu.at[0, 0], sems.at[0])
     first.start()
     dn[...] = renormed(down[...], dot(steps[2 * hidden :, :], values[window:, :]), 0)
-    second = pltpu.make_async_copy(dn, new_dn.at[0, 0], sems.at[2])
+    second = pltpu.make_async_copy(dn, new_dn.at[0, 0], sems.at[1])
     second.start()
-    out_copy.wait()
+    for t in range(rows // tile):
+        start = pl.multiple_of(head * rows + t * tile, tile)
+        place = total - rows + t * tile
+        span = slice(place, place + tile)
+        normed = fast_rows(highs[span, :], lows[span, :], start, length, down2, gain)
+        keys_here = keys[pl.ds(start, tile + window), :]
+        store_weights(queries[span, :], keys_here, start, length, linked, weights.at[t])
+        attended = dot(weights[t], values[pl.ds(start, tile + window), :])
+        own[t * tile : (t + 1) * tile, :] = (attended + normed).astype(bf16)
     first.wait()
     second.wait()
 
 
-def place_received(count, *refs):
-    got = refs[1:count]
-    mixed, sems = refs[count:]
-    width = got[0].shape[1]
+def place(count, *refs):
+    parts, (mixed, sems) = refs[:count], refs[count:]
+    width = parts[0].shape[1]
     head = lax.axis_index("head")
     run_copies(
         [
-            (got[s - 1], mixed.at[0, :, head_columns(lax.rem(head + count - s, count), width)])
-            for s in range(1, count)
+            (parts[s], mixed.at[0, :, head_columns(lax.rem(head + count - s, count), width)])
+            for s in range(count)
         ],
         sems,
     )
@@ -534,11 +529,11 @@
         aliases={2: 0},
     )
     mixed_in = [from_behind(mixed_out[s - 1], "head", s) for s in shifts]
-    mixed, new_gu, new_down = call(
+    mixed_own, new_gu, new_down = call(
         functools.partial(own_rows_and_update, tile),
         "own_rows_and_update",
         [
-            in_hbm_out(queries.shape, bf16),
+            piece,
             in_hbm_out(state_in_gu.shape, f32),
             in_hbm_out(state_in_down.shape, f32),
         ],
@@ -558,20 +553,18 @@
         ),
         scratch=[
             VMEM((rows // tile, tile, span), bf16),
-            VMEM((rows, width), bf16),
             VMEM((3 * hidden, total), bf16),
             VMEM(state_in_gu.shape[2:], f32),
             VMEM(state_in_down.shape[2:], f32),
-            dma((3,)),
+            dma((2,)),
         ],
     )
     (mixed,) = call(
-        functools.partial(place_received, count),
+        functools.partial(place, count),
         "place_received",
         [in_hbm_out(queries.shape, bf16)],
-        [(in_main, mixed)] + all_local(*mixed_in),
-        scratch=[dma((count - 1,))],
-        aliases={0: 0},
+        all_local(mixed_own, *mixed_in),
+        scratch=[dma((count,))],
     )
     return (mixed, new_gu, new_down)
 

time: 21.7 us -> 21.8 us (level)
  no operation moved by 1% of the time
where the time goes in v6:
time: 21.8 us; the launch traced here: 21.6 us
  Pallas kernels  8.8 us (40%)
  starting transfers between devices  7.03 us (32%)
  waiting for transfers between devices  5.09 us (23%)
  between operations  0.7 us (3%)
    pallas_call x10, Pallas kernels, call(): pl.pallas_call(body, out_shape=[shape for _, shape in outs], in_specs=[sp...  8.8 us
    ppermute x6, starting transfers between devices, from_behind(): lax.ppermute(shard, axis, [(i, (i + by) % size) for i in range(size)])  7.03 us
    ppermute x6, waiting for transfers between devices, from_behind(): lax.ppermute(shard, axis, [(i, (i + by) % size) for i in range(size)])  5.09 us
  transfers between devices with their start and end apart: 6, of which 5 were waited for; matrix products, arithmetic and copies ran while one was open for 0% of the time, Pallas kernels for 36%

profile of v6, /device:TPU:0, one launch (start us, length us, event | category | flops | bytes accessed | tf_op | source)
XLA Modules:
  0.0 21.6 jit_solution(16952239656564271308)
XLA Ops:
  0.6 0.5 %collective-permute-start.1 = (f32[256,256]{1,0:T(8,128)}, f32[256,256]{1,0:T(8,128)S(1)}, u32[]{:S(2)}, u32[]{:S(2)}) collective-permute-start(f32[256,256]{1,0:T(8,128)} %bitcast.7), channel_id=1, source_target_pairs={{0,2},{2,4},{4,6},{6,8},{8,10},{10,12},{12,14},{14,16},{16,18},{18... | collective-permute-start | bytes 786440 | tf_op jit(solution)/shard_map/ppermute | solution.py:24
  1.1 1.3 %pack.1 = (bf16[1024,128]{1,0:T(8,128)(2,1)S(1)}, bf16[512,128]{1,0:T(8,128)(2,1)S(1)}, bf16[1024,128]{1,0:T(8,128)(2,1)S(1)}, bf16[512,128]{1,0:T(8,128)(2,1)S(1)}) custom-call(bf16[1,512,256]{2,1,0:T(8,128)(2,1)} %q_ref.3, bf16[1,512,256]{2,1,0:T(8,128)(2,1)} %k_ref.3, bf16[1,512,256]{2,1,0:T(8,128)(2,1)} %v_ref.3, f32[1,1,256,128]{3,2,1,0:T(8,128)} %dn_ref.1, ...), custom_call_target="tpu_custom_call" | custom-call | flops 1000000 | bytes 1024 | tf_op jit(solution)/shard_map/pack/pallas_call | solution.py:374
  2.4 2.6 %collective-permute-start.2 = (bf16[1024,128]{1,0:T(8,128)(2,1)S(1)}, bf16[1024,128]{1,0:T(8,128)(2,1)S(1)}, u32[]{:S(2)}, u32[]{:S(2)}) collective-permute-start(bf16[1024,128]{1,0:T(8,128)(2,1)S(1)} %get-tuple-element.34._), channel_id=1, source_target_pairs={{0,1},{1,0},{2,3},{3,2},{4,5},{5,4},{6,7},{7,6},{8,9},{9,8},{10,11... | collective-permute-start | bytes 786440 | tf_op jit(solution)/shard_map/ppermute | solution.py:24
  5.0 1.3 %collective-permute-start = (bf16[1024,128]{1,0:T(8,128)(2,1)S(1)}, bf16[1024,128]{1,0:T(8,128)(2,1)S(1)}, u32[]{:S(2)}, u32[]{:S(2)}) collective-permute-start(bf16[1024,128]{1,0:T(8,128)(2,1)S(1)} %get-tuple-element.36), channel_id=1, source_target_pairs={{0,2},{2,4},{4,6},{6,8},{8,10},{10,12},{12,14},{14,16},{16,18},{18... | collective-permute-start | bytes 786440 | tf_op jit(solution)/shard_map/ppermute | solution.py:24
  6.3 0.3 %collective-permute-start.3 = (bf16[512,128]{1,0:T(8,128)(2,1)S(1)}, bf16[512,128]{1,0:T(8,128)(2,1)S(1)}, u32[]{:S(2)}, u32[]{:S(2)}) collective-permute-start(bf16[512,128]{1,0:T(8,128)(2,1)S(1)} %get-tuple-element.52), channel_id=1, source_target_pairs={{0,2},{2,4},{4,6},{6,8},{8,10},{10,12},{12,14},{14,16},{16,18},{18... | collective-permute-start | bytes 393224 | tf_op jit(solution)/shard_map/ppermute | solution.py:24
  6.6 1.3 %load.1 = (bf16[512,128]{1,0:T(8,128)(2,1)S(1)}, bf16[512,128]{1,0:T(8,128)(2,1)S(1)}, bf16[512,128]{1,0:T(8,128)(2,1)S(1)}, f32[384,256]{1,0:T(8,128)S(1)}, f32...) custom-call(bf16[1,512,256]{2,1,0:T(8,128)(2,1)} %q_ref.3, bf16[1,512,256]{2,1,0:T(8,128)(2,1)} %k_ref.3, ...), custom_call_target="tpu_custom_call" | custom-call | flops 1000000 | bytes 1024 | tf_op jit(solution)/shard_map/load/pallas_call | solution.py:374
  7.9 0.6 %collective-permute-start.4 = (bf16[512,128]{1,0:T(8,128)(2,1)S(1)}, bf16[512,128]{1,0:T(8,128)(2,1)S(1)}, u32[]{:S(2)}, u32[]{:S(2)}) collective-permute-start(bf16[512,128]{1,0:T(8,128)(2,1)S(1)} %get-tuple-element.55), channel_id=1, source_target_pairs={{0,1},{1,0},{2,3},{3,2},{4,5},{5,4},{6,7},{7,6},{8,9},{9,8},{10,11... | collective-permute-start | bytes 393224 | tf_op jit(solution)/shard_map/ppermute | solution.py:24
  8.5 1.9 %collective-permute-done.1.got_gu = f32[256,256]{1,0:T(8,128)S(1)} collective-permute-done((f32[256,256]{1,0:T(8,128)}, f32[256,256]{1,0:T(8,128)S(1)}, u32[]{:S(2)}, u32[]{:S(2)}) %collective-permute-start.1) | collective-permute-done | bytes 262176 | tf_op jit(solution)/shard_map/ppermute | solution.py:24
  10.4 0.1 choose_gate_up.1
  10.6 0.5 %collective-permute-done.2.refs_0_ = bf16[1024,128]{1,0:T(8,128)(2,1)S(1)} collective-permute-done((bf16[1024,128]{1,0:T(8,128)(2,1)S(1)}, bf16[1024,128]{1,0:T(8,128)(2,1)S(1)}, u32[]{:S(2)}, u32[]{:S(2)}) %collective-permute-start.2) | collective-permute-done | bytes 262176 | tf_op jit(solution)/shard_map/ppermute | solution.py:24
  11.1 0.6 %query_hidden.1 = (bf16[1024,128]{1,0:T(8,128)(2,1)S(1)}, bf16[1024,256]{1,0:T(8,128)(2,1)S(1)}, bf16[1024,256]{1,0:T(8,128)(2,1)S(1)}, bf16[1536,128]{1,0:T(8,128)(2,1)S(1)}) custom-call(bf16[256,256]{1,0:T(8,128)(2,1)S(1)} %get-tuple-element.39.gate2, bf16[256,256]{1,0:T(8,128)(2,1)S(1)} %get-tuple-element.40.up2, ...), custom_call_target="tpu_custom_call" | custom-call | flops 500000000 | bytes 1024 | tf_op jit(solution)/shard_map/query_hidden/pallas_call | solution.py:374
  11.7 1.7 %collective-permute-done.down_keys = bf16[1024,128]{1,0:T(8,128)(2,1)S(1)} collective-permute-done((bf16[1024,128]{1,0:T(8,128)(2,1)S(1)}, bf16[1024,128]{1,0:T(8,128)(2,1)S(1)}, u32[]{:S(2)}, u32[]{:S(2)}) %collective-permute-start) | collective-permute-done | bytes 262176 | tf_op jit(solution)/shard_map/ppermute | solution.py:24
  13.5 0.9 %sent_rows.1 = (bf16[2,256,768]{2,1,0:T(8,128)(2,1)S(1)}, f32[512,128]{1,0:T(8,128)S(1)}) custom-call(s32[2]{0:T(128)S(4)} %get-tuple-element.35.flags, bf16[256,256]{1,0:T(8,128)(2,1)S(1)} %get-tuple-element.44.down2, f32[1,128]{1,0:T(1,128)S(1)} %get-tuple-element.45.gain, bf16[1536,128]{1,0:T(8,128)(2,1)S(1)} %get-tuple-element.49.keys, ...), custom_call_target="tpu_custom_call" | custom-call | flops 1000000 | bytes 1024 | tf_op jit(solution)/shard_map/sent_rows/pallas_call | solution.py:374
  14.4 0.5 %collective-permute-done.3.tail_v = bf16[512,128]{1,0:T(8,128)(2,1)S(1)} collective-permute-done((bf16[512,128]{1,0:T(8,128)(2,1)S(1)}, bf16[512,128]{1,0:T(8,128)(2,1)S(1)}, u32[]{:S(2)}, u32[]{:S(2)}) %collective-permute-start.3) | collective-permute-done | bytes 131104 | tf_op jit(solution)/shard_map/ppermute | solution.py:24
  14.9 0.0 collective-permute-done.4.refs_0_
  14.9 0.4 %mix_sent.1 = (bf16[1536,128]{1,0:T(8,128)(2,1)S(1)}, bf16[512,128]{1,0:T(8,128)(2,1)S(1)}) custom-call(bf16[2,256,768]{2,1,0:T(8,128)(2,1)S(1)} %get-tuple-element.50.weights, f32[512,128]{1,0:T(8,128)S(1)} %get-tuple-element.51._.normed, bf16[1536,128]{1,0:T(8,128)(2,1)S(1)} %start_values.1._, ...), custom_call_target="tpu_custom_call", output_to_operand_aliasing={{0}: (2, {})} | custom-call | flops 1000000 | bytes 1024 | tf_op jit(solution)/shard_map/mix_sent/pallas_call | solution.py:374
  15.3 1.7 %collective-permute-start.5 = (bf16[512,128]{1,0:T(8,128)(2,1)S(1)}, bf16[512,128]{1,0:T(8,128)(2,1)S(1)}, u32[]{:S(2)}, u32[]{:S(2)}) collective-permute-start(bf16[512,128]{1,0:T(8,128)(2,1)S(1)} %get-tuple-element.62), channel_id=1, source_target_pairs={{0,1},{1,0},{2,3},{3,2},{4,5},{5,4},{6,7},{7,6},{8,9},{9,8},{10,11... | collective-permute-start | bytes 393224 | tf_op jit(solution)/shard_map/ppermute | solution.py:24
  17.0 3.4 %own_rows_and_update.1 = (bf16[512,128]{1,0:T(8,128)(2,1)S(1)}, f32[1,1,2,128,256]{4,3,2,1,0:T(8,128)}, f32[1,1,256,128]{3,2,1,0:T(8,128)}) custom-call(s32[2]{0:T(128)S(4)} %get-tuple-element.35.flags, bf16[256,256]{1,0:T(8,128)(2,1)S(1)} %get-tuple-element.44.down2, f32[1,128]{1,0:T(1,128)S(1)} %get-tuple-element.45.gain, ...), custom_call_target="tpu_custom_call" | custom-call | flops 1000000 | bytes 1024 | tf_op jit(solution)/shard_map/own_rows_and_update/pallas_call | solution.py:374
  20.4 0.5 %collective-permute-done.5.refs_1_ = bf16[512,128]{1,0:T(8,128)(2,1)S(1)} collective-permute-done((bf16[512,128]{1,0:T(8,128)(2,1)S(1)}, bf16[512,128]{1,0:T(8,128)(2,1)S(1)}, u32[]{:S(2)}, u32[]{:S(2)}) %collective-permute-start.5) | collective-permute-done | bytes 131104 | tf_op jit(solution)/shard_map/ppermute | solution.py:24
  20.9 0.7 %place_received.1 = bf16[1,512,256]{2,1,0:T(8,128)(2,1)} custom-call(bf16[512,128]{1,0:T(8,128)(2,1)S(1)} %get-tuple-element.61.refs_0_, bf16[512,128]{1,0:T(8,128)(2,1)S(1)} %collective-permute-done.5.refs_1_), custom_call_target="tpu_custom_call" | custom-call | flops 1000000 | bytes 1024 | tf_op jit(solution)/shard_map/place_received/pallas_call | solution.py:374
  (2 shorter events, 0.1 us)
Async XLA Ops:
  0.6 9.8 %collective-permute-start.1 = (f32[256,256]{1,0:T(8,128)}, f32[256,256]{1,0:T(8,128)S(1)}, u32[]{:S(2)}, u32[]{:S(2)}) collective-permute-start(f32[256,256]{1,0:T(8,128)} %bitcast.7), channel_id=1, source_target_pairs={{0,2},{2,4},{4,6},{6,8},{8,10},{10,12},{12,14},{14,16},{16,18},{18... | collective-permute-start | bytes 786440 | tf_op jit(solution)/shard_map/ppermute | solution.py:24
  2.4 8.7 %collective-permute-start.2 = (bf16[1024,128]{1,0:T(8,128)(2,1)S(1)}, bf16[1024,128]{1,0:T(8,128)(2,1)S(1)}, u32[]{:S(2)}, u32[]{:S(2)}) collective-permute-start(bf16[1024,128]{1,0:T(8,128)(2,1)S(1)} %get-tuple-element.34._), channel_id=1, source_target_pairs={{0,1},{1,0},{2,3},{3,2},{4,5},{5,4},{6,7},{7,6},{8,9},{9,8},{10,11... | collective-permute-start | bytes 786440 | tf_op jit(solution)/shard_map/ppermute | solution.py:24
  5.0 8.5 %collective-permute-start = (bf16[1024,128]{1,0:T(8,128)(2,1)S(1)}, bf16[1024,128]{1,0:T(8,128)(2,1)S(1)}, u32[]{:S(2)}, u32[]{:S(2)}) collective-permute-start(bf16[1024,128]{1,0:T(8,128)(2,1)S(1)} %get-tuple-element.36), channel_id=1, source_target_pairs={{0,2},{2,4},{4,6},{6,8},{8,10},{10,12},{12,14},{14,16},{16,18},{18... | collective-permute-start | bytes 786440 | tf_op jit(solution)/shard_map/ppermute | solution.py:24
  6.3 8.6 %collective-permute-start.3 = (bf16[512,128]{1,0:T(8,128)(2,1)S(1)}, bf16[512,128]{1,0:T(8,128)(2,1)S(1)}, u32[]{:S(2)}, u32[]{:S(2)}) collective-permute-start(bf16[512,128]{1,0:T(8,128)(2,1)S(1)} %get-tuple-element.52), channel_id=1, source_target_pairs={{0,2},{2,4},{4,6},{6,8},{8,10},{10,12},{12,14},{14,16},{16,18},{18... | collective-permute-start | bytes 393224 | tf_op jit(solution)/shard_map/ppermute | solution.py:24
  7.9 7.0 %collective-permute-start.4 = (bf16[512,128]{1,0:T(8,128)(2,1)S(1)}, bf16[512,128]{1,0:T(8,128)(2,1)S(1)}, u32[]{:S(2)}, u32[]{:S(2)}) collective-permute-start(bf16[512,128]{1,0:T(8,128)(2,1)S(1)} %get-tuple-element.55), channel_id=1, source_target_pairs={{0,1},{1,0},{2,3},{3,2},{4,5},{5,4},{6,7},{7,6},{8,9},{9,8},{10,11... | collective-permute-start | bytes 393224 | tf_op jit(solution)/shard_map/ppermute | solution.py:24
  15.3 5.6 %collective-permute-start.5 = (bf16[512,128]{1,0:T(8,128)(2,1)S(1)}, bf16[512,128]{1,0:T(8,128)(2,1)S(1)}, u32[]{:S(2)}, u32[]{:S(2)}) collective-permute-start(bf16[512,128]{1,0:T(8,128)(2,1)S(1)} %get-tuple-element.62), channel_id=1, source_target_pairs={{0,1},{1,0},{2,3},{3,2},{4,5},{5,4},{6,7},{7,6},{8,9},{9,8},{10,11... | collective-permute-start | bytes 393224 | tf_op jit(solution)/shard_map/ppermute | solution.py:24
